TPU v7x, 512 devices: a whole 4x4x16 slice. The times are simulated.
512 devices in a mesh: expert: 8 (over z_lo, core), dp: 64 (over z_hi, x, y).
Axes of the slice: x: 4, y: 4, z: 16 (z_hi: 4, z_lo: 4; z = z_hi * 4 + z_lo), core: 2. Of those that a mesh axis runs over, the one named last changes fastest.
Arguments:
- x_rows: bfloat16 [8, 64, 8, 2, 3072], P('expert', 'dp'), may hold values from -6 to 6
- cot_rows: bfloat16 [8, 64, 8, 2, 3072], P('expert', 'dp'), may hold values from -3 to 3
- counts: int32 [8, 64, 8], P(None, 'dp'), may hold values from 0 to 2, as said below
- w_gate: bfloat16 [8, 3072, 8192], P('expert', None, 'dp'), may hold values from -0.109375 to 0.109375
- w_up: bfloat16 [8, 3072, 8192], P('expert', None, 'dp'), may hold values from -0.109375 to 0.109375
- w_down: bfloat16 [8, 8192, 3072], P('expert', 'dp'), may hold values from -0.0625 to 0.0625
- kept_blocks: int32 [8], P('expert'), may hold values from 16 to 64
- block_rank: int32 [8, 64], P('expert', 'dp'), may hold values from 0 to 63, each once within a row
Outputs:
- grad_rows: bfloat16 [8, 64, 8, 2, 3072], P('expert', 'dp')
- grad_gate: bfloat16 [8, 3072, 8192], P('expert', None, 'dp')
- grad_up: bfloat16 [8, 3072, 8192], P('expert', None, 'dp')
- grad_down: bfloat16 [8, 8192, 3072], P('expert', 'dp')
Inputs may be any that keep to these rules, and one draw needn't show every extreme that they name: The live slots of a source's buffer for an expert are its first ones. For every expert e and index d the sum over sources s of counts[s, d, e] is at most 4, and it equals 4 for every d of some expert.
All inputs are finite; a program needn't handle non-finite values.
Results may differ from a plain program's by a relative error of at most 0.005.
Values may be sent and summed in bfloat16 or wider, within the bound.
No kernel may reach another device: no remote copies, remote signals or barrier semaphores. Data moves between devices by JAX's collectives and lax.ppermute only.
A program may use at most 64 MiB of HBM per device.

v0:
```python
import jax
import jax.numpy as jnp
from jax import lax
from jax.sharding import PartitionSpec as P

LIVE = 4


def compact_matrix(slot_counts, live_rows, capacity):
    sources = slot_counts.shape[0]
    within_slot = jnp.tile(jnp.arange(capacity, dtype=jnp.int32), sources)
    count_slot = jnp.repeat(slot_counts, capacity)
    offsets = jnp.repeat(jnp.cumsum(slot_counts) - slot_counts, capacity)
    target = offsets + within_slot
    alive = within_slot < count_slot
    row_index = jnp.arange(live_rows, dtype=jnp.int32)[:, None]
    return ((row_index == target[None, :]) & alive[None, :]).astype(jnp.bfloat16)


def contract(left, right, left_dim, right_dim):
    return lax.dot_general(
        left, right, (((left_dim,), (right_dim,)), ((), ())), preferred_element_type=jnp.float32
    )


def body(x_rows, cot_rows, counts, w_gate, w_up, w_down, kept_blocks, block_rank):
    expert_count = x_rows.shape[2]
    capacity = x_rows.shape[3]
    model_width = x_rows.shape[4]
    slot_rows = x_rows.reshape(expert_count, capacity, model_width)
    slot_cots = cot_rows.reshape(expert_count, capacity, model_width)
    my_expert = lax.axis_index("expert")
    picked = jnp.arange(expert_count, dtype=jnp.int32)[None, :] == my_expert
    own_counts = jnp.sum(jnp.where(picked, counts[:, 0, :], 0), axis=1)
    chooser = compact_matrix(own_counts, LIVE, capacity)

    def pack_rows(received):
        flat_rows = received.reshape(-1, model_width)
        return jnp.dot(chooser, flat_rows, preferred_element_type=jnp.float32).astype(jnp.bfloat16)

    got_rows, got_cots = (
        lax.all_to_all(slot_rows, "expert", split_axis=0, concat_axis=0, tiled=True),
        lax.all_to_all(slot_cots, "expert", split_axis=0, concat_axis=0, tiled=True),
    )
    group_rows, group_cots = (
        lax.all_gather(pack_rows(got_rows), "dp", axis=0, tiled=True),
        lax.all_gather(pack_rows(got_cots), "dp", axis=0, tiled=True),
    )
    gate_weight = w_gate[0]
    up_weight = w_up[0]
    down_weight = w_down[0]
    keep_mask = (block_rank.reshape(()) < kept_blocks.reshape(())).astype(jnp.float32)
    gate_pre = jnp.dot(group_rows, gate_weight, preferred_element_type=jnp.float32)
    up_pre = jnp.dot(group_rows, up_weight, preferred_element_type=jnp.float32)
    sigmoid_gate = jax.nn.sigmoid(gate_pre)
    activated = gate_pre * sigmoid_gate
    hidden = (activated * up_pre * keep_mask).astype(jnp.bfloat16)
    hidden_grad = contract(group_cots, down_weight, 1, 1)
    up_grad = (hidden_grad * activated * keep_mask).astype(jnp.bfloat16)
    gate_grad = (
        hidden_grad * up_pre * sigmoid_gate * (1.0 + gate_pre * (1.0 - sigmoid_gate)) * keep_mask
    ).astype(jnp.bfloat16)
    grad_down = contract(hidden, group_cots, 0, 0).astype(jnp.bfloat16)
    grad_gate = contract(group_rows, gate_grad, 0, 0).astype(jnp.bfloat16)
    grad_up = contract(group_rows, up_grad, 0, 0).astype(jnp.bfloat16)
    whole_term = contract(gate_grad, gate_weight, 1, 1) + contract(up_grad, up_weight, 1, 1)
    row_grads = lax.psum_scatter(whole_term, "dp", scatter_dimension=0, tiled=True)
    row_grads = row_grads.astype(jnp.bfloat16)
    slot_grads = contract(chooser, row_grads, 0, 0).astype(jnp.bfloat16)
    slot_grads = slot_grads.reshape(expert_count, capacity, model_width)
    returned = lax.all_to_all(slot_grads, "expert", split_axis=0, concat_axis=0, tiled=True)
    grad_rows = returned.reshape(1, 1, expert_count, capacity, model_width)
    return (grad_rows, grad_gate[None], grad_up[None], grad_down[None])


def solution(mesh):
    in_specs = (
        P("expert", "dp", None, None, None),
        P("expert", "dp", None, None, None),
        P(None, "dp", None),
        P("expert", None, "dp"),
        P("expert", None, "dp"),
        P("expert", "dp", None),
        P("expert"),
        P("expert", "dp"),
    )
    out_specs = (
        P("expert", "dp", None, None, None),
        P("expert", None, "dp"),
        P("expert", None, "dp"),
        P("expert", "dp", None),
    )
    return jax.shard_map(body, mesh=mesh, in_specs=in_specs, out_specs=out_specs, check_vma=False)
```

profile of v0, /device:TPU:1, one launch (start us, length us, event | category | flops | bytes accessed | tf_op | source)
XLA Modules:
  0.0 771.1 jit_solution(15349936523839550636)
XLA Ops:
  7.2 0.0 copy-start
  7.2 10.3 %all-to-all-start.1 = ((bf16[8,2,3072]{2,1,0:T(2,128)(2,1)}), bf16[8,2,3072]{2,1,0:T(2,128)(2,1)S(1)}, u32[]{:S(2)}, u32[]{:S(2)}) async-start(bf16[8,2,3072]{2,1,0:T(2,128)(2,1)} %bitcast.50), calls=%async_computation.1 | async-start | bytes 196608 | tf_op jit(solution)/shard_map/all_to_all | solution.py:42
  17.5 0.0 all-gather.7.cloned.1.call-start
  17.5 0.8 select_reduce_fusion
  18.3 0.1 iota_compare_fusion
  18.4 0.1 lt.14
  18.4 0.2 reduce-window.9
  18.6 0.1 iota_add_fusion
  18.7 0.1 add.22
  18.8 4.2 all-to-all-done.1
  23.0 0.7 fusion.4
  23.8 0.0 all-gather.7.cloned.1.call-update
  23.8 0.0 all-gather.5.cloned.1.call-start
  23.8 9.6 %all_to_all.15 = bf16[8,2,3072]{2,1,0:T(2,128)(2,1)S(1)} all-to-all(bf16[8,2,3072]{2,1,0:T(2,128)(2,1)} %bitcast.51), channel_id=1, replica_groups=mesh['expert'=8,'dp'=64] {'expert'}, dimensions={0} | all-to-all | bytes 196608 | tf_op jit(solution)/shard_map/all_to_all | solution.py:43
  33.5 0.7 fusion.3
  34.2 0.0 all-gather.5.cloned.1.call-update
  35.6 1.3 dynamic-slice
  37.5 93.3 %all-gather.7.cloned.1.call-done = bf16[64,4,3072]{2,1,0:T(4,128)(2,1)} async-done(((bf16[1,4,3072]{2,1,0:T(4,128)(2,1)}), bf16[64,4,3072]{2,1,0:T(4,128)(2,1)}) %all-gather.7.cloned.1.call-update) | async-done | bytes 1572880 | tf_op jit(solution)/shard_map/all_gather | solution.py:46
  130.8 2.7 reshape.98
  133.5 0.0 copy-done
  133.5 0.0 copy-start.2
  133.5 0.6 fusion.7
  134.1 0.6 copy-done.2
  134.7 0.6 fusion.10
  135.2 102.1 %all-gather.5.cloned.1.call-done = bf16[64,4,3072]{2,1,0:T(4,128)(2,1)} async-done(((bf16[1,4,3072]{2,1,0:T(4,128)(2,1)}), bf16[64,4,3072]{2,1,0:T(4,128)(2,1)}) %all-gather.5.cloned.1.call-update) | async-done | bytes 1572880 | tf_op jit(solution)/shard_map/all_gather | solution.py:47
  237.3 3.7 reshape.96
  241.0 2.2 multiply_convert_fusion.1
  243.2 1.5 fusion.1
  244.7 0.6 fusion.5
  245.3 2.3 convolution_add_fusion
  247.5 448.0 %all-reduce.2 = bf16[256,3072]{1,0:T(8,128)(2,1)} all-reduce(f32[256,3072]{1,0:T(8,128)} %convolution_add_fusion), channel_id=2, replica_groups=mesh['expert'=8,'dp'=64] {'dp'}, use_global_device_ids=true, to_apply=%region_2.3.clone | all-reduce | flops 786432 | bytes 4718592
  695.5 1.0 convolution_convert_fusion.3
  696.6 0.7 reshape.93
  697.3 60.9 %all-to-all-start.2 = ((bf16[8,2,3072]{2,1,0:T(2,128)(2,1)}), bf16[8,2,3072]{2,1,0:T(2,128)(2,1)S(1)}, u32[]{:S(2)}, u32[]{:S(2)}) async-start(bf16[8,2,3072]{2,1,0:T(2,128)(2,1)} %reshape.93), calls=%async_computation.2 | async-start | bytes 196608 | tf_op jit(solution)/shard_map/all_to_all | solution.py:71
  758.1 0.0 copy-start.1
  758.1 1.5 fusion
  759.6 0.0 copy-done.1
  759.6 1.3 fusion.2
  761.0 2.6 all-to-all-done.2
  763.6 0.6 copy.17
  (4 shorter events, 0.1 us)
Async XLA Ops:
  7.2 126.4 %copy-start = (bf16[1,3072,128]{2,1,0:T(8,128)(2,1)S(1)}, bf16[1,3072,128]{2,1,0:T(8,128)(2,1)}, u32[]{:S(2)}) copy-start(bf16[1,3072,128]{2,1,0:T(8,128)(2,1)} %param.11) | copy-start | bytes 2359300
  7.2 15.8 %all-to-all-start.1 = ((bf16[8,2,3072]{2,1,0:T(2,128)(2,1)}), bf16[8,2,3072]{2,1,0:T(2,128)(2,1)S(1)}, u32[]{:S(2)}, u32[]{:S(2)}) async-start(bf16[8,2,3072]{2,1,0:T(2,128)(2,1)} %bitcast.50), calls=%async_computation.1 | async-start | bytes 196608 | tf_op jit(solution)/shard_map/all_to_all | solution.py:42
  17.5 113.3 %all-gather.7.cloned.1.call-start = ((), (), s32[]{:S(2)}) async-start(), calls=%async_computation.4 | async-start | bytes 1597440 | tf_op jit(solution)/shard_map/all_gather | solution.py:46
  23.8 213.5 %all-gather.5.cloned.1.call-start = ((), (), s32[]{:S(2)}) async-start(), calls=%async_computation.3 | async-start | bytes 1597440 | tf_op jit(solution)/shard_map/all_gather | solution.py:47
  133.5 1.1 copy-start.2
  697.3 66.3 %all-to-all-start.2 = ((bf16[8,2,3072]{2,1,0:T(2,128)(2,1)}), bf16[8,2,3072]{2,1,0:T(2,128)(2,1)S(1)}, u32[]{:S(2)}, u32[]{:S(2)}) async-start(bf16[8,2,3072]{2,1,0:T(2,128)(2,1)} %reshape.93), calls=%async_computation.2 | async-start | bytes 196608 | tf_op jit(solution)/shard_map/all_to_all | solution.py:71
  758.1 1.5 copy-start.1
Sparse Core Ops, SparseCore 0:
  23.9 106.8 all-gather.6
  135.4 101.8 all-gather.4
where the time goes:
time: 772 us; the launch traced here: 771 us
  blocking collectives  458 us (59%)
  waiting for transfers between devices  202 us (26%)
  starting transfers between devices  71.2 us (9%)
  between operations  16.1 us (2%)
  matrix products  13 us (2%)
  local copies, waits for them, and re-layouts  9.87 us (1%)
    unnamed x1, blocking collectives  448 us
    all_gather x1, waiting for transfers between devices, body(): lax.all_gather(pack_rows(got_cots), 'dp', axis=0, tiled=True)  102 us
    all_gather x1, waiting for transfers between devices, body(): lax.all_gather(pack_rows(got_rows), 'dp', axis=0, tiled=True)  93.3 us
    all_to_all x1, starting transfers between devices, body(): lax.all_to_all(slot_grads, 'expert', split_axis=0, concat_axis=0, tiled=T...  60.9 us
  transfers between devices with their start and end apart: 4, of which 4 were waited for; matrix products, arithmetic and copies ran while one was open for 1% of the time, Pallas kernels for 0%

commit v1 on v0

--- a/solution.py
+++ b/solution.py
@@ -10,7 +10,8 @@
     sources = slot_counts.shape[0]
     within_slot = jnp.tile(jnp.arange(capacity, dtype=jnp.int32), sources)
     count_slot = jnp.repeat(slot_counts, capacity)
-    offsets = jnp.repeat(jnp.cumsum(slot_counts) - slot_counts, capacity)
+    earlier = jnp.arange(sources)[None, :] < jnp.arange(sources)[:, None]
+    offsets = jnp.repeat(jnp.sum(jnp.where(earlier, slot_counts[None, :], 0), axis=1), capacity)
     target = offsets + within_slot
     alive = within_slot < count_slot
     row_index = jnp.arange(live_rows, dtype=jnp.int32)[:, None]

time: 772 us -> 772 us (level)
  no operation moved by 1% of the time
where the time goes in v1:
time: 772 us; the launch traced here: 771 us
  blocking collectives  458 us (59%)
  waiting for transfers between devices  202 us (26%)
  starting transfers between devices  71.2 us (9%)
  between operations  16.1 us (2%)
  matrix products  13 us (2%)
  local copies, waits for them, and re-layouts  9.87 us (1%)
    unnamed x1, blocking collectives  448 us
    all_gather x1, waiting for transfers between devices, body(): lax.all_gather(pack_rows(got_cots), 'dp', axis=0, tiled=True)  102 us
    all_gather x1, waiting for transfers between devices, body(): lax.all_gather(pack_rows(got_rows), 'dp', axis=0, tiled=True)  93.3 us
    all_to_all x1, starting transfers between devices, body(): lax.all_to_all(slot_grads, 'expert', split_axis=0, concat_axis=0, tiled=T...  60.9 us
  transfers between devices with their start and end apart: 4, of which 4 were waited for; matrix products, arithmetic and copies ran while one was open for 1% of the time, Pallas kernels for 0%

profile of v1, /device:TPU:1, one launch (start us, length us, event | category | flops | bytes accessed | tf_op | source)
XLA Modules:
  0.0 771.1 jit_solution(6798377600060864773)
XLA Ops:
  7.2 0.0 copy-start
  7.2 10.3 %all-to-all-start.1 = ((bf16[8,2,3072]{2,1,0:T(2,128)(2,1)}), bf16[8,2,3072]{2,1,0:T(2,128)(2,1)S(1)}, u32[]{:S(2)}, u32[]{:S(2)}) async-start(bf16[8,2,3072]{2,1,0:T(2,128)(2,1)} %bitcast.47), calls=%async_computation.1 | async-start | bytes 196608 | tf_op jit(solution)/shard_map/all_to_all | solution.py:43
  17.5 0.0 all-gather.7.cloned.1.call-start
  17.5 0.8 select_reduce_fusion.1
  18.3 0.1 iota_compare_fusion
  18.4 0.1 lt.30
  18.4 0.1 select_reduce_fusion
  18.6 0.1 iota_add_fusion
  18.6 0.1 add.22
  18.7 4.3 all-to-all-done.1
  23.0 0.7 fusion.4
  23.8 0.0 all-gather.7.cloned.1.call-update
  23.8 0.0 all-gather.5.cloned.1.call-start
  23.8 9.6 %all_to_all.15 = bf16[8,2,3072]{2,1,0:T(2,128)(2,1)S(1)} all-to-all(bf16[8,2,3072]{2,1,0:T(2,128)(2,1)} %bitcast.48), channel_id=1, replica_groups=mesh['expert'=8,'dp'=64] {'expert'}, dimensions={0} | all-to-all | bytes 196608 | tf_op jit(solution)/shard_map/all_to_all | solution.py:44
  33.5 0.7 fusion.3
  34.2 0.0 all-gather.5.cloned.1.call-update
  35.6 1.3 dynamic-slice
  37.5 93.3 %all-gather.7.cloned.1.call-done = bf16[64,4,3072]{2,1,0:T(4,128)(2,1)} async-done(((bf16[1,4,3072]{2,1,0:T(4,128)(2,1)}), bf16[64,4,3072]{2,1,0:T(4,128)(2,1)}) %all-gather.7.cloned.1.call-update) | async-done | bytes 1572880 | tf_op jit(solution)/shard_map/all_gather | solution.py:47
  130.8 2.7 reshape.71
  133.5 0.0 copy-done
  133.5 0.0 copy-start.2
  133.5 0.6 fusion.7
  134.1 0.6 copy-done.2
  134.7 0.6 fusion.10
  135.2 102.1 %all-gather.5.cloned.1.call-done = bf16[64,4,3072]{2,1,0:T(4,128)(2,1)} async-done(((bf16[1,4,3072]{2,1,0:T(4,128)(2,1)}), bf16[64,4,3072]{2,1,0:T(4,128)(2,1)}) %all-gather.5.cloned.1.call-update) | async-done | bytes 1572880 | tf_op jit(solution)/shard_map/all_gather | solution.py:48
  237.3 3.7 reshape.69
  241.0 2.2 multiply_convert_fusion.1
  243.2 1.5 fusion.1
  244.7 0.6 fusion.5
  245.3 2.3 convolution_add_fusion
  247.5 448.0 %all-reduce.2 = bf16[256,3072]{1,0:T(8,128)(2,1)} all-reduce(f32[256,3072]{1,0:T(8,128)} %convolution_add_fusion), channel_id=2, replica_groups=mesh['expert'=8,'dp'=64] {'dp'}, use_global_device_ids=true, to_apply=%region_2.3.clone | all-reduce | flops 786432 | bytes 4718592
  695.5 1.0 convolution_convert_fusion.3
  696.6 0.7 reshape.66
  697.3 60.9 %all-to-all-start.2 = ((bf16[8,2,3072]{2,1,0:T(2,128)(2,1)}), bf16[8,2,3072]{2,1,0:T(2,128)(2,1)S(1)}, u32[]{:S(2)}, u32[]{:S(2)}) async-start(bf16[8,2,3072]{2,1,0:T(2,128)(2,1)} %reshape.66), calls=%async_computation.2 | async-start | bytes 196608 | tf_op jit(solution)/shard_map/all_to_all | solution.py:72
  758.1 0.0 copy-start.1
  758.1 1.5 fusion
  759.6 0.0 copy-done.1
  759.6 1.3 fusion.2
  761.0 2.6 all-to-all-done.2
  763.6 0.6 copy.17
  (3 shorter events, 0.1 us)
Async XLA Ops:
  7.2 126.4 %copy-start = (bf16[1,3072,128]{2,1,0:T(8,128)(2,1)S(1)}, bf16[1,3072,128]{2,1,0:T(8,128)(2,1)}, u32[]{:S(2)}) copy-start(bf16[1,3072,128]{2,1,0:T(8,128)(2,1)} %param.11) | copy-start | bytes 2359300
  7.2 15.8 %all-to-all-start.1 = ((bf16[8,2,3072]{2,1,0:T(2,128)(2,1)}), bf16[8,2,3072]{2,1,0:T(2,128)(2,1)S(1)}, u32[]{:S(2)}, u32[]{:S(2)}) async-start(bf16[8,2,3072]{2,1,0:T(2,128)(2,1)} %bitcast.47), calls=%async_computation.1 | async-start | bytes 196608 | tf_op jit(solution)/shard_map/all_to_all | solution.py:43
  17.5 113.3 %all-gather.7.cloned.1.call-start = ((), (), s32[]{:S(2)}) async-start(), calls=%async_computation.4 | async-start | bytes 1597440 | tf_op jit(solution)/shard_map/all_gather | solution.py:47
  23.8 213.5 %all-gather.5.cloned.1.call-start = ((), (), s32[]{:S(2)}) async-start(), calls=%async_computation.3 | async-start | bytes 1597440 | tf_op jit(solution)/shard_map/all_gather | solution.py:48
  133.5 1.1 copy-start.2
  697.3 66.3 %all-to-all-start.2 = ((bf16[8,2,3072]{2,1,0:T(2,128)(2,1)}), bf16[8,2,3072]{2,1,0:T(2,128)(2,1)S(1)}, u32[]{:S(2)}, u32[]{:S(2)}) async-start(bf16[8,2,3072]{2,1,0:T(2,128)(2,1)} %reshape.66), calls=%async_computation.2 | async-start | bytes 196608 | tf_op jit(solution)/shard_map/all_to_all | solution.py:72
  758.1 1.5 copy-start.1
Sparse Core Ops, SparseCore 0:
  23.9 106.8 all-gather.6
  135.4 101.8 all-gather.4

commit v2 on v0

v2 whole, which is shorter than its diff:
```python
import jax
import jax.numpy as jnp
import numpy as np
from jax import lax
from jax.sharding import Mesh
from jax.sharding import PartitionSpec as P

LIVE = 4
EXPERT = ("z_lo", "core")
PLANE = ("x", "y")
DP = ("z_hi", "x", "y")


def contract(left, right, left_dim, right_dim):
    return lax.dot_general(
        left, right, (((left_dim,), (right_dim,)), ((), ())), preferred_element_type=jnp.float32
    )


def compact_matrix(slot_counts, capacity):
    sources = slot_counts.shape[0]
    earlier = jnp.arange(sources)[None, :] < jnp.arange(sources)[:, None]
    offsets = jnp.sum(jnp.where(earlier, slot_counts[None, :], 0), axis=1)
    within = jnp.arange(capacity, dtype=jnp.int32)[None, :]
    target = jnp.where(within < slot_counts[:, None], offsets[:, None] + within, -1)
    row = jnp.arange(LIVE, dtype=jnp.int32)[:, None, None]
    return (row == target[None]).astype(jnp.bfloat16)


def exchange(array, axes):
    return lax.all_to_all(array, axes, split_axis=0, concat_axis=0, tiled=True)


def spread(array, axes, size):
    return exchange(jnp.broadcast_to(array[None], (size,) + array.shape), axes)


def body(x_rows, cot_rows, counts, w_gate, w_up, w_down, kept_blocks, block_rank):
    experts, capacity, width = x_rows.shape[2:]
    my_expert = lax.axis_index(EXPERT)
    picked = jnp.arange(experts, dtype=jnp.int32)[None, :] == my_expert
    own_counts = jnp.sum(jnp.where(picked, counts[:, 0, :], 0), axis=1)
    chooser = compact_matrix(own_counts, capacity)
    none = jnp.zeros_like(chooser)
    both = jnp.concatenate(
        (jnp.concatenate((chooser, none), 2), jnp.concatenate((none, chooser), 2)), 0
    ).reshape(2 * LIVE, 2 * experts * capacity)

    slots = jnp.concatenate((x_rows[0, 0], cot_rows[0, 0]), axis=1)
    got = exchange(slots, EXPERT).reshape(2 * experts * capacity, width)
    packed = jnp.dot(both, got, preferred_element_type=jnp.float32).astype(jnp.bfloat16)
    column = spread(packed, "z_hi", 4)
    column = column.reshape(4, 2, LIVE, width).transpose(1, 0, 2, 3).reshape(8 * LIVE, width)
    group = spread(column, PLANE, 16)
    rows = group[:, : 4 * LIVE].reshape(64 * LIVE, width)
    cots = group[:, 4 * LIVE :].reshape(64 * LIVE, width)

    gate_weight, up_weight, down_weight = w_gate[0], w_up[0], w_down[0]
    keep = (block_rank.reshape(()) < kept_blocks.reshape(())).astype(jnp.float32)
    gate = jnp.dot(rows, gate_weight, preferred_element_type=jnp.float32)
    up = jnp.dot(rows, up_weight, preferred_element_type=jnp.float32)
    hidden_grad = contract(cots, down_weight, 1, 1)
    sig = jax.nn.sigmoid(gate)
    act = gate * sig
    hidden = (act * up * keep).astype(jnp.bfloat16)
    up_grad = (hidden_grad * act * keep).astype(jnp.bfloat16)
    gate_grad = (hidden_grad * up * sig * (1.0 + gate * (1.0 - sig)) * keep).astype(jnp.bfloat16)
    term = contract(gate_grad, gate_weight, 1, 1) + contract(up_grad, up_weight, 1, 1)
    parts = exchange(term.astype(jnp.bfloat16).reshape(16, 4 * LIVE, width), PLANE)
    plane_sum = jnp.sum(parts.astype(jnp.float32), axis=0).astype(jnp.bfloat16)
    parts = exchange(plane_sum.reshape(4, LIVE, width), "z_hi")
    row_grads = jnp.sum(parts.astype(jnp.float32), axis=0).astype(jnp.bfloat16)
    slot_grads = contract(chooser.reshape(LIVE, experts * capacity), row_grads, 0, 0)
    slot_grads = slot_grads.astype(jnp.bfloat16).reshape(experts, capacity, width)
    grad_rows = exchange(slot_grads, EXPERT)[None, None]

    grad_down = contract(hidden, cots, 0, 0).astype(jnp.bfloat16)
    grad_gate = contract(rows, gate_grad, 0, 0).astype(jnp.bfloat16)
    grad_up = contract(rows, up_grad, 0, 0).astype(jnp.bfloat16)
    return (grad_rows, grad_gate[None], grad_up[None], grad_down[None])


def solution(mesh):
    fine = Mesh(np.asarray(mesh.devices).reshape(4, 2, 4, 4, 4), EXPERT + DP)
    in_specs = (
        P(EXPERT, DP, None, None, None),
        P(EXPERT, DP, None, None, None),
        P(None, DP, None),
        P(EXPERT, None, DP),
        P(EXPERT, None, DP),
        P(EXPERT, DP, None),
        P(EXPERT),
        P(EXPERT, DP),
    )
    out_specs = (
        P(EXPERT, DP, None, None, None),
        P(EXPERT, None, DP),
        P(EXPERT, None, DP),
        P(EXPERT, DP, None),
    )
    return jax.shard_map(body, mesh=fine, in_specs=in_specs, out_specs=out_specs, check_vma=False)
```

time: 772 us -> 169 us (0.22)
  blocking collectives: 458 us -> 23.2 us
  waiting for transfers between devices: 202 us -> 73.4 us
  starting transfers between devices: 71.2 us -> 47.6 us
  between operations: 16.1 us -> 2.07 us
    unnamed x1 -> x0, blocking collectives: 448 us -> none
    all_gather x2 -> x0, waiting for transfers between devices: 195 us -> none  [the longest x1 102 us: body(): lax.all_gather(pack_rows(got_cots), 'dp', axis=0, tiled=True)]
    all_to_all x2 -> x5, waiting for transfers between devices: 6.82 us -> 73.4 us  [exchange(): return lax.all_to_all(array, axes, split_axis=0, concat_axis=0, tiled=True)]
    all_to_all x2 -> x5, starting transfers between devices: 71.2 us -> 47.6 us  [exchange(): return lax.all_to_all(array, axes, split_axis=0, concat_axis=0, tiled=True)]
    all_to_all x1, blocking collectives: 9.62 us -> 23.2 us  [exchange(): return lax.all_to_all(array, axes, split_axis=0, concat_axis=0, tiled=True)]
  transfers between devices with their start and end apart: 4 -> 5, of which waited for: 4 -> 5; matrix products, arithmetic and copies ran while one was open for 1% -> 3% of each run, Pallas kernels for 0% -> 0%
where the time goes in v2:
time: 169 us; the launch traced here: 168 us
  waiting for transfers between devices  73.4 us (43%)
  starting transfers between devices  47.6 us (28%)
  blocking collectives  23.2 us (14%)
  matrix products  8.86 us (5%)
  local copies, waits for them, and re-layouts  8.64 us (5%)
  other arithmetic  4.53 us (3%)
  between operations  2.07 us (1%)
    all_to_all x5, waiting for transfers between devices, exchange(): return lax.all_to_all(array, axes, split_axis=0, concat_axis=0, tiled=True)  73.4 us
    all_to_all x5, starting transfers between devices, exchange(): return lax.all_to_all(array, axes, split_axis=0, concat_axis=0, tiled=True)  47.6 us
    all_to_all x1, blocking collectives, exchange(): return lax.all_to_all(array, axes, split_axis=0, concat_axis=0, tiled=True)  23.2 us
    dot_general x7, matrix products, contract(): lax.dot_general(left, right, (((left_dim,), (right_dim,)), ((), ())), pre...  7.47 us
  transfers between devices with their start and end apart: 5, of which 5 were waited for; matrix products, arithmetic and copies ran while one was open for 3% of the time, Pallas kernels for 0%

profile of v2, /device:TPU:1, one launch (start us, length us, event | category | flops | bytes accessed | tf_op | source)
XLA Modules:
  0.0 168.3 jit_solution(10610540170797786015)
XLA Ops:
  0.6 0.0 copy-start
  0.6 1.9 %pad_maximum_fusion = bf16[8,4,3072]{2,1,0:T(4,128)(2,1)} fusion(bf16[8,2,3072]{2,1,0:T(2,128)(2,1)} %bitcast.63, bf16[8,2,3072]{2,1,0:T(2,128)(2,1)} %bitcast.64), kind=kLoop, calls=%fused_computation.20 | loop fusion | flops 393216 | bytes 393216 | tf_op jit(solution)/shard_map/concatenate | solution.py:49
  2.5 10.2 %all-to-all-start = ((bf16[8,4,3072]{2,1,0:T(4,128)(2,1)}), bf16[8,4,3072]{2,1,0:T(4,128)(2,1)S(1)}, u32[]{:S(2)}, u32[]{:S(2)}) async-start(bf16[8,4,3072]{2,1,0:T(4,128)(2,1)} %pad_maximum_fusion), calls=%async_computation | async-start | bytes 393216 | tf_op jit(solution)/shard_map/all_to_all | solution.py:31
  12.7 0.8 select_reduce_fusion.1
  13.5 0.1 select_reduce_fusion
  13.7 5.5 %all-to-all-done = bf16[8,4,3072]{2,1,0:T(4,128)(2,1)S(1)} async-done(((bf16[8,4,3072]{2,1,0:T(4,128)(2,1)}), bf16[8,4,3072]{2,1,0:T(4,128)(2,1)S(1)}, u32[]{:S(2)}, u32[]{:S(2)}) %all-to-all-start) | async-done | bytes 196640 | tf_op jit(solution)/shard_map/all_to_all | solution.py:31
  19.2 0.3 fusion.4
  19.5 23.2 %all_to_all.30 = bf16[4,8,3072]{2,1,0:T(8,128)(2,1)S(1)} all-to-all(bf16[4,8,3072]{2,1,0:T(8,128)(2,1)S(1)} %broadcast_in_dim.68), channel_id=1, replica_groups=mesh['z_lo'=4,'core'=2,'z_hi'=4,'x'=4,'y'=4] {'z_hi'}, dimensions={0} | all-to-all | bytes 393216 | tf_op jit(solution)/shard_map/all_to_all | solution.py:31
  42.7 0.2 copy.23
  42.9 0.1 copy.24
  43.0 2.1 %broadcast_in_dim.70 = bf16[16,32,3072]{2,1,0:T(8,128)(2,1)} broadcast(bf16[32,3072]{1,0:T(8,128)(2,1)S(1)} %broadcast_in_dim.69), dimensions={1,2} | broadcast | bytes 3342336 | tf_op jit(solution)/shard_map/broadcast_in_dim | solution.py:35
  45.1 6.8 %all-to-all-start.2 = ((bf16[16,32,3072]{2,1,0:T(8,128)(2,1)}), bf16[16,32,3072]{2,1,0:T(8,128)(2,1)}, u32[]{:S(2)}, u32[]{:S(2)}) async-start(bf16[16,32,3072]{2,1,0:T(8,128)(2,1)} %broadcast_in_dim.70), calls=%async_computation.2 | async-start | bytes 6291456 | tf_op jit(solution)/shard_map/all_to_all | solution.py:31
  53.2 34.7 %all-to-all-done.2 = bf16[16,32,3072]{2,1,0:T(8,128)(2,1)} async-done(((bf16[16,32,3072]{2,1,0:T(8,128)(2,1)}), bf16[16,32,3072]{2,1,0:T(8,128)(2,1)}, u32[]{:S(2)}, u32[]{:S(2)}) %all-to-all-start.2) | async-done | bytes 3145760 | tf_op jit(solution)/shard_map/all_to_all | solution.py:31
  87.9 2.2 %fusion.33 = (bf16[16,16,3072]{2,1,0:T(8,128)(2,1)S(1)}, bf16[16,16,3072]{2,1,0:T(8,128)(2,1)S(1)}) fusion(bf16[16,32,3072]{2,1,0:T(8,128)(2,1)} %all-to-all-done.2), kind=kLoop, calls=%fused_computation.51 | loop fusion | bytes 6291456 | tf_op jit(solution)/shard_map/slice | solution.py:56
  90.1 0.0 copy-start.1
  90.1 0.0 copy-start.3
  90.1 0.0 copy-done
  90.1 0.6 fusion.7
  90.7 1.1 copy-done.3
  91.8 0.0 copy-start.4
  91.8 0.6 fusion.10
  92.3 0.0 copy-done.1
  92.4 0.5 copy-done.4
  92.9 0.6 multiply_convert_fusion.1
  93.5 0.6 fusion.5
  94.1 1.7 %fusion = bf16[256,3072]{1,0:T(8,128)(2,1)} fusion(f32[256,3072]{1,0:T(8,128)S(1)} %fusion.5, bf16[256,128]{1,0:T(8,128)(2,1)S(1)} %get-tuple-element.6, bf16[1,3072,128]{2,1,0:T(8,128)(2,1)S(1)} %copy-done.3), kind=kOutput, calls=%fused_computation.1 | convolution fusion | flops 202899456 | bytes 5570560 | tf_op jit(solution)/shard_map/dot_general | solution.py:15
  95.8 9.8 %all-to-all-start.3 = ((bf16[16,16,3072]{2,1,0:T(8,128)(2,1)}), bf16[16,16,3072]{2,1,0:T(8,128)(2,1)}, u32[]{:S(2)}, u32[]{:S(2)}) async-start(bf16[16,16,3072]{2,1,0:T(8,128)(2,1)} %bitcast.60), calls=%async_computation.3 | async-start | bytes 3145728 | tf_op jit(solution)/shard_map/all_to_all | solution.py:31
  105.6 0.1 lt.52
  105.7 0.1 lt.53
  105.8 0.1 add.39
  105.8 0.1 add.40
  105.9 0.1 lt.51
  106.0 20.0 %all-to-all-done.3 = bf16[16,16,3072]{2,1,0:T(8,128)(2,1)} async-done(((bf16[16,16,3072]{2,1,0:T(8,128)(2,1)}), bf16[16,16,3072]{2,1,0:T(8,128)(2,1)}, u32[]{:S(2)}, u32[]{:S(2)}) %all-to-all-start.3) | async-done | bytes 1572896 | tf_op jit(solution)/shard_map/all_to_all | solution.py:31
  126.0 1.6 reduce_sum.44
  127.7 0.7 reshape.94
  128.4 5.0 %all-to-all-start.4 = ((bf16[4,4,3072]{2,1,0:T(4,128)(2,1)}), bf16[4,4,3072]{2,1,0:T(4,128)(2,1)S(1)}, u32[]{:S(2)}, u32[]{:S(2)}) async-start(bf16[4,4,3072]{2,1,0:T(4,128)(2,1)} %reshape.94), calls=%async_computation.4 | async-start | bytes 196608 | tf_op jit(solution)/shard_map/all_to_all | solution.py:31
  133.3 1.5 fusion.2
  134.8 10.5 %all-to-all-done.4 = bf16[4,4,3072]{2,1,0:T(4,128)(2,1)S(1)} async-done(((bf16[4,4,3072]{2,1,0:T(4,128)(2,1)}), bf16[4,4,3072]{2,1,0:T(4,128)(2,1)S(1)}, u32[]{:S(2)}, u32[]{:S(2)}) %all-to-all-start.4) | async-done | bytes 98336 | tf_op jit(solution)/shard_map/all_to_all | solution.py:31
  145.3 0.1 reduce_sum.45
  145.4 0.2 convolution_convert_fusion.3
  145.6 0.7 reshape.95
  146.3 15.8 %all-to-all-start.5 = ((bf16[8,2,3072]{2,1,0:T(2,128)(2,1)}), bf16[8,2,3072]{2,1,0:T(2,128)(2,1)S(1)}, u32[]{:S(2)}, u32[]{:S(2)}) async-start(bf16[8,2,3072]{2,1,0:T(2,128)(2,1)} %reshape.95), calls=%async_computation.5 | async-start | bytes 196608 | tf_op jit(solution)/shard_map/all_to_all | solution.py:31
  162.1 0.0 copy-start.2
  162.1 1.5 fusion.1
  163.7 0.0 copy-done.2
  163.7 1.3 fusion.3
  165.0 2.6 %all-to-all-done.5 = bf16[8,2,3072]{2,1,0:T(2,128)(2,1)S(1)} async-done(((bf16[8,2,3072]{2,1,0:T(2,128)(2,1)}), bf16[8,2,3072]{2,1,0:T(2,128)(2,1)S(1)}, u32[]{:S(2)}, u32[]{:S(2)}) %all-to-all-start.5) | async-done | bytes 98336 | tf_op jit(solution)/shard_map/all_to_all | solution.py:31
  167.6 0.6 copy.30
  (7 shorter events, 0.1 us)
Async XLA Ops:
  0.6 89.4 %copy-start = (bf16[1,3072,128]{2,1,0:T(8,128)(2,1)S(1)}, bf16[1,3072,128]{2,1,0:T(8,128)(2,1)}, u32[]{:S(2)}) copy-start(bf16[1,3072,128]{2,1,0:T(8,128)(2,1)} %param.11) | copy-start | bytes 2359300
  2.5 16.6 %all-to-all-start = ((bf16[8,4,3072]{2,1,0:T(4,128)(2,1)}), bf16[8,4,3072]{2,1,0:T(4,128)(2,1)S(1)}, u32[]{:S(2)}, u32[]{:S(2)}) async-start(bf16[8,4,3072]{2,1,0:T(4,128)(2,1)} %pad_maximum_fusion), calls=%async_computation | async-start | bytes 393216 | tf_op jit(solution)/shard_map/all_to_all | solution.py:31
  45.1 42.8 %all-to-all-start.2 = ((bf16[16,32,3072]{2,1,0:T(8,128)(2,1)}), bf16[16,32,3072]{2,1,0:T(8,128)(2,1)}, u32[]{:S(2)}, u32[]{:S(2)}) async-start(bf16[16,32,3072]{2,1,0:T(8,128)(2,1)} %broadcast_in_dim.70), calls=%async_computation.2 | async-start | bytes 6291456 | tf_op jit(solution)/shard_map/all_to_all | solution.py:31
  90.1 2.3 %copy-start.1 = (bf16[16,16,3072]{2,1,0:T(8,128)(2,1)}, bf16[16,16,3072]{2,1,0:T(8,128)(2,1)S(1)}, u32[]{:S(2)}) copy-start(bf16[16,16,3072]{2,1,0:T(8,128)(2,1)S(1)} %get-tuple-element.4) | copy-start | bytes 4718596
  90.1 1.7 %copy-start.3 = (bf16[1,3072,128]{2,1,0:T(8,128)(2,1)S(1)}, bf16[1,3072,128]{2,1,0:T(8,128)(2,1)}, u32[]{:S(2)}) copy-start(bf16[1,3072,128]{2,1,0:T(8,128)(2,1)} %param.12) | copy-start | bytes 2359300
  91.8 1.1 copy-start.4
  95.8 30.2 %all-to-all-start.3 = ((bf16[16,16,3072]{2,1,0:T(8,128)(2,1)}), bf16[16,16,3072]{2,1,0:T(8,128)(2,1)}, u32[]{:S(2)}, u32[]{:S(2)}) async-start(bf16[16,16,3072]{2,1,0:T(8,128)(2,1)} %bitcast.60), calls=%async_computation.3 | async-start | bytes 3145728 | tf_op jit(solution)/shard_map/all_to_all | solution.py:31
  128.4 17.0 %all-to-all-start.4 = ((bf16[4,4,3072]{2,1,0:T(4,128)(2,1)}), bf16[4,4,3072]{2,1,0:T(4,128)(2,1)S(1)}, u32[]{:S(2)}, u32[]{:S(2)}) async-start(bf16[4,4,3072]{2,1,0:T(4,128)(2,1)} %reshape.94), calls=%async_computation.4 | async-start | bytes 196608 | tf_op jit(solution)/shard_map/all_to_all | solution.py:31
  146.3 21.3 %all-to-all-start.5 = ((bf16[8,2,3072]{2,1,0:T(2,128)(2,1)}), bf16[8,2,3072]{2,1,0:T(2,128)(2,1)S(1)}, u32[]{:S(2)}, u32[]{:S(2)}) async-start(bf16[8,2,3072]{2,1,0:T(2,128)(2,1)} %reshape.95), calls=%async_computation.5 | async-start | bytes 196608 | tf_op jit(solution)/shard_map/all_to_all | solution.py:31
  162.1 1.5 copy-start.2

commit v3 on v2

v3 whole, which is shorter than its diff:
```python
import jax
import jax.numpy as jnp
import numpy as np
from jax import lax
from jax.experimental import pallas as pl
from jax.experimental.pallas import tpu as pltpu
from jax.sharding import Mesh
from jax.sharding import PartitionSpec as P

LIVE = 4
EXPERT = ("z_lo", "core")
PLANE = ("x", "y")
DP = ("z_hi", "x", "y")
STEP = 512
NN = (((1,), (0,)), ((), ()))
NT = (((1,), (1,)), ((), ()))
TN = (((0,), (0,)), ((), ()))
VMEM_LIMIT = 40 * 2**20


def dot(left, right, dims=NN):
    return lax.dot_general(left, right, dims, preferred_element_type=jnp.float32)


def compact_matrix(slot_counts, capacity):
    sources = slot_counts.shape[0]
    earlier = jnp.arange(sources)[None, :] < jnp.arange(sources)[:, None]
    offsets = jnp.sum(jnp.where(earlier, slot_counts[None, :], 0), axis=1)
    within = jnp.arange(capacity, dtype=jnp.int32)[None, :]
    target = jnp.where(within < slot_counts[:, None], offsets[:, None] + within, -1)
    row = jnp.arange(LIVE, dtype=jnp.int32)[:, None, None]
    return (row == target[None]).astype(jnp.bfloat16)


def exchange(array, axes):
    return lax.all_to_all(array, axes, split_axis=0, concat_axis=0, tiled=True)


def fan_kernel(column, fan, ordered, sems):
    size = column.shape[0]
    out = lax.broadcasted_iota(jnp.int32, (size, size), 0)
    source = ((out & 15) >> 2) * 8 + (out >> 4) * 4 + (out & 3)
    order = (source == lax.broadcasted_iota(jnp.int32, (size, size), 1)).astype(jnp.bfloat16)
    ordered[...] = dot(order, column[...]).astype(jnp.bfloat16)
    copies = [
        pltpu.make_async_copy(ordered, fan.at[i], sems.at[i]) for i in range(fan.shape[0])
    ]
    for copy in copies:
        copy.start()
    for copy in copies:
        copy.wait()


def fan_out(column, receivers):
    size, width = column.shape
    return pl.pallas_call(
        fan_kernel,
        out_shape=jax.ShapeDtypeStruct((receivers, size, width), jnp.bfloat16),
        in_specs=[pl.BlockSpec(memory_space=pltpu.VMEM)],
        out_specs=pl.BlockSpec(memory_space=pl.ANY),
        scratch_shapes=[
            pltpu.VMEM((size, width), jnp.bfloat16),
            pltpu.SemaphoreType.DMA((receivers,)),
        ],
        compiler_params=pltpu.CompilerParams(vmem_limit_bytes=VMEM_LIMIT),
    )(column)


def middle_kernel(
    keep_row, group, w_gate, w_up, w_down, term, hidden, gate_grad, up_grad, sums, both
):
    blocks, pair, width = group.shape
    half = pair // 2
    size = blocks * half
    sums[...] = jnp.zeros_like(sums)

    def forward(i, carry):
        part = pl.ds(pl.multiple_of(i * STEP, STEP), STEP)
        rows = group[:, :half, part].reshape(size, STEP)
        cots = group[:, half:, part].reshape(size, STEP)
        sums[0] += dot(rows, w_gate[part, :])
        sums[1] += dot(rows, w_up[part, :])
        sums[2] += dot(cots, w_down[:, part], NT)
        return carry

    lax.fori_loop(0, width // STEP, forward, 0)
    keep = keep_row[0:1, :]
    gate, up, hidden_grad = sums[0], sums[1], sums[2]
    sig = jax.nn.sigmoid(gate)
    act = gate * sig
    hidden[...] = (act * up * keep).astype(jnp.bfloat16)
    dup = (hidden_grad * act * keep).astype(jnp.bfloat16)
    dgate = (hidden_grad * up * sig * (1.0 + gate * (1.0 - sig)) * keep).astype(jnp.bfloat16)
    up_grad[...] = dup
    gate_grad[...] = dgate
    both[...] = jnp.concatenate((dgate, dup), axis=1)

    def backward(i, carry):
        part = pl.ds(pl.multiple_of(i * STEP, STEP), STEP)
        weights = jnp.concatenate((w_gate[part, :], w_up[part, :]), axis=1)
        out = dot(both[...], weights, NT).astype(jnp.bfloat16)
        term[:, :, part] = out.reshape(blocks, half, STEP)
        return carry

    lax.fori_loop(0, width // STEP, backward, 0)


def middle(keep, group, w_gate, w_up, w_down):
    blocks, pair, width = group.shape
    units = w_gate.shape[1]
    size = blocks * pair // 2
    vmem = pl.BlockSpec(memory_space=pltpu.VMEM)
    grads = jax.ShapeDtypeStruct((size, units), jnp.bfloat16)
    return pl.pallas_call(
        middle_kernel,
        out_shape=(
            jax.ShapeDtypeStruct((blocks, pair // 2, width), jnp.bfloat16),
            grads,
            grads,
            grads,
        ),
        in_specs=[vmem, vmem, vmem, vmem, vmem],
        out_specs=(vmem, vmem, vmem, vmem),
        scratch_shapes=[
            pltpu.VMEM((3, size, units), jnp.float32),
            pltpu.VMEM((size, 2 * units), jnp.bfloat16),
        ],
        compiler_params=pltpu.CompilerParams(vmem_limit_bytes=VMEM_LIMIT),
        cost_estimate=pl.CostEstimate(
            flops=10 * size * units * width, bytes_accessed=8 * 2**20, transcendentals=size * units
        ),
    )(keep, group, w_gate, w_up, w_down)


def body(x_rows, cot_rows, counts, w_gate, w_up, w_down, kept_blocks, block_rank):
    experts, capacity, width = x_rows.shape[2:]
    my_expert = lax.axis_index(EXPERT)
    picked = jnp.arange(experts, dtype=jnp.int32)[None, :] == my_expert
    own_counts = jnp.sum(jnp.where(picked, counts[:, 0, :], 0), axis=1)
    chooser = compact_matrix(own_counts, capacity)
    back = chooser.reshape(LIVE, experts * capacity).T
    kind = jnp.eye(2, dtype=jnp.bfloat16)
    both = kind[:, None, None, :, None] * chooser[None, :, :, None, :]
    both = both.reshape(2 * LIVE, experts * 2 * capacity)

    slots = jnp.stack((x_rows[0, 0], cot_rows[0, 0]), axis=1)
    keep = (block_rank.reshape(()) < kept_blocks.reshape(())).astype(jnp.float32)
    keep = jnp.broadcast_to(keep, (8, w_gate.shape[2]))
    got = exchange(slots, EXPERT)
    got, both, back, keep = lax.optimization_barrier((got, both, back, keep))
    got = got.reshape(experts * 2 * capacity, width)
    packed = dot(both, got).astype(jnp.bfloat16)
    column = lax.all_gather(packed, "z_hi", axis=0, tiled=True)
    group = exchange(fan_out(column, 16), PLANE)
    term, hidden, gate_grad, up_grad = middle(
        keep, group, w_gate[0], w_up[0], w_down[0]
    )
    parts = exchange(term, PLANE)
    plane_sum = jnp.sum(parts.astype(jnp.float32), axis=0).astype(jnp.bfloat16)
    plane_sum, hidden, gate_grad, up_grad = lax.optimization_barrier(
        (plane_sum, hidden, gate_grad, up_grad)
    )
    parts = exchange(plane_sum.reshape(4, LIVE, width), "z_hi")
    row_grads = jnp.sum(parts.astype(jnp.float32), axis=0).astype(jnp.bfloat16)
    slot_grads = dot(back, row_grads)
    slot_grads = slot_grads.astype(jnp.bfloat16).reshape(experts, capacity, width)
    grad_rows = exchange(slot_grads, EXPERT)[None, None]

    rows = group[:, : 4 * LIVE].reshape(64 * LIVE, width)
    cots = group[:, 4 * LIVE :].reshape(64 * LIVE, width)
    grad_down = dot(hidden, cots, TN).astype(jnp.bfloat16)
    grad_gate = dot(rows, gate_grad, TN).astype(jnp.bfloat16)
    grad_up = dot(rows, up_grad, TN).astype(jnp.bfloat16)
    return (grad_rows, grad_gate[None], grad_up[None], grad_down[None])


def solution(mesh):
    fine = Mesh(np.asarray(mesh.devices).reshape(4, 2, 4, 4, 4), EXPERT + DP)
    in_specs = (
        P(EXPERT, DP, None, None, None),
        P(EXPERT, DP, None, None, None),
        P(None, DP, None),
        P(EXPERT, None, DP),
        P(EXPERT, None, DP),
        P(EXPERT, DP, None),
        P(EXPERT),
        P(EXPERT, DP),
    )
    out_specs = (
        P(EXPERT, DP, None, None, None),
        P(EXPERT, None, DP),
        P(EXPERT, None, DP),
        P(EXPERT, DP, None),
    )
    return jax.shard_map(body, mesh=fine, in_specs=in_specs, out_specs=out_specs, check_vma=False)
```

time: 169 us -> 151 us (0.89)
  waiting for transfers between devices: 73.4 us -> 12.5 us
  blocking collectives: 23.2 us -> 78.8 us
  starting transfers between devices: 47.6 us -> 32.8 us
  Pallas kernels: 0 us -> 8.24 us
  local copies, waits for them, and re-layouts: 8.64 us -> 5.14 us
  matrix products: 8.86 us -> 6.04 us
    all_to_all x5 -> x3, waiting for transfers between devices: 73.4 us -> 12.5 us  [exchange(): return lax.all_to_all(array, axes, split_axis=0, concat_axis=0, tiled=True)]
    all_to_all x1 -> x2, blocking collectives: 23.2 us -> 59.9 us  [exchange(): return lax.all_to_all(array, axes, split_axis=0, concat_axis=0, tiled=True)]
    all_gather x0 -> x1, blocking collectives: none -> 18.8 us  [body(): column = lax.all_gather(packed, 'z_hi', axis=0, tiled=True)]
    all_to_all x5 -> x3, starting transfers between devices: 47.6 us -> 32.8 us  [exchange(): return lax.all_to_all(array, axes, split_axis=0, concat_axis=0, tiled=True)]
    pallas_call x0 -> x2, Pallas kernels: none -> 8.24 us  [the longest x1 4.4 us: fan_out(): pl.pallas_call(fan_kernel, out_shape=jax.ShapeDtypeStruct((receivers, siz...]
    dot_general x10 -> x5, matrix products: 8.86 us -> 6.04 us  [dot(): lax.dot_general(left, right, dims, preferred_element_type=jnp.float32)]
    broadcast_in_dim x3 -> x1, local copies, waits for them, and re-layouts: 2.13 us -> 0.01 us  [body(): keep = jnp.broadcast_to(keep, (8, w_gate.shape[2]))]
    concatenate x1 -> x0, other arithmetic: 1.9 us -> none  [body(): slots = jnp.concatenate((x_rows[0, 0], cot_rows[0, 0]), axis=1)]
  transfers between devices with their start and end apart: 5 -> 3, of which waited for: 5 -> 3; matrix products, arithmetic and copies ran while one was open for 3% -> 6% of each run, Pallas kernels for 0% -> 0%
where the time goes in v3:
time: 151 us; the launch traced here: 150 us
  blocking collectives  78.8 us (52%)
  starting transfers between devices  32.8 us (22%)
  waiting for transfers between devices  12.5 us (8%)
  Pallas kernels  8.24 us (5%)
  matrix products  6.04 us (4%)
  local copies, waits for them, and re-layouts  5.14 us (3%)
  other arithmetic  4.81 us (3%)
  between operations  2.04 us (1%)
    all_to_all x2, blocking collectives, exchange(): return lax.all_to_all(array, axes, split_axis=0, concat_axis=0, tiled=True)  59.9 us
    all_to_all x3, starting transfers between devices, exchange(): return lax.all_to_all(array, axes, split_axis=0, concat_axis=0, tiled=True)  32.8 us
    all_gather x1, blocking collectives, body(): column = lax.all_gather(packed, 'z_hi', axis=0, tiled=True)  18.8 us
    all_to_all x3, waiting for transfers between devices, exchange(): return lax.all_to_all(array, axes, split_axis=0, concat_axis=0, tiled=True)  12.5 us
    dot_general x5, matrix products, dot(): lax.dot_general(left, right, dims, preferred_element_type=jnp.float32)  6.04 us
    pallas_call x1, Pallas kernels, fan_out(): pl.pallas_call(fan_kernel, out_shape=jax.ShapeDtypeStruct((receivers, siz...  4.4 us
    pallas_call x1, Pallas kernels, middle(): pl.pallas_call(middle_kernel, out_shape=(jax.ShapeDtypeStruct((blocks, pa...  3.84 us
  transfers between devices with their start and end apart: 3, of which 3 were waited for; matrix products, arithmetic and copies ran while one was open for 6% of the time, Pallas kernels for 0%

profile of v3, /device:TPU:1, one launch (start us, length us, event | category | flops | bytes accessed | tf_op | source)
XLA Modules:
  0.0 150.3 jit_solution(9934821178942859805)
XLA Ops:
  0.6 1.9 %pad_maximum_fusion = bf16[8,2,2,3072]{3,2,1,0:T(2,128)(2,1)} fusion(bf16[8,1,2,3072]{3,2,1,0:T(2,128)(2,1)} %bitcast.42, bf16[8,1,2,3072]{3,2,1,0:T(2,128)(2,1)} %bitcast.43), kind=kLoop, calls=%fused_computation.8 | loop fusion | flops 98304 | bytes 393216 | tf_op jit(solution)/shard_map/stack | solution.py:146
  2.5 10.2 %all-to-all-start = ((bf16[8,2,2,3072]{3,2,1,0:T(2,128)(2,1)}), bf16[8,2,2,3072]{3,2,1,0:T(2,128)(2,1)S(1)}, u32[]{:S(2)}, u32[]{:S(2)}) async-start(bf16[8,2,2,3072]{3,2,1,0:T(2,128)(2,1)} %pad_maximum_fusion), calls=%async_computation | async-start | bytes 393216 | tf_op jit(solution)/shard_map/all_to_all | solution.py:36
  12.7 0.8 select_reduce_fusion.1
  13.5 0.1 select_reduce_fusion
  13.6 0.1 add_select_fusion
  13.7 0.1 compare_convert_fusion
  13.8 0.1 broadcast_multiply_fusion
  13.9 0.1 mul.24
  14.0 0.1 lt.58
  14.0 0.1 lt.59
  14.1 0.1 lt.60
  14.2 0.1 add.28
  14.3 0.1 add.29
  15.7 0.1 fusion.3
  15.7 3.4 %all-to-all-done = bf16[8,2,2,3072]{3,2,1,0:T(2,128)(2,1)S(1)} async-done(((bf16[8,2,2,3072]{3,2,1,0:T(2,128)(2,1)}), bf16[8,2,2,3072]{3,2,1,0:T(2,128)(2,1)S(1)}, u32[]{:S(2)}, u32[]{:S(2)}) %all-to-all-start) | async-done | bytes 196640 | tf_op jit(solution)/shard_map/all_to_all | solution.py:36
  19.2 0.1 reshape.99
  19.2 0.2 convolution_convert_fusion.4
  19.4 18.8 %all_gather.3.column = bf16[32,3072]{1,0:T(8,128)(2,1)S(1)} all-gather(bf16[8,3072]{1,0:T(8,128)(2,1)S(1)} %convolution_convert_fusion.4), channel_id=1, replica_groups=mesh['z_lo'=4,'core'=2,'z_hi'=4,'x'=4,'y'=4] {'z_hi'}, dimensions={0}, use_global_device_ids=true | all-gather | bytes 245760 | tf_op jit(solution)/shard_map/all_gather | solution.py:153
  38.3 4.4 %shard_map.111 = bf16[16,32,3072]{2,1,0:T(8,128)(2,1)S(1)} custom-call(bf16[32,3072]{1,0:T(8,128)(2,1)S(1)} %all_gather.3.column), custom_call_target="tpu_custom_call" | custom-call | tf_op jit(solution)/shard_map/pallas_call | solution.py:56
  42.7 0.0 copy-start
  42.7 0.0 copy-start.1
  42.7 0.0 copy-start.2
  42.7 40.2 %all_to_all.25.group = bf16[16,32,3072]{2,1,0:T(8,128)(2,1)S(1)} all-to-all(bf16[16,32,3072]{2,1,0:T(8,128)(2,1)S(1)} %shard_map.111), channel_id=1, replica_groups=mesh['z_lo'=4,'core'=2,'z_hi'=4,'x'=4,'y'=4] {'x','y'}, dimensions={0} | all-to-all | bytes 6291456 | tf_op jit(solution)/shard_map/all_to_all | solution.py:36
  82.9 0.0 copy-done
  82.9 0.0 copy-done.1
  82.9 0.0 copy-done.2
  82.9 3.8 %shard_map.112 = (bf16[16,16,3072]{2,1,0:T(8,128)(2,1)S(1)}, bf16[256,128]{1,0:T(8,128)(2,1)S(1)}, bf16[256,128]{1,0:T(8,128)(2,1)S(1)}, bf16[256,128]{1,0:T(8,128)(2,1)S(1)}) custom-call(f32[8,128]{1,0:T(8,128)S(1)} %broadcast_in_dim.59.keep_row, bf16[16,32,3072]{2,1,0:T(8,128)(2,1)S(1)} %all_to_all.25.group, bf16[3072,128]{1,0:T(8,128)(2,1)S(1)} %bitcast.35, ...), custom_call_target="tpu_custom_call" | custom-call | flops 1006632960 | bytes 8388608 | tf_op jit(solution)/shard_map/pallas_call | solution.py:114
  86.7 19.7 %all_to_all.26 = bf16[16,16,3072]{2,1,0:T(8,128)(2,1)} all-to-all(bf16[16,16,3072]{2,1,0:T(8,128)(2,1)S(1)} %get-tuple-element.20), channel_id=1, replica_groups=mesh['z_lo'=4,'core'=2,'z_hi'=4,'x'=4,'y'=4] {'x','y'}, dimensions={0} | all-to-all | bytes 3145728 | tf_op jit(solution)/shard_map/all_to_all | solution.py:36
  106.5 1.6 %reduce_sum.44 = bf16[16,3072]{1,0:T(8,128)(2,1)S(1)} reduce(bf16[16,16,3072]{2,1,0:T(8,128)(2,1)} %all_to_all.26, bf16[]{:T(256)} %constant.21.clone.1), dimensions={0}, to_apply=%region_2.3 | reduce | flops 737280 | bytes 1671170 | tf_op jit(solution)/shard_map/reduce_sum | solution.py:159
  108.1 0.7 reshape.100
  108.8 6.4 %all-to-all-start.3 = ((bf16[4,4,3072]{2,1,0:T(4,128)(2,1)}), bf16[4,4,3072]{2,1,0:T(4,128)(2,1)S(1)}, u32[]{:S(2)}, u32[]{:S(2)}) async-start(bf16[4,4,3072]{2,1,0:T(4,128)(2,1)} %reshape.100), calls=%async_computation.3 | async-start | bytes 196608 | tf_op jit(solution)/shard_map/all_to_all | solution.py:36
  115.2 1.4 fusion.4
  116.6 0.0 copy-start.3
  116.6 1.1 copy-done.3
  117.7 1.5 %fusion = bf16[1,3072,128]{2,1,0:T(8,128)(2,1)} fusion(bf16[256,3072]{1,0:T(8,128)(2,1)S(1)} %bitcast.38, bf16[256,128]{1,0:T(8,128)(2,1)S(1)} %get-tuple-element.25), kind=kOutput, calls=%fused_computation.3 | convolution fusion | flops 201719808 | bytes 2424832 | tf_op jit(solution)/shard_map/dot_general | solution.py:22
  119.2 0.0 copy-start.4
  119.2 7.8 %all-to-all-done.3 = bf16[4,4,3072]{2,1,0:T(4,128)(2,1)S(1)} async-done(((bf16[4,4,3072]{2,1,0:T(4,128)(2,1)}), bf16[4,4,3072]{2,1,0:T(4,128)(2,1)S(1)}, u32[]{:S(2)}, u32[]{:S(2)}) %all-to-all-start.3) | async-done | bytes 98336 | tf_op jit(solution)/shard_map/all_to_all | solution.py:36
  127.0 0.1 reduce_sum.45
  127.1 0.1 convolution_convert_fusion.3
  127.2 0.7 reshape.101
  127.9 16.2 %all-to-all-start.4 = ((bf16[8,2,3072]{2,1,0:T(2,128)(2,1)}), bf16[8,2,3072]{2,1,0:T(2,128)(2,1)S(1)}, u32[]{:S(2)}, u32[]{:S(2)}) async-start(bf16[8,2,3072]{2,1,0:T(2,128)(2,1)} %reshape.101), calls=%async_computation.4 | async-start | bytes 196608 | tf_op jit(solution)/shard_map/all_to_all | solution.py:36
  144.2 2.9 %fusion.1 = bf16[1,3072,128]{2,1,0:T(8,128)(2,1)} fusion(bf16[256,3072]{1,0:T(8,128)(2,1)} %bitcast.39, bf16[256,128]{1,0:T(8,128)(2,1)S(1)} %get-tuple-element.26), kind=kOutput, calls=%fused_computation.4 | convolution fusion | flops 201719808 | bytes 2424832 | tf_op jit(solution)/shard_map/dot_general | solution.py:22
  147.1 0.0 copy-done.4
  147.1 1.3 fusion.2
  148.4 1.3 all-to-all-done.4
  149.6 0.6 copy.16
  (5 shorter events, 0.0 us)
Async XLA Ops:
  2.5 16.6 %all-to-all-start = ((bf16[8,2,2,3072]{3,2,1,0:T(2,128)(2,1)}), bf16[8,2,2,3072]{3,2,1,0:T(2,128)(2,1)S(1)}, u32[]{:S(2)}, u32[]{:S(2)}) async-start(bf16[8,2,2,3072]{3,2,1,0:T(2,128)(2,1)} %pad_maximum_fusion), calls=%async_computation | async-start | bytes 393216 | tf_op jit(solution)/shard_map/all_to_all | solution.py:36
  42.7 40.2 %copy-start = (bf16[1,3072,128]{2,1,0:T(8,128)(2,1)S(1)}, bf16[1,3072,128]{2,1,0:T(8,128)(2,1)}, u32[]{:S(2)}) copy-start(bf16[1,3072,128]{2,1,0:T(8,128)(2,1)} %param.11) | copy-start | bytes 2359300
  42.7 40.2 %copy-start.1 = (bf16[1,3072,128]{2,1,0:T(8,128)(2,1)S(1)}, bf16[1,3072,128]{2,1,0:T(8,128)(2,1)}, u32[]{:S(2)}) copy-start(bf16[1,3072,128]{2,1,0:T(8,128)(2,1)} %param.12) | copy-start | bytes 2359300
  42.7 40.2 %copy-start.2 = (bf16[1,128,3072]{2,1,0:T(8,128)(2,1)S(1)}, bf16[1,128,3072]{2,1,0:T(8,128)(2,1)}, u32[]{:S(2)}) copy-start(bf16[1,128,3072]{2,1,0:T(8,128)(2,1)} %param.13) | copy-start | bytes 2359300
  108.8 18.2 %all-to-all-start.3 = ((bf16[4,4,3072]{2,1,0:T(4,128)(2,1)}), bf16[4,4,3072]{2,1,0:T(4,128)(2,1)S(1)}, u32[]{:S(2)}, u32[]{:S(2)}) async-start(bf16[4,4,3072]{2,1,0:T(4,128)(2,1)} %reshape.100), calls=%async_computation.3 | async-start | bytes 196608 | tf_op jit(solution)/shard_map/all_to_all | solution.py:36
  116.6 1.1 copy-start.3
  119.2 27.8 %copy-start.4 = (bf16[16,16,3072]{2,1,0:T(8,128)(2,1)S(1)}, bf16[16,16,3072]{2,1,0:T(8,128)(2,1)}, u32[]{:S(2)}) copy-start(bf16[16,16,3072]{2,1,0:T(8,128)(2,1)} %get-tuple-element.28) | copy-start | bytes 4718596
  127.9 21.7 %all-to-all-start.4 = ((bf16[8,2,3072]{2,1,0:T(2,128)(2,1)}), bf16[8,2,3072]{2,1,0:T(2,128)(2,1)S(1)}, u32[]{:S(2)}, u32[]{:S(2)}) async-start(bf16[8,2,3072]{2,1,0:T(2,128)(2,1)} %reshape.101), calls=%async_computation.4 | async-start | bytes 196608 | tf_op jit(solution)/shard_map/all_to_all | solution.py:36

commit v4 on v3

--- a/solution.py
+++ b/solution.py
@@ -9,7 +9,6 @@
 
 LIVE = 4
 EXPERT = ("z_lo", "core")
-PLANE = ("x", "y")
 DP = ("z_hi", "x", "y")
 STEP = 512
 NN = (((1,), (0,)), ((), ()))
@@ -32,38 +31,49 @@
     return (row == target[None]).astype(jnp.bfloat16)
 
 
-def exchange(array, axes):
-    return lax.all_to_all(array, axes, split_axis=0, concat_axis=0, tiled=True)
-
-
-def fan_kernel(column, fan, ordered, sems):
+CHIP_PLANE = ("core", "x", "y")
+ALONG_X = [[x * 4 + y for x in range(4)] for y in range(4)]
+ALONG_Y = [[x * 4 + y for y in range(4)] for x in range(4)]
+
+
+def per_core(first, second):
+    return first + [[16 + place for place in group] for group in second]
+
+
+NEAR = per_core(ALONG_X, ALONG_Y)
+FAR = per_core(ALONG_Y, ALONG_X)
+WHOLE = per_core([sum(ALONG_X, [])], [sum(ALONG_Y, [])])
+
+
+def exchange(array, axes, groups=None):
+    return lax.all_to_all(
+        array, axes, split_axis=0, concat_axis=0, axis_index_groups=groups, tiled=True
+    )
+
+
+def order_kernel(column, fan):
     size = column.shape[0]
     out = lax.broadcasted_iota(jnp.int32, (size, size), 0)
     source = ((out & 15) >> 2) * 8 + (out >> 4) * 4 + (out & 3)
     order = (source == lax.broadcasted_iota(jnp.int32, (size, size), 1)).astype(jnp.bfloat16)
-    ordered[...] = dot(order, column[...]).astype(jnp.bfloat16)
-    copies = [
-        pltpu.make_async_copy(ordered, fan.at[i], sems.at[i]) for i in range(fan.shape[0])
-    ]
-    for copy in copies:
-        copy.start()
-    for copy in copies:
-        copy.wait()
-
-
-def fan_out(column, receivers):
-    size, width = column.shape
+    ordered = dot(order, column[...]).astype(jnp.bfloat16)
+    for i in range(fan.shape[0]):
+        fan[i] = ordered
+
+
+def copy_kernel(block, fan):
+    for i in range(fan.shape[0]):
+        fan[i] = block[...]
+
+
+def fan_out(kernel, block, receivers):
     return pl.pallas_call(
-        fan_kernel,
-        out_shape=jax.ShapeDtypeStruct((receivers, size, width), jnp.bfloat16),
+        kernel,
+        out_shape=jax.ShapeDtypeStruct((receivers,) + block.shape, jnp.bfloat16),
         in_specs=[pl.BlockSpec(memory_space=pltpu.VMEM)],
-        out_specs=pl.BlockSpec(memory_space=pl.ANY),
-        scratch_shapes=[
-            pltpu.VMEM((size, width), jnp.bfloat16),
-            pltpu.SemaphoreType.DMA((receivers,)),
-        ],
+        out_specs=pl.BlockSpec(memory_space=pltpu.VMEM),
         compiler_params=pltpu.CompilerParams(vmem_limit_bytes=VMEM_LIMIT),
-    )(column)
+    )(block)
 
 
 def middle_kernel(
@@ -151,26 +161,30 @@
     got = got.reshape(experts * 2 * capacity, width)
     packed = dot(both, got).astype(jnp.bfloat16)
     column = lax.all_gather(packed, "z_hi", axis=0, tiled=True)
-    group = exchange(fan_out(column, 16), PLANE)
+    line = exchange(fan_out(order_kernel, column, 4), CHIP_PLANE, NEAR)
+    group = exchange(fan_out(copy_kernel, line, 4), CHIP_PLANE, FAR)
+    group = group.reshape(16, 8 * LIVE, width)
     term, hidden, gate_grad, up_grad = middle(
         keep, group, w_gate[0], w_up[0], w_down[0]
     )
-    parts = exchange(term, PLANE)
+    parts = exchange(term, CHIP_PLANE, WHOLE)
     plane_sum = jnp.sum(parts.astype(jnp.float32), axis=0).astype(jnp.bfloat16)
-    plane_sum, hidden, gate_grad, up_grad = lax.optimization_barrier(
-        (plane_sum, hidden, gate_grad, up_grad)
+    plane_sum, group, hidden, gate_grad, up_grad = lax.optimization_barrier(
+        (plane_sum, group, hidden, gate_grad, up_grad)
     )
     parts = exchange(plane_sum.reshape(4, LIVE, width), "z_hi")
-    row_grads = jnp.sum(parts.astype(jnp.float32), axis=0).astype(jnp.bfloat16)
-    slot_grads = dot(back, row_grads)
-    slot_grads = slot_grads.astype(jnp.bfloat16).reshape(experts, capacity, width)
-    grad_rows = exchange(slot_grads, EXPERT)[None, None]
-
     rows = group[:, : 4 * LIVE].reshape(64 * LIVE, width)
     cots = group[:, 4 * LIVE :].reshape(64 * LIVE, width)
     grad_down = dot(hidden, cots, TN).astype(jnp.bfloat16)
     grad_gate = dot(rows, gate_grad, TN).astype(jnp.bfloat16)
     grad_up = dot(rows, up_grad, TN).astype(jnp.bfloat16)
+    parts, grad_gate, grad_up, grad_down = lax.optimization_barrier(
+        (parts, grad_gate, grad_up, grad_down)
+    )
+    row_grads = jnp.sum(parts.astype(jnp.float32), axis=0).astype(jnp.bfloat16)
+    slot_grads = dot(back, row_grads)
+    slot_grads = slot_grads.astype(jnp.bfloat16).reshape(experts, capacity, width)
+    grad_rows = exchange(slot_grads, EXPERT)[None, None]
     return (grad_rows, grad_gate[None], grad_up[None], grad_down[None])
 
 

time: 151 us -> 140 us (0.927)
  starting transfers between devices: 32.8 us -> 16.5 us
  blocking collectives: 78.8 us -> 94.5 us
  Pallas kernels: 8.24 us -> 4.23 us
  local copies, waits for them, and re-layouts: 5.14 us -> 2.17 us
  waiting for transfers between devices: 12.5 us -> 10.7 us
    all_to_all x3 -> x2, starting transfers between devices: 32.8 us -> 16.5 us  [exchange(): lax.all_to_all(array, axes, split_axis=0, concat_axis=0, axis_index_group...]
    all_to_all x2 -> x4, blocking collectives: 59.9 us -> 75.7 us  [exchange(): lax.all_to_all(array, axes, split_axis=0, concat_axis=0, axis_index_group...]
    pallas_call x1 -> x2, Pallas kernels: 4.4 us -> 0.39 us  [fan_out(): pl.pallas_call(kernel, out_shape=jax.ShapeDtypeStruct((receivers,) + bloc...]
    all_to_all x3 -> x2, waiting for transfers between devices: 12.5 us -> 10.7 us  [exchange(): lax.all_to_all(array, axes, split_axis=0, concat_axis=0, axis_index_group...]
  transfers between devices with their start and end apart: 3 -> 2, of which waited for: 3 -> 2; matrix products, arithmetic and copies ran while one was open for 6% -> 4% of each run, Pallas kernels for 0% -> 0%
where the time goes in v4:
time: 140 us
  blocking collectives  94.5 us (68%)
  starting transfers between devices  16.5 us (12%)
  waiting for transfers between devices  10.7 us (8%)
  other arithmetic  4.82 us (3%)
  matrix products  4.65 us (3%)
  Pallas kernels  4.23 us (3%)
  local copies, waits for them, and re-layouts  2.17 us (2%)
  between operations  2.04 us (1%)
    all_to_all x4, blocking collectives, exchange(): lax.all_to_all(array, axes, split_axis=0, concat_axis=0, axis_index_group...  75.7 us
    all_gather x1, blocking collectives, body(): column = lax.all_gather(packed, 'z_hi', axis=0, tiled=True)  18.8 us
    all_to_all x2, starting transfers between devices, exchange(): lax.all_to_all(array, axes, split_axis=0, concat_axis=0, axis_index_group...  16.5 us
    all_to_all x2, waiting for transfers between devices, exchange(): lax.all_to_all(array, axes, split_axis=0, concat_axis=0, axis_index_group...  10.7 us
    dot_general x5, matrix products, dot(): lax.dot_general(left, right, dims, preferred_element_type=jnp.float32)  4.65 us
    pallas_call x1, Pallas kernels, middle(): pl.pallas_call(middle_kernel, out_shape=(jax.ShapeDtypeStruct((blocks, pa...  3.83 us
  transfers between devices with their start and end apart: 2, of which 2 were waited for; matrix products, arithmetic and copies ran while one was open for 4% of the time, Pallas kernels for 0%

profile of v4, /device:TPU:1, one launch (start us, length us, event | category | flops | bytes accessed | tf_op | source)
XLA Modules:
  0.0 139.7 jit_solution(17908543863384489855)
XLA Ops:
  0.6 1.9 %pad_maximum_fusion = bf16[8,2,2,3072]{3,2,1,0:T(2,128)(2,1)} fusion(bf16[8,1,2,3072]{3,2,1,0:T(2,128)(2,1)} %bitcast.45, bf16[8,1,2,3072]{3,2,1,0:T(2,128)(2,1)} %bitcast.46), kind=kLoop, calls=%fused_computation.5 | loop fusion | flops 98304 | bytes 393216 | tf_op jit(solution)/shard_map/stack | solution.py:156
  2.5 10.2 %all-to-all-start = ((bf16[8,2,2,3072]{3,2,1,0:T(2,128)(2,1)}), bf16[8,2,2,3072]{3,2,1,0:T(2,128)(2,1)S(1)}, u32[]{:S(2)}, u32[]{:S(2)}) async-start(bf16[8,2,2,3072]{3,2,1,0:T(2,128)(2,1)} %pad_maximum_fusion), calls=%async_computation | async-start | bytes 393216 | tf_op jit(solution)/shard_map/all_to_all | solution.py:49
  12.7 0.8 select_reduce_fusion.1
  13.5 0.1 select_reduce_fusion
  13.6 0.1 add_select_fusion
  13.7 0.1 compare_convert_fusion
  15.1 0.1 add.28
  15.1 0.1 add.29
  15.2 0.1 lt.59
  15.3 0.1 lt.60
  15.4 0.1 lt.58
  15.5 0.1 broadcast_multiply_fusion
  15.6 0.1 mul.24
  15.7 0.1 fusion
  15.7 3.4 %all-to-all-done = bf16[8,2,2,3072]{3,2,1,0:T(2,128)(2,1)S(1)} async-done(((bf16[8,2,2,3072]{3,2,1,0:T(2,128)(2,1)}), bf16[8,2,2,3072]{3,2,1,0:T(2,128)(2,1)S(1)}, u32[]{:S(2)}, u32[]{:S(2)}) %all-to-all-start) | async-done | bytes 196640 | tf_op jit(solution)/shard_map/all_to_all | solution.py:49
  19.2 0.1 reshape.102
  19.2 0.2 convolution_convert_fusion.4
  19.4 18.8 %all_gather.3.column = bf16[32,3072]{1,0:T(8,128)(2,1)S(1)} all-gather(bf16[8,3072]{1,0:T(8,128)(2,1)S(1)} %convolution_convert_fusion.4), channel_id=1, replica_groups=mesh['z_lo'=4,'core'=2,'z_hi'=4,'x'=4,'y'=4] {'z_hi'}, dimensions={0}, use_global_device_ids=true | all-gather | bytes 245760 | tf_op jit(solution)/shard_map/all_gather | solution.py:163
  38.3 0.2 shard_map.111
  38.5 12.3 %all_to_all.30.block = bf16[4,32,3072]{2,1,0:T(8,128)(2,1)S(1)} all-to-all(bf16[4,32,3072]{2,1,0:T(8,128)(2,1)S(1)} %shard_map.111), channel_id=1, replica_groups={{0,4,8,12},{1,5,9,13},{2,6,10,14},{3,7,11,15},{64,65,66,67},{68,69,70,7..., dimensions={0} | all-to-all | bytes 1572864 | tf_op jit(solution)/shard_map/all_to_all | solution.py:49
  50.8 0.2 shard_map.112
  51.0 0.0 copy-start
  51.0 0.0 copy-start.1
  51.0 0.0 copy-start.2
  51.0 25.2 %all_to_all.31 = bf16[4,4,32,3072]{3,2,1,0:T(8,128)(2,1)S(1)} all-to-all(bf16[4,4,32,3072]{3,2,1,0:T(8,128)(2,1)S(1)} %shard_map.112), channel_id=1, replica_groups={{0,1,2,3},{4,5,6,7},{8,9,10,11},{12,13,14,15},{64,68,72,76},{65,69,73,7..., dimensions={0} | all-to-all | bytes 6291456 | tf_op jit(solution)/shard_map/all_to_all | solution.py:49
  76.2 0.0 copy-done
  76.2 0.0 copy-done.1
  76.2 0.0 copy-done.2
  76.3 3.8 %shard_map.113 = (bf16[16,16,3072]{2,1,0:T(8,128)(2,1)S(1)}, bf16[256,128]{1,0:T(8,128)(2,1)S(1)}, bf16[256,128]{1,0:T(8,128)(2,1)S(1)}, bf16[256,128]{1,0:T(8,128)(2,1)S(1)}) custom-call(f32[8,128]{1,0:T(8,128)S(1)} %broadcast_in_dim.59.keep_row, bf16[16,32,3072]{2,1,0:T(8,128)(2,1)S(1)} %bitcast.33, bf16[3072,128]{1,0:T(8,128)(2,1)S(1)} %bitcast.35, ...), custom_call_target="tpu_custom_call" | custom-call | flops 1006632960 | bytes 8388608 | tf_op jit(solution)/shard_map/pallas_call | solution.py:124
  80.1 18.3 %all_to_all.32 = bf16[16,16,3072]{2,1,0:T(8,128)(2,1)} all-to-all(bf16[16,16,3072]{2,1,0:T(8,128)(2,1)S(1)} %get-tuple-element.25), channel_id=1, replica_groups={{0,4,8,12,1,5,9,13,2,6,10,14,3,7,11,15},{64,65,66,67,68,69,70,71,72,73,..., dimensions={0} | all-to-all | bytes 3145728 | tf_op jit(solution)/shard_map/all_to_all | solution.py:49
  98.4 1.6 %reduce_sum.44 = bf16[16,3072]{1,0:T(8,128)(2,1)S(1)} reduce(bf16[16,16,3072]{2,1,0:T(8,128)(2,1)} %all_to_all.32, bf16[]{:T(256)} %constant.21.clone.1), dimensions={0}, to_apply=%region_2.3 | reduce | flops 737280 | bytes 1671170 | tf_op jit(solution)/shard_map/reduce_sum | solution.py:171
  100.1 0.7 reshape.104
  100.8 6.4 %all-to-all-start.4 = ((bf16[4,4,3072]{2,1,0:T(4,128)(2,1)}), bf16[4,4,3072]{2,1,0:T(4,128)(2,1)S(1)}, u32[]{:S(2)}, u32[]{:S(2)}) async-start(bf16[4,4,3072]{2,1,0:T(4,128)(2,1)} %reshape.104), calls=%async_computation.4 | async-start | bytes 196608 | tf_op jit(solution)/shard_map/all_to_all | solution.py:49
  107.1 0.2 fusion.1
  107.4 1.5 %convolution_convert_fusion.1 = bf16[3072,128]{1,0:T(8,128)(2,1)} fusion(bf16[256,3072]{1,0:T(8,128)(2,1)S(1)} %bitcast.38, bf16[256,128]{1,0:T(8,128)(2,1)S(1)} %get-tuple-element.32), kind=kOutput, calls=%fused_computation.1 | convolution fusion | flops 201719808 | bytes 2424832 | tf_op jit(solution)/shard_map/dot_general | solution.py:21
  108.9 1.5 %convolution_convert_fusion.2 = bf16[3072,128]{1,0:T(8,128)(2,1)} fusion(bf16[256,3072]{1,0:T(8,128)(2,1)S(1)} %bitcast.39, bf16[256,128]{1,0:T(8,128)(2,1)S(1)} %get-tuple-element.31), kind=kOutput, calls=%fused_computation.2 | convolution fusion | flops 201719808 | bytes 2424832 | tf_op jit(solution)/shard_map/dot_general | solution.py:21
  110.4 1.3 convolution_convert_fusion
  111.7 7.3 %all-to-all-done.4 = bf16[4,4,3072]{2,1,0:T(4,128)(2,1)S(1)} async-done(((bf16[4,4,3072]{2,1,0:T(4,128)(2,1)}), bf16[4,4,3072]{2,1,0:T(4,128)(2,1)S(1)}, u32[]{:S(2)}, u32[]{:S(2)}) %all-to-all-start.4) | async-done | bytes 98336 | tf_op jit(solution)/shard_map/all_to_all | solution.py:49
  119.0 0.1 reduce_sum.45
  119.0 0.1 convolution_convert_fusion.3
  119.2 19.8 %all_to_all.33 = bf16[8,2,3072]{2,1,0:T(2,128)(2,1)S(1)} all-to-all(bf16[8,2,3072]{2,1,0:T(2,128)(2,1)S(1)} %reshape.107), channel_id=1, replica_groups=mesh['z_lo'=4,'core'=2,'z_hi'=4,'x'=4,'y'=4] {'z_lo','core'}, dimensions={0} | all-to-all | bytes 196608 | tf_op jit(solution)/shard_map/all_to_all | solution.py:49
  139.1 0.6 copy.16
  (6 shorter events, 0.1 us)
Async XLA Ops:
  2.5 16.6 %all-to-all-start = ((bf16[8,2,2,3072]{3,2,1,0:T(2,128)(2,1)}), bf16[8,2,2,3072]{3,2,1,0:T(2,128)(2,1)S(1)}, u32[]{:S(2)}, u32[]{:S(2)}) async-start(bf16[8,2,2,3072]{3,2,1,0:T(2,128)(2,1)} %pad_maximum_fusion), calls=%async_computation | async-start | bytes 393216 | tf_op jit(solution)/shard_map/all_to_all | solution.py:49
  51.0 25.3 %copy-start = (bf16[1,3072,128]{2,1,0:T(8,128)(2,1)S(1)}, bf16[1,3072,128]{2,1,0:T(8,128)(2,1)}, u32[]{:S(2)}) copy-start(bf16[1,3072,128]{2,1,0:T(8,128)(2,1)} %param.11) | copy-start | bytes 2359300
  51.0 25.2 %copy-start.1 = (bf16[1,3072,128]{2,1,0:T(8,128)(2,1)S(1)}, bf16[1,3072,128]{2,1,0:T(8,128)(2,1)}, u32[]{:S(2)}) copy-start(bf16[1,3072,128]{2,1,0:T(8,128)(2,1)} %param.12) | copy-start | bytes 2359300
  51.0 25.2 %copy-start.2 = (bf16[1,128,3072]{2,1,0:T(8,128)(2,1)S(1)}, bf16[1,128,3072]{2,1,0:T(8,128)(2,1)}, u32[]{:S(2)}) copy-start(bf16[1,128,3072]{2,1,0:T(8,128)(2,1)} %param.13) | copy-start | bytes 2359300
  100.8 18.2 %all-to-all-start.4 = ((bf16[4,4,3072]{2,1,0:T(4,128)(2,1)}), bf16[4,4,3072]{2,1,0:T(4,128)(2,1)S(1)}, u32[]{:S(2)}, u32[]{:S(2)}) async-start(bf16[4,4,3072]{2,1,0:T(4,128)(2,1)} %reshape.104), calls=%async_computation.4 | async-start | bytes 196608 | tf_op jit(solution)/shard_map/all_to_all | solution.py:49

commit v5 on v4

--- a/solution.py
+++ b/solution.py
@@ -41,8 +41,17 @@
 
 
 NEAR = per_core(ALONG_X, ALONG_Y)
-FAR = per_core(ALONG_Y, ALONG_X)
 WHOLE = per_core([sum(ALONG_X, [])], [sum(ALONG_Y, [])])
+
+
+def far_step(by):
+    along_y = [(x * 4 + y, x * 4 + (y + by) % 4) for x in range(4) for y in range(4)]
+    along_x = [(16 + x * 4 + y, 16 + (x + by) % 4 * 4 + y) for x in range(4) for y in range(4)]
+    return along_y + along_x
+
+
+def send(array, by):
+    return lax.ppermute(array, CHIP_PLANE, far_step(by))
 
 
 def exchange(array, axes, groups=None):
@@ -61,11 +70,6 @@
         fan[i] = ordered
 
 
-def copy_kernel(block, fan):
-    for i in range(fan.shape[0]):
-        fan[i] = block[...]
-
-
 def fan_out(kernel, block, receivers):
     return pl.pallas_call(
         kernel,
@@ -76,21 +80,26 @@
     )(block)
 
 
-def middle_kernel(
-    keep_row, group, w_gate, w_up, w_down, term, hidden, gate_grad, up_grad, sums, both
-):
-    blocks, pair, width = group.shape
-    half = pair // 2
+def middle_kernel(keep_row, *refs):
+    group, (w_gate, w_up, w_down) = refs[:7], refs[7:10]
+    term, rows, cots, hidden, gate_grad, up_grad, sums, both = refs[10:]
+    blocks, half, width = term.shape
     size = blocks * half
+    core = lax.axis_index("core")
+    place = jnp.where(core == 0, lax.axis_index("y"), lax.axis_index("x"))
     sums[...] = jnp.zeros_like(sums)
 
     def forward(i, carry):
         part = pl.ds(pl.multiple_of(i * STEP, STEP), STEP)
-        rows = group[:, :half, part].reshape(size, STEP)
-        cots = group[:, half:, part].reshape(size, STEP)
-        sums[0] += dot(rows, w_gate[part, :])
-        sums[1] += dot(rows, w_up[part, :])
-        sums[2] += dot(cots, w_down[:, part], NT)
+        start = 0
+        for block in group:
+            count = block.shape[0] * half
+            rows[start : start + count, part] = block[:, :half, part].reshape(count, STEP)
+            cots[start : start + count, part] = block[:, half:, part].reshape(count, STEP)
+            start += count
+        sums[0] += dot(rows[:, part], w_gate[part, :])
+        sums[1] += dot(rows[:, part], w_up[part, :])
+        sums[2] += dot(cots[:, part], w_down[:, part], NT)
         return carry
 
     lax.fori_loop(0, width // STEP, forward, 0)
@@ -109,28 +118,34 @@
         part = pl.ds(pl.multiple_of(i * STEP, STEP), STEP)
         weights = jnp.concatenate((w_gate[part, :], w_up[part, :]), axis=1)
         out = dot(both[...], weights, NT).astype(jnp.bfloat16)
-        term[:, :, part] = out.reshape(blocks, half, STEP)
+        for j, by in enumerate((0, 3, 1, 2)):
+            line = out[j * size // 4 : (j + 1) * size // 4].reshape(blocks // 4, half, STEP)
+            term[pl.ds(((place + by) & 3) * (blocks // 4), blocks // 4), :, part] = line
         return carry
 
     lax.fori_loop(0, width // STEP, backward, 0)
 
 
 def middle(keep, group, w_gate, w_up, w_down):
-    blocks, pair, width = group.shape
+    blocks = sum(block.shape[0] for block in group)
+    pair, width = group[0].shape[1:]
     units = w_gate.shape[1]
     size = blocks * pair // 2
     vmem = pl.BlockSpec(memory_space=pltpu.VMEM)
+    rows = jax.ShapeDtypeStruct((size, width), jnp.bfloat16)
     grads = jax.ShapeDtypeStruct((size, units), jnp.bfloat16)
     return pl.pallas_call(
         middle_kernel,
         out_shape=(
             jax.ShapeDtypeStruct((blocks, pair // 2, width), jnp.bfloat16),
+            rows,
+            rows,
             grads,
             grads,
             grads,
         ),
-        in_specs=[vmem, vmem, vmem, vmem, vmem],
-        out_specs=(vmem, vmem, vmem, vmem),
+        in_specs=[vmem] * 11,
+        out_specs=(vmem,) * 6,
         scratch_shapes=[
             pltpu.VMEM((3, size, units), jnp.float32),
             pltpu.VMEM((size, 2 * units), jnp.bfloat16),
@@ -139,7 +154,7 @@
         cost_estimate=pl.CostEstimate(
             flops=10 * size * units * width, bytes_accessed=8 * 2**20, transcendentals=size * units
         ),
-    )(keep, group, w_gate, w_up, w_down)
+    )(keep, *group, w_gate, w_up, w_down)
 
 
 def body(x_rows, cot_rows, counts, w_gate, w_up, w_down, kept_blocks, block_rank):
@@ -162,19 +177,18 @@
     packed = dot(both, got).astype(jnp.bfloat16)
     column = lax.all_gather(packed, "z_hi", axis=0, tiled=True)
     line = exchange(fan_out(order_kernel, column, 4), CHIP_PLANE, NEAR)
-    group = exchange(fan_out(copy_kernel, line, 4), CHIP_PLANE, FAR)
-    group = group.reshape(16, 8 * LIVE, width)
-    term, hidden, gate_grad, up_grad = middle(
-        keep, group, w_gate[0], w_up[0], w_down[0]
-    )
+    low, high = line[:2], line[2:]
+    left_low, right_high = send(low, 1), send(high, -1)
+    left_high, right_low = send(high, 1), send(low, -1)
+    far_low, far_high = send(left_low, 1), send(right_high, -1)
+    group = (line, left_low, left_high, right_low, right_high, far_low, far_high)
+    term, rows, cots, hidden, gate_grad, up_grad = middle(keep, group, w_gate[0], w_up[0], w_down[0])
     parts = exchange(term, CHIP_PLANE, WHOLE)
     plane_sum = jnp.sum(parts.astype(jnp.float32), axis=0).astype(jnp.bfloat16)
-    plane_sum, group, hidden, gate_grad, up_grad = lax.optimization_barrier(
-        (plane_sum, group, hidden, gate_grad, up_grad)
+    plane_sum, rows, cots, hidden, gate_grad, up_grad = lax.optimization_barrier(
+        (plane_sum, rows, cots, hidden, gate_grad, up_grad)
     )
     parts = exchange(plane_sum.reshape(4, LIVE, width), "z_hi")
-    rows = group[:, : 4 * LIVE].reshape(64 * LIVE, width)
-    cots = group[:, 4 * LIVE :].reshape(64 * LIVE, width)
     grad_down = dot(hidden, cots, TN).astype(jnp.bfloat16)
     grad_gate = dot(rows, gate_grad, TN).astype(jnp.bfloat16)
     grad_up = dot(rows, up_grad, TN).astype(jnp.bfloat16)

time: 140 us -> 142 us (1.014)
  blocking collectives: 94.5 us -> 69.7 us
  starting transfers between devices: 16.5 us -> 34.6 us
  waiting for transfers between devices: 10.7 us -> 19.1 us
    all_to_all x4 -> x3, blocking collectives: 75.7 us -> 50.9 us  [exchange(): lax.all_to_all(array, axes, split_axis=0, concat_axis=0, axis_index_group...]
    ppermute x0 -> x6, starting transfers between devices: none -> 18.1 us  [send(): return lax.ppermute(array, CHIP_PLANE, far_step(by))]
    ppermute x0 -> x6, waiting for transfers between devices: none -> 7.93 us  [send(): return lax.ppermute(array, CHIP_PLANE, far_step(by))]
  transfers between devices with their start and end apart: 2 -> 8, of which waited for: 2 -> 5; matrix products, arithmetic and copies ran while one was open for 4% -> 4% of each run, Pallas kernels for 0% -> 0%
where the time goes in v5:
time: 142 us; the launch traced here: 141 us
  blocking collectives  69.7 us (49%)
  starting transfers between devices  34.6 us (24%)
  waiting for transfers between devices  19.1 us (13%)
  other arithmetic  4.82 us (3%)
  matrix products  4.64 us (3%)
  Pallas kernels  4.02 us (3%)
  between operations  2.09 us (1%)
  local copies, waits for them, and re-layouts  1.99 us (1%)
    all_to_all x3, blocking collectives, exchange(): lax.all_to_all(array, axes, split_axis=0, concat_axis=0, axis_index_group...  50.9 us
    all_gather x1, blocking collectives, body(): column = lax.all_gather(packed, 'z_hi', axis=0, tiled=True)  18.8 us
    ppermute x6, starting transfers between devices, send(): return lax.ppermute(array, CHIP_PLANE, far_step(by))  18.1 us
    all_to_all x2, starting transfers between devices, exchange(): lax.all_to_all(array, axes, split_axis=0, concat_axis=0, axis_index_group...  16.5 us
    all_to_all x2, waiting for transfers between devices, exchange(): lax.all_to_all(array, axes, split_axis=0, concat_axis=0, axis_index_group...  11.2 us
    ppermute x6, waiting for transfers between devices, send(): return lax.ppermute(array, CHIP_PLANE, far_step(by))  7.93 us
    dot_general x5, matrix products, dot(): lax.dot_general(left, right, dims, preferred_element_type=jnp.float32)  4.64 us
    pallas_call x1, Pallas kernels, middle(): pl.pallas_call(middle_kernel, out_shape=(jax.ShapeDtypeStruct((blocks, pa...  3.83 us
  transfers between devices with their start and end apart: 8, of which 5 were waited for; matrix products, arithmetic and copies ran while one was open for 4% of the time, Pallas kernels for 0%

profile of v5, /device:TPU:1, one launch (start us, length us, event | category | flops | bytes accessed | tf_op | source)
XLA Modules:
  0.0 141.0 jit_solution(11260030980499570421)
XLA Ops:
  0.6 1.9 %pad_maximum_fusion = bf16[8,2,2,3072]{3,2,1,0:T(2,128)(2,1)} fusion(bf16[8,1,2,3072]{3,2,1,0:T(2,128)(2,1)} %bitcast.37, bf16[8,1,2,3072]{3,2,1,0:T(2,128)(2,1)} %bitcast.38), kind=kLoop, calls=%fused_computation.5 | loop fusion | flops 98304 | bytes 393216 | tf_op jit(solution)/shard_map/stack | solution.py:171
  2.5 10.2 %all-to-all-start = ((bf16[8,2,2,3072]{3,2,1,0:T(2,128)(2,1)}), bf16[8,2,2,3072]{3,2,1,0:T(2,128)(2,1)S(1)}, u32[]{:S(2)}, u32[]{:S(2)}) async-start(bf16[8,2,2,3072]{3,2,1,0:T(2,128)(2,1)} %pad_maximum_fusion), calls=%async_computation | async-start | bytes 393216 | tf_op jit(solution)/shard_map/all_to_all | solution.py:58
  12.7 0.8 select_reduce_fusion.1
  13.5 0.1 select_reduce_fusion
  13.6 0.1 add_select_fusion
  13.7 0.1 compare_convert_fusion
  15.1 0.1 add.28
  15.1 0.1 add.29
  15.2 0.1 lt.59
  15.3 0.1 lt.60
  15.4 0.1 lt.58
  15.5 0.1 broadcast_multiply_fusion
  15.6 0.1 mul.24
  15.7 0.1 fusion
  15.7 3.4 %all-to-all-done = bf16[8,2,2,3072]{3,2,1,0:T(2,128)(2,1)S(1)} async-done(((bf16[8,2,2,3072]{3,2,1,0:T(2,128)(2,1)}), bf16[8,2,2,3072]{3,2,1,0:T(2,128)(2,1)S(1)}, u32[]{:S(2)}, u32[]{:S(2)}) %all-to-all-start) | async-done | bytes 196640 | tf_op jit(solution)/shard_map/all_to_all | solution.py:58
  19.2 0.1 reshape.93
  19.2 0.2 convolution_convert_fusion.4
  19.4 18.8 %all_gather.3.column = bf16[32,3072]{1,0:T(8,128)(2,1)S(1)} all-gather(bf16[8,3072]{1,0:T(8,128)(2,1)S(1)} %convolution_convert_fusion.4), channel_id=1, replica_groups=mesh['z_lo'=4,'core'=2,'z_hi'=4,'x'=4,'y'=4] {'z_hi'}, dimensions={0}, use_global_device_ids=true | all-gather | bytes 245760 | tf_op jit(solution)/shard_map/all_gather | solution.py:178
  38.3 0.2 shard_map.111
  38.5 0.0 copy-start
  38.5 0.0 copy-start.1
  38.5 0.0 copy-start.2
  38.5 12.5 %all_to_all.25.refs_0_ = bf16[4,32,3072]{2,1,0:T(8,128)(2,1)S(1)} all-to-all(bf16[4,32,3072]{2,1,0:T(8,128)(2,1)S(1)} %shard_map.111), channel_id=1, replica_groups={{0,4,8,12},{1,5,9,13},{2,6,10,14},{3,7,11,15},{64,65,66,67},{68,69,70,7..., dimensions={0} | all-to-all | bytes 1572864 | tf_op jit(solution)/shard_map/all_to_all | solution.py:58
  51.0 0.1 fusion.1
  51.0 4.4 %collective-permute-start.3 = (bf16[2,32,3072]{2,1,0:T(8,128)(2,1)S(1)}, bf16[2,32,3072]{2,1,0:T(8,128)(2,1)S(1)}, u32[]{:S(2)}, u32[]{:S(2)}) collective-permute-start(bf16[2,32,3072]{2,1,0:T(8,128)(2,1)S(1)} %get-tuple-element.44), channel_id=1, source_target_pairs={{0,3},{1,0},{2,1},{3,2},{4,7},{5,4},{6,5},{7,6},{8,11},{9,8},{10,9... | collective-permute-start | bytes 1179656 | tf_op jit(solution)/shard_map/ppermute | solution.py:54
  55.4 1.9 %collective-permute-start = (bf16[2,32,3072]{2,1,0:T(8,128)(2,1)S(1)}, bf16[2,32,3072]{2,1,0:T(8,128)(2,1)S(1)}, u32[]{:S(2)}, u32[]{:S(2)}) collective-permute-start(bf16[2,32,3072]{2,1,0:T(8,128)(2,1)S(1)} %get-tuple-element.45), channel_id=1, source_target_pairs={{0,1},{1,2},{2,3},{3,0},{4,5},{5,6},{6,7},{7,4},{8,9},{9,10},{10,1... | collective-permute-start | bytes 1179656 | tf_op jit(solution)/shard_map/ppermute | solution.py:54
  57.3 2.1 %collective-permute-start.1 = (bf16[2,32,3072]{2,1,0:T(8,128)(2,1)S(1)}, bf16[2,32,3072]{2,1,0:T(8,128)(2,1)S(1)}, u32[]{:S(2)}, u32[]{:S(2)}) collective-permute-start(bf16[2,32,3072]{2,1,0:T(8,128)(2,1)S(1)} %get-tuple-element.44), channel_id=1, source_target_pairs={{0,1},{1,2},{2,3},{3,0},{4,5},{5,6},{6,7},{7,4},{8,9},{9,10},{10,1... | collective-permute-start | bytes 1179656 | tf_op jit(solution)/shard_map/ppermute | solution.py:54
  59.4 4.4 %collective-permute-start.2 = (bf16[2,32,3072]{2,1,0:T(8,128)(2,1)S(1)}, bf16[2,32,3072]{2,1,0:T(8,128)(2,1)S(1)}, u32[]{:S(2)}, u32[]{:S(2)}) collective-permute-start(bf16[2,32,3072]{2,1,0:T(8,128)(2,1)S(1)} %get-tuple-element.45), channel_id=1, source_target_pairs={{0,3},{1,0},{2,1},{3,2},{4,7},{5,4},{6,5},{7,6},{8,11},{9,8},{10,9... | collective-permute-start | bytes 1179656 | tf_op jit(solution)/shard_map/ppermute | solution.py:54
  63.8 0.0 collective-permute-done.3.refs_4_
  63.8 3.4 %collective-permute-start.5 = (bf16[2,32,3072]{2,1,0:T(8,128)(2,1)S(1)}, bf16[2,32,3072]{2,1,0:T(8,128)(2,1)S(1)}, u32[]{:S(2)}, u32[]{:S(2)}) collective-permute-start(bf16[2,32,3072]{2,1,0:T(8,128)(2,1)S(1)} %collective-permute-done.3.refs_4_), channel_id=1, source_target_pairs={{0,3},{1,0},{2,1},{3,2},{4,7},{5,4},{6,5},{7,6},{8,11},{9,8},{10,9... | collective-permute-start | bytes 1179656 | tf_op jit(solution)/shard_map/ppermute | solution.py:54
  67.2 0.0 collective-permute-done.refs_1_
  67.2 1.9 %collective-permute-start.4 = (bf16[2,32,3072]{2,1,0:T(8,128)(2,1)S(1)}, bf16[2,32,3072]{2,1,0:T(8,128)(2,1)S(1)}, u32[]{:S(2)}, u32[]{:S(2)}) collective-permute-start(bf16[2,32,3072]{2,1,0:T(8,128)(2,1)S(1)} %collective-permute-done.refs_1_), channel_id=1, source_target_pairs={{0,1},{1,2},{2,3},{3,0},{4,5},{5,6},{6,7},{7,4},{8,9},{9,10},{10,1... | collective-permute-start | bytes 1179656 | tf_op jit(solution)/shard_map/ppermute | solution.py:54
  69.2 0.5 collective-permute-done.1.refs_2_
  69.6 3.1 %collective-permute-done.5.refs_6_ = bf16[2,32,3072]{2,1,0:T(8,128)(2,1)S(1)} collective-permute-done((bf16[2,32,3072]{2,1,0:T(8,128)(2,1)S(1)}, bf16[2,32,3072]{2,1,0:T(8,128)(2,1)S(1)}, u32[]{:S(2)}, u32[]{:S(2)}) %collective-permute-start.5) | collective-permute-done | bytes 393248 | tf_op jit(solution)/shard_map/ppermute | solution.py:54
  72.8 4.3 %collective-permute-done.4.refs_5_ = bf16[2,32,3072]{2,1,0:T(8,128)(2,1)S(1)} collective-permute-done((bf16[2,32,3072]{2,1,0:T(8,128)(2,1)S(1)}, bf16[2,32,3072]{2,1,0:T(8,128)(2,1)S(1)}, u32[]{:S(2)}, u32[]{:S(2)}) %collective-permute-start.4) | collective-permute-done | bytes 393248 | tf_op jit(solution)/shard_map/ppermute | solution.py:54
  77.1 3.8 %shard_map.112 = (bf16[16,16,3072]{2,1,0:T(8,128)(2,1)S(1)}, bf16[256,3072]{1,0:T(8,128)(2,1)S(1)}, bf16[256,3072]{1,0:T(8,128)(2,1)S(1)}, bf16[256,128]{1,0:T(8...) custom-call(f32[8,128]{1,0:T(8,128)S(1)} %broadcast_in_dim.59.keep_row, ...), custom_call_target="tpu_custom_call" | custom-call | flops 1006632960 | bytes 8388608 | tf_op jit(solution)/shard_map/pallas_call | solution.py:137
  80.9 17.9 %all_to_all.26 = bf16[16,16,3072]{2,1,0:T(8,128)(2,1)} all-to-all(bf16[16,16,3072]{2,1,0:T(8,128)(2,1)S(1)} %get-tuple-element.28), channel_id=1, replica_groups={{0,4,8,12,1,5,9,13,2,6,10,14,3,7,11,15},{64,65,66,67,68,69,70,71,72,73,..., dimensions={0} | all-to-all | bytes 3145728 | tf_op jit(solution)/shard_map/all_to_all | solution.py:58
  98.8 1.6 %reduce_sum.44 = bf16[16,3072]{1,0:T(8,128)(2,1)S(1)} reduce(bf16[16,16,3072]{2,1,0:T(8,128)(2,1)} %all_to_all.26, bf16[]{:T(256)} %constant.21.clone.1), dimensions={0}, to_apply=%region_2.3 | reduce | flops 737280 | bytes 1671170 | tf_op jit(solution)/shard_map/reduce_sum | solution.py:187
  100.4 0.7 reshape.94
  101.1 6.4 %all-to-all-start.3 = ((bf16[4,4,3072]{2,1,0:T(4,128)(2,1)}), bf16[4,4,3072]{2,1,0:T(4,128)(2,1)S(1)}, u32[]{:S(2)}, u32[]{:S(2)}) async-start(bf16[4,4,3072]{2,1,0:T(4,128)(2,1)} %reshape.94), calls=%async_computation.3 | async-start | bytes 196608 | tf_op jit(solution)/shard_map/all_to_all | solution.py:58
  107.5 1.5 %convolution_convert_fusion.2 = bf16[3072,128]{1,0:T(8,128)(2,1)} fusion(bf16[256,3072]{1,0:T(8,128)(2,1)S(1)} %get-tuple-element.35, bf16[256,128]{1,0:T(8,128)(2,1)S(1)} %get-tuple-element.36), kind=kOutput, calls=%fused_computation.2 | convolution fusion | flops 201719808 | bytes 2424832 | tf_op jit(solution)/shard_map/dot_general | solution.py:21
  109.0 1.5 %convolution_convert_fusion.1 = bf16[3072,128]{1,0:T(8,128)(2,1)} fusion(bf16[256,3072]{1,0:T(8,128)(2,1)S(1)} %get-tuple-element.35, bf16[256,128]{1,0:T(8,128)(2,1)S(1)} %get-tuple-element.37), kind=kOutput, calls=%fused_computation.1 | convolution fusion | flops 201719808 | bytes 2424832 | tf_op jit(solution)/shard_map/dot_general | solution.py:21
  110.5 1.3 convolution_convert_fusion
  111.8 7.8 %all-to-all-done.3 = bf16[4,4,3072]{2,1,0:T(4,128)(2,1)S(1)} async-done(((bf16[4,4,3072]{2,1,0:T(4,128)(2,1)}), bf16[4,4,3072]{2,1,0:T(4,128)(2,1)S(1)}, u32[]{:S(2)}, u32[]{:S(2)}) %all-to-all-start.3) | async-done | bytes 98336 | tf_op jit(solution)/shard_map/all_to_all | solution.py:58
  119.6 0.1 reduce_sum.45
  119.7 0.1 convolution_convert_fusion.3
  119.9 20.5 %all_to_all.27 = bf16[8,2,3072]{2,1,0:T(2,128)(2,1)S(1)} all-to-all(bf16[8,2,3072]{2,1,0:T(2,128)(2,1)S(1)} %reshape.95), channel_id=1, replica_groups=mesh['z_lo'=4,'core'=2,'z_hi'=4,'x'=4,'y'=4] {'z_lo','core'}, dimensions={0} | all-to-all | bytes 196608 | tf_op jit(solution)/shard_map/all_to_all | solution.py:58
  140.4 0.6 copy.16
  (10 shorter events, 0.1 us)
Async XLA Ops:
  2.5 16.6 %all-to-all-start = ((bf16[8,2,2,3072]{3,2,1,0:T(2,128)(2,1)}), bf16[8,2,2,3072]{3,2,1,0:T(2,128)(2,1)S(1)}, u32[]{:S(2)}, u32[]{:S(2)}) async-start(bf16[8,2,2,3072]{3,2,1,0:T(2,128)(2,1)} %pad_maximum_fusion), calls=%async_computation | async-start | bytes 393216 | tf_op jit(solution)/shard_map/all_to_all | solution.py:58
  38.5 38.6 %copy-start = (bf16[1,3072,128]{2,1,0:T(8,128)(2,1)S(1)}, bf16[1,3072,128]{2,1,0:T(8,128)(2,1)}, u32[]{:S(2)}) copy-start(bf16[1,3072,128]{2,1,0:T(8,128)(2,1)} %param.11) | copy-start | bytes 2359300
  38.5 38.6 %copy-start.1 = (bf16[1,3072,128]{2,1,0:T(8,128)(2,1)S(1)}, bf16[1,3072,128]{2,1,0:T(8,128)(2,1)}, u32[]{:S(2)}) copy-start(bf16[1,3072,128]{2,1,0:T(8,128)(2,1)} %param.12) | copy-start | bytes 2359300
  38.5 38.6 %copy-start.2 = (bf16[1,128,3072]{2,1,0:T(8,128)(2,1)S(1)}, bf16[1,128,3072]{2,1,0:T(8,128)(2,1)}, u32[]{:S(2)}) copy-start(bf16[1,128,3072]{2,1,0:T(8,128)(2,1)} %param.13) | copy-start | bytes 2359300
  51.0 12.8 %collective-permute-start.3 = (bf16[2,32,3072]{2,1,0:T(8,128)(2,1)S(1)}, bf16[2,32,3072]{2,1,0:T(8,128)(2,1)S(1)}, u32[]{:S(2)}, u32[]{:S(2)}) collective-permute-start(bf16[2,32,3072]{2,1,0:T(8,128)(2,1)S(1)} %get-tuple-element.44), channel_id=1, source_target_pairs={{0,3},{1,0},{2,1},{3,2},{4,7},{5,4},{6,5},{7,6},{8,11},{9,8},{10,9... | collective-permute-start | bytes 1179656 | tf_op jit(solution)/shard_map/ppermute | solution.py:54
  55.4 11.8 %collective-permute-start = (bf16[2,32,3072]{2,1,0:T(8,128)(2,1)S(1)}, bf16[2,32,3072]{2,1,0:T(8,128)(2,1)S(1)}, u32[]{:S(2)}, u32[]{:S(2)}) collective-permute-start(bf16[2,32,3072]{2,1,0:T(8,128)(2,1)S(1)} %get-tuple-element.45), channel_id=1, source_target_pairs={{0,1},{1,2},{2,3},{3,0},{4,5},{5,6},{6,7},{7,4},{8,9},{9,10},{10,1... | collective-permute-start | bytes 1179656 | tf_op jit(solution)/shard_map/ppermute | solution.py:54
  57.3 12.3 %collective-permute-start.1 = (bf16[2,32,3072]{2,1,0:T(8,128)(2,1)S(1)}, bf16[2,32,3072]{2,1,0:T(8,128)(2,1)S(1)}, u32[]{:S(2)}, u32[]{:S(2)}) collective-permute-start(bf16[2,32,3072]{2,1,0:T(8,128)(2,1)S(1)} %get-tuple-element.44), channel_id=1, source_target_pairs={{0,1},{1,2},{2,3},{3,0},{4,5},{5,6},{6,7},{7,4},{8,9},{9,10},{10,1... | collective-permute-start | bytes 1179656 | tf_op jit(solution)/shard_map/ppermute | solution.py:54
  59.4 10.2 %collective-permute-start.2 = (bf16[2,32,3072]{2,1,0:T(8,128)(2,1)S(1)}, bf16[2,32,3072]{2,1,0:T(8,128)(2,1)S(1)}, u32[]{:S(2)}, u32[]{:S(2)}) collective-permute-start(bf16[2,32,3072]{2,1,0:T(8,128)(2,1)S(1)} %get-tuple-element.45), channel_id=1, source_target_pairs={{0,3},{1,0},{2,1},{3,2},{4,7},{5,4},{6,5},{7,6},{8,11},{9,8},{10,9... | collective-permute-start | bytes 1179656 | tf_op jit(solution)/shard_map/ppermute | solution.py:54
  63.8 8.9 %collective-permute-start.5 = (bf16[2,32,3072]{2,1,0:T(8,128)(2,1)S(1)}, bf16[2,32,3072]{2,1,0:T(8,128)(2,1)S(1)}, u32[]{:S(2)}, u32[]{:S(2)}) collective-permute-start(bf16[2,32,3072]{2,1,0:T(8,128)(2,1)S(1)} %collective-permute-done.3.refs_4_), channel_id=1, source_target_pairs={{0,3},{1,0},{2,1},{3,2},{4,7},{5,4},{6,5},{7,6},{8,11},{9,8},{10,9... | collective-permute-start | bytes 1179656 | tf_op jit(solution)/shard_map/ppermute | solution.py:54
  67.2 9.9 %collective-permute-start.4 = (bf16[2,32,3072]{2,1,0:T(8,128)(2,1)S(1)}, bf16[2,32,3072]{2,1,0:T(8,128)(2,1)S(1)}, u32[]{:S(2)}, u32[]{:S(2)}) collective-permute-start(bf16[2,32,3072]{2,1,0:T(8,128)(2,1)S(1)} %collective-permute-done.refs_1_), channel_id=1, source_target_pairs={{0,1},{1,2},{2,3},{3,0},{4,5},{5,6},{6,7},{7,4},{8,9},{9,10},{10,1... | collective-permute-start | bytes 1179656 | tf_op jit(solution)/shard_map/ppermute | solution.py:54
  101.1 18.5 %all-to-all-start.3 = ((bf16[4,4,3072]{2,1,0:T(4,128)(2,1)}), bf16[4,4,3072]{2,1,0:T(4,128)(2,1)S(1)}, u32[]{:S(2)}, u32[]{:S(2)}) async-start(bf16[4,4,3072]{2,1,0:T(4,128)(2,1)} %reshape.94), calls=%async_computation.3 | async-start | bytes 196608 | tf_op jit(solution)/shard_map/all_to_all | solution.py:58

commit v6 on v4

--- a/solution.py
+++ b/solution.py
@@ -40,8 +40,6 @@
     return first + [[16 + place for place in group] for group in second]
 
 
-NEAR = per_core(ALONG_X, ALONG_Y)
-FAR = per_core(ALONG_Y, ALONG_X)
 WHOLE = per_core([sum(ALONG_X, [])], [sum(ALONG_Y, [])])
 
 
@@ -61,14 +59,9 @@
         fan[i] = ordered
 
 
-def copy_kernel(block, fan):
-    for i in range(fan.shape[0]):
-        fan[i] = block[...]
-
-
-def fan_out(kernel, block, receivers):
+def fan_out(block, receivers):
     return pl.pallas_call(
-        kernel,
+        order_kernel,
         out_shape=jax.ShapeDtypeStruct((receivers,) + block.shape, jnp.bfloat16),
         in_specs=[pl.BlockSpec(memory_space=pltpu.VMEM)],
         out_specs=pl.BlockSpec(memory_space=pltpu.VMEM),
@@ -82,20 +75,21 @@
     blocks, pair, width = group.shape
     half = pair // 2
     size = blocks * half
+    units = w_gate.shape[1]
     sums[...] = jnp.zeros_like(sums)
 
     def forward(i, carry):
         part = pl.ds(pl.multiple_of(i * STEP, STEP), STEP)
         rows = group[:, :half, part].reshape(size, STEP)
         cots = group[:, half:, part].reshape(size, STEP)
-        sums[0] += dot(rows, w_gate[part, :])
-        sums[1] += dot(rows, w_up[part, :])
-        sums[2] += dot(cots, w_down[:, part], NT)
+        weights = jnp.concatenate((w_gate[part, :], w_up[part, :]), axis=1)
+        sums[:, : 2 * units] += dot(rows, weights)
+        sums[:, 2 * units :] += dot(cots, w_down[:, part], NT)
         return carry
 
     lax.fori_loop(0, width // STEP, forward, 0)
     keep = keep_row[0:1, :]
-    gate, up, hidden_grad = sums[0], sums[1], sums[2]
+    gate, up, hidden_grad = sums[:, :units], sums[:, units : 2 * units], sums[:, 2 * units :]
     sig = jax.nn.sigmoid(gate)
     act = gate * sig
     hidden[...] = (act * up * keep).astype(jnp.bfloat16)
@@ -132,7 +126,7 @@
         in_specs=[vmem, vmem, vmem, vmem, vmem],
         out_specs=(vmem, vmem, vmem, vmem),
         scratch_shapes=[
-            pltpu.VMEM((3, size, units), jnp.float32),
+            pltpu.VMEM((size, 3 * units), jnp.float32),
             pltpu.VMEM((size, 2 * units), jnp.bfloat16),
         ],
         compiler_params=pltpu.CompilerParams(vmem_limit_bytes=VMEM_LIMIT),
@@ -140,6 +134,28 @@
             flops=10 * size * units * width, bytes_accessed=8 * 2**20, transcendentals=size * units
         ),
     )(keep, group, w_gate, w_up, w_down)
+
+
+def sum_kernel(parts, out):
+    def step(i, carry):
+        part = pl.ds(pl.multiple_of(i * STEP, STEP), STEP)
+        total = parts[0, :, part].astype(jnp.float32)
+        for j in range(1, parts.shape[0]):
+            total += parts[j, :, part].astype(jnp.float32)
+        out[:, part] = total.astype(jnp.bfloat16)
+        return carry
+
+    lax.fori_loop(0, out.shape[1] // STEP, step, 0)
+
+
+def sum_parts(parts):
+    return pl.pallas_call(
+        sum_kernel,
+        out_shape=jax.ShapeDtypeStruct(parts.shape[1:], jnp.bfloat16),
+        in_specs=[pl.BlockSpec(memory_space=pltpu.VMEM)],
+        out_specs=pl.BlockSpec(memory_space=pltpu.VMEM),
+        compiler_params=pltpu.CompilerParams(vmem_limit_bytes=VMEM_LIMIT),
+    )(parts)
 
 
 def body(x_rows, cot_rows, counts, w_gate, w_up, w_down, kept_blocks, block_rank):
@@ -161,14 +177,12 @@
     got = got.reshape(experts * 2 * capacity, width)
     packed = dot(both, got).astype(jnp.bfloat16)
     column = lax.all_gather(packed, "z_hi", axis=0, tiled=True)
-    line = exchange(fan_out(order_kernel, column, 4), CHIP_PLANE, NEAR)
-    group = exchange(fan_out(copy_kernel, line, 4), CHIP_PLANE, FAR)
-    group = group.reshape(16, 8 * LIVE, width)
+    group = exchange(fan_out(column, 16), CHIP_PLANE, WHOLE)
     term, hidden, gate_grad, up_grad = middle(
         keep, group, w_gate[0], w_up[0], w_down[0]
     )
     parts = exchange(term, CHIP_PLANE, WHOLE)
-    plane_sum = jnp.sum(parts.astype(jnp.float32), axis=0).astype(jnp.bfloat16)
+    plane_sum = sum_parts(parts)
     plane_sum, group, hidden, gate_grad, up_grad = lax.optimization_barrier(
         (plane_sum, group, hidden, gate_grad, up_grad)
     )

time: 140 us -> 145 us (1.036)
  blocking collectives: 94.5 us -> 101 us
  other arithmetic: 4.82 us -> 3.19 us
    all_to_all x4 -> x3, blocking collectives: 75.7 us -> 82 us  [exchange(): lax.all_to_all(array, axes, split_axis=0, concat_axis=0, axis_index_group...]
    reduce_sum x1 -> x0, other arithmetic: 1.63 us -> none  [body(): plane_sum = jnp.sum(parts.astype(jnp.float32), axis=0).astype(jnp.bfloat16)]
where the time goes in v6:
time: 145 us; the launch traced here: 144 us
  blocking collectives  101 us (70%)
  starting transfers between devices  16.5 us (11%)
  waiting for transfers between devices  10.7 us (7%)
  matrix products  4.65 us (3%)
  Pallas kernels  4.25 us (3%)
  other arithmetic  3.19 us (2%)
  local copies, waits for them, and re-layouts  2.17 us (1%)
  between operations  2.03 us (1%)
    all_to_all x3, blocking collectives, exchange(): lax.all_to_all(array, axes, split_axis=0, concat_axis=0, axis_index_group...  82 us
    all_gather x1, blocking collectives, body(): column = lax.all_gather(packed, 'z_hi', axis=0, tiled=True)  18.8 us
    all_to_all x2, starting transfers between devices, exchange(): lax.all_to_all(array, axes, split_axis=0, concat_axis=0, axis_index_group...  16.5 us
    all_to_all x2, waiting for transfers between devices, exchange(): lax.all_to_all(array, axes, split_axis=0, concat_axis=0, axis_index_group...  10.7 us
    dot_general x5, matrix products, dot(): lax.dot_general(left, right, dims, preferred_element_type=jnp.float32)  4.65 us
    pallas_call x1, Pallas kernels, middle(): pl.pallas_call(middle_kernel, out_shape=(jax.ShapeDtypeStruct((blocks, pa...  3.57 us
  transfers between devices with their start and end apart: 2, of which 2 were waited for; matrix products, arithmetic and copies ran while one was open for 4% of the time, Pallas kernels for 0%

profile of v6, /device:TPU:1, one launch (start us, length us, event | category | flops | bytes accessed | tf_op | source)
XLA Modules:
  0.0 144.4 jit_solution(1291156722513218178)
XLA Ops:
  0.6 1.9 %pad_maximum_fusion = bf16[8,2,2,3072]{3,2,1,0:T(2,128)(2,1)} fusion(bf16[8,1,2,3072]{3,2,1,0:T(2,128)(2,1)} %bitcast.42, bf16[8,1,2,3072]{3,2,1,0:T(2,128)(2,1)} %bitcast.43), kind=kLoop, calls=%fused_computation.5 | loop fusion | flops 98304 | bytes 393216 | tf_op jit(solution)/shard_map/stack | solution.py:172
  2.5 10.2 %all-to-all-start = ((bf16[8,2,2,3072]{3,2,1,0:T(2,128)(2,1)}), bf16[8,2,2,3072]{3,2,1,0:T(2,128)(2,1)S(1)}, u32[]{:S(2)}, u32[]{:S(2)}) async-start(bf16[8,2,2,3072]{3,2,1,0:T(2,128)(2,1)} %pad_maximum_fusion), calls=%async_computation | async-start | bytes 393216 | tf_op jit(solution)/shard_map/all_to_all | solution.py:47
  12.7 0.8 select_reduce_fusion.1
  13.5 0.1 select_reduce_fusion
  13.6 0.1 add_select_fusion
  13.7 0.1 compare_convert_fusion
  15.1 0.1 add.28
  15.1 0.1 add.29
  15.2 0.1 lt.59
  15.3 0.1 lt.60
  15.4 0.1 lt.58
  15.5 0.1 broadcast_multiply_fusion
  15.6 0.1 mul.24
  15.7 0.1 fusion
  15.7 3.4 %all-to-all-done = bf16[8,2,2,3072]{3,2,1,0:T(2,128)(2,1)S(1)} async-done(((bf16[8,2,2,3072]{3,2,1,0:T(2,128)(2,1)}), bf16[8,2,2,3072]{3,2,1,0:T(2,128)(2,1)S(1)}, u32[]{:S(2)}, u32[]{:S(2)}) %all-to-all-start) | async-done | bytes 196640 | tf_op jit(solution)/shard_map/all_to_all | solution.py:47
  19.2 0.1 reshape.99
  19.2 0.2 convolution_convert_fusion.4
  19.4 18.8 %all_gather.3.column = bf16[32,3072]{1,0:T(8,128)(2,1)S(1)} all-gather(bf16[8,3072]{1,0:T(8,128)(2,1)S(1)} %convolution_convert_fusion.4), channel_id=1, replica_groups=mesh['z_lo'=4,'core'=2,'z_hi'=4,'x'=4,'y'=4] {'z_hi'}, dimensions={0}, use_global_device_ids=true | all-gather | bytes 245760 | tf_op jit(solution)/shard_map/all_gather | solution.py:179
  38.3 0.4 shard_map.111
  38.7 0.0 copy-start
  38.7 0.0 copy-start.1
  38.7 0.0 copy-start.2
  38.7 40.2 %all_to_all.25.group = bf16[16,32,3072]{2,1,0:T(8,128)(2,1)S(1)} all-to-all(bf16[16,32,3072]{2,1,0:T(8,128)(2,1)S(1)} %shard_map.111), channel_id=1, replica_groups={{0,4,8,12,1,5,9,13,2,6,10,14,3,7,11,15},{64,65,66,67,68,69,70,71,72,73,..., dimensions={0} | all-to-all | bytes 6291456 | tf_op jit(solution)/shard_map/all_to_all | solution.py:47
  78.9 0.0 copy-done
  78.9 0.0 copy-done.1
  78.9 0.0 copy-done.2
  78.9 3.6 %shard_map.112 = (bf16[16,16,3072]{2,1,0:T(8,128)(2,1)S(1)}, bf16[256,128]{1,0:T(8,128)(2,1)S(1)}, bf16[256,128]{1,0:T(8,128)(2,1)S(1)}, bf16[256,128]{1,0:T(8,128)(2,1)S(1)}) custom-call(f32[8,128]{1,0:T(8,128)S(1)} %broadcast_in_dim.59.keep_row, bf16[16,32,3072]{2,1,0:T(8,128)(2,1)S(1)} %all_to_all.25.group, bf16[3072,128]{1,0:T(8,128)(2,1)S(1)} %bitcast.32, ...), custom_call_target="tpu_custom_call" | custom-call | flops 1006632960 | bytes 8388608 | tf_op jit(solution)/shard_map/pallas_call | solution.py:118
  82.5 20.4 %all_to_all.26.parts = bf16[16,16,3072]{2,1,0:T(8,128)(2,1)S(1)} all-to-all(bf16[16,16,3072]{2,1,0:T(8,128)(2,1)S(1)} %get-tuple-element.25), channel_id=1, replica_groups={{0,4,8,12,1,5,9,13,2,6,10,14,3,7,11,15},{64,65,66,67,68,69,70,71,72,73,..., dimensions={0} | all-to-all | bytes 3145728 | tf_op jit(solution)/shard_map/all_to_all | solution.py:47
  102.9 0.2 shard_map.113
  103.2 0.7 reshape.100
  103.9 6.4 %all-to-all-start.3 = ((bf16[4,4,3072]{2,1,0:T(4,128)(2,1)}), bf16[4,4,3072]{2,1,0:T(4,128)(2,1)S(1)}, u32[]{:S(2)}, u32[]{:S(2)}) async-start(bf16[4,4,3072]{2,1,0:T(4,128)(2,1)} %reshape.100), calls=%async_computation.3 | async-start | bytes 196608 | tf_op jit(solution)/shard_map/all_to_all | solution.py:47
  110.2 0.2 fusion.1
  110.5 1.5 %convolution_convert_fusion.1 = bf16[3072,128]{1,0:T(8,128)(2,1)} fusion(bf16[256,3072]{1,0:T(8,128)(2,1)S(1)} %bitcast.35, bf16[256,128]{1,0:T(8,128)(2,1)S(1)} %get-tuple-element.32), kind=kOutput, calls=%fused_computation.1 | convolution fusion | flops 201719808 | bytes 2424832 | tf_op jit(solution)/shard_map/dot_general | solution.py:21
  112.0 1.5 %convolution_convert_fusion.2 = bf16[3072,128]{1,0:T(8,128)(2,1)} fusion(bf16[256,3072]{1,0:T(8,128)(2,1)S(1)} %bitcast.36, bf16[256,128]{1,0:T(8,128)(2,1)S(1)} %get-tuple-element.31), kind=kOutput, calls=%fused_computation.2 | convolution fusion | flops 201719808 | bytes 2424832 | tf_op jit(solution)/shard_map/dot_general | solution.py:21
  113.5 1.3 convolution_convert_fusion
  114.8 7.3 %all-to-all-done.3 = bf16[4,4,3072]{2,1,0:T(4,128)(2,1)S(1)} async-done(((bf16[4,4,3072]{2,1,0:T(4,128)(2,1)}), bf16[4,4,3072]{2,1,0:T(4,128)(2,1)S(1)}, u32[]{:S(2)}, u32[]{:S(2)}) %all-to-all-start.3) | async-done | bytes 98336 | tf_op jit(solution)/shard_map/all_to_all | solution.py:47
  122.1 0.1 reduce_sum.32
  122.2 0.1 convolution_convert_fusion.3
  122.4 21.4 %all_to_all.27 = bf16[8,2,3072]{2,1,0:T(2,128)(2,1)S(1)} all-to-all(bf16[8,2,3072]{2,1,0:T(2,128)(2,1)S(1)} %reshape.103), channel_id=1, replica_groups=mesh['z_lo'=4,'core'=2,'z_hi'=4,'x'=4,'y'=4] {'z_lo','core'}, dimensions={0} | all-to-all | bytes 196608 | tf_op jit(solution)/shard_map/all_to_all | solution.py:47
  143.8 0.6 copy.16
  (6 shorter events, 0.1 us)
Async XLA Ops:
  2.5 16.6 %all-to-all-start = ((bf16[8,2,2,3072]{3,2,1,0:T(2,128)(2,1)}), bf16[8,2,2,3072]{3,2,1,0:T(2,128)(2,1)S(1)}, u32[]{:S(2)}, u32[]{:S(2)}) async-start(bf16[8,2,2,3072]{3,2,1,0:T(2,128)(2,1)} %pad_maximum_fusion), calls=%async_computation | async-start | bytes 393216 | tf_op jit(solution)/shard_map/all_to_all | solution.py:47
  38.7 40.2 %copy-start = (bf16[1,3072,128]{2,1,0:T(8,128)(2,1)S(1)}, bf16[1,3072,128]{2,1,0:T(8,128)(2,1)}, u32[]{:S(2)}) copy-start(bf16[1,3072,128]{2,1,0:T(8,128)(2,1)} %param.11) | copy-start | bytes 2359300
  38.7 40.2 %copy-start.1 = (bf16[1,3072,128]{2,1,0:T(8,128)(2,1)S(1)}, bf16[1,3072,128]{2,1,0:T(8,128)(2,1)}, u32[]{:S(2)}) copy-start(bf16[1,3072,128]{2,1,0:T(8,128)(2,1)} %param.12) | copy-start | bytes 2359300
  38.7 40.2 %copy-start.2 = (bf16[1,128,3072]{2,1,0:T(8,128)(2,1)S(1)}, bf16[1,128,3072]{2,1,0:T(8,128)(2,1)}, u32[]{:S(2)}) copy-start(bf16[1,128,3072]{2,1,0:T(8,128)(2,1)} %param.13) | copy-start | bytes 2359300
  103.9 18.2 %all-to-all-start.3 = ((bf16[4,4,3072]{2,1,0:T(4,128)(2,1)}), bf16[4,4,3072]{2,1,0:T(4,128)(2,1)S(1)}, u32[]{:S(2)}, u32[]{:S(2)}) async-start(bf16[4,4,3072]{2,1,0:T(4,128)(2,1)} %reshape.100), calls=%async_computation.3 | async-start | bytes 196608 | tf_op jit(solution)/shard_map/all_to_all | solution.py:47

commit v7 on v6

--- a/solution.py
+++ b/solution.py
@@ -40,7 +40,18 @@
     return first + [[16 + place for place in group] for group in second]
 
 
+FAR = per_core(ALONG_Y, ALONG_X)
 WHOLE = per_core([sum(ALONG_X, [])], [sum(ALONG_Y, [])])
+
+
+CHIP = ("core", "z_hi", "x", "y")
+
+
+def snake(line):
+    return [z * 16 + place for z in range(4) for place in (line[::-1] if z % 2 else line)]
+
+
+NEAR = [snake(line) for line in ALONG_X] + [[64 + p for p in snake(line)] for line in ALONG_Y]
 
 
 def exchange(array, axes, groups=None):
@@ -49,24 +60,32 @@
     )
 
 
-def order_kernel(column, fan):
-    size = column.shape[0]
+def order_kernel(line, fan):
+    size, width = line.shape
     out = lax.broadcasted_iota(jnp.int32, (size, size), 0)
-    source = ((out & 15) >> 2) * 8 + (out >> 4) * 4 + (out & 3)
+    z_hi = (out >> 2) & 3
+    place = z_hi * 4 + ((out >> 5) ^ (3 * (z_hi & 1)))
+    source = place * 8 + ((out >> 4) & 1) * 4 + (out & 3)
     order = (source == lax.broadcasted_iota(jnp.int32, (size, size), 1)).astype(jnp.bfloat16)
-    ordered = dot(order, column[...]).astype(jnp.bfloat16)
-    for i in range(fan.shape[0]):
-        fan[i] = ordered
-
-
-def fan_out(block, receivers):
+
+    def step(i, carry):
+        part = pl.ds(pl.multiple_of(i * STEP, STEP), STEP)
+        ordered = dot(order, line[:, part]).astype(jnp.bfloat16).reshape(4, size // 4, STEP)
+        for j in range(fan.shape[0]):
+            fan[j, :, :, part] = ordered
+        return carry
+
+    lax.fori_loop(0, width // STEP, step, 0)
+
+
+def fan_out(line):
     return pl.pallas_call(
         order_kernel,
-        out_shape=jax.ShapeDtypeStruct((receivers,) + block.shape, jnp.bfloat16),
+        out_shape=jax.ShapeDtypeStruct((4, 4, line.shape[0] // 4, line.shape[1]), jnp.bfloat16),
         in_specs=[pl.BlockSpec(memory_space=pltpu.VMEM)],
         out_specs=pl.BlockSpec(memory_space=pltpu.VMEM),
         compiler_params=pltpu.CompilerParams(vmem_limit_bytes=VMEM_LIMIT),
-    )(block)
+    )(line)
 
 
 def middle_kernel(
@@ -176,8 +195,8 @@
     got, both, back, keep = lax.optimization_barrier((got, both, back, keep))
     got = got.reshape(experts * 2 * capacity, width)
     packed = dot(both, got).astype(jnp.bfloat16)
-    column = lax.all_gather(packed, "z_hi", axis=0, tiled=True)
-    group = exchange(fan_out(column, 16), CHIP_PLANE, WHOLE)
+    line = lax.all_gather(packed, CHIP, axis=0, tiled=True, axis_index_groups=NEAR)
+    group = exchange(fan_out(line), CHIP_PLANE, FAR).reshape(16, 8 * LIVE, width)
     term, hidden, gate_grad, up_grad = middle(
         keep, group, w_gate[0], w_up[0], w_down[0]
     )

time: 145 us -> 154 us (1.062)
  blocking collectives: 101 us -> 108 us
    all_gather x1, blocking collectives: 18.8 us -> 44.6 us  [body(): lax.all_gather(packed, CHIP, axis=0, tiled=True, axis_index_groups=NEAR)]
    all_to_all x3, blocking collectives: 82 us -> 63.6 us  [exchange(): lax.all_to_all(array, axes, split_axis=0, concat_axis=0, axis_index_group...]
where the time goes in v7:
time: 154 us
  blocking collectives  108 us (70%)
  starting transfers between devices  17.8 us (12%)
  waiting for transfers between devices  10.7 us (7%)
  Pallas kernels  4.95 us (3%)
  matrix products  4.65 us (3%)
  other arithmetic  3.19 us (2%)
  local copies, waits for them, and re-layouts  2.17 us (1%)
  between operations  2.03 us (1%)
    all_to_all x3, blocking collectives, exchange(): lax.all_to_all(array, axes, split_axis=0, concat_axis=0, axis_index_group...  63.6 us
    all_gather x1, blocking collectives, body(): lax.all_gather(packed, CHIP, axis=0, tiled=True, axis_index_groups=NEAR)  44.6 us
    all_to_all x2, starting transfers between devices, exchange(): lax.all_to_all(array, axes, split_axis=0, concat_axis=0, axis_index_group...  17.8 us
    all_to_all x2, waiting for transfers between devices, exchange(): lax.all_to_all(array, axes, split_axis=0, concat_axis=0, axis_index_group...  10.7 us
    dot_general x5, matrix products, dot(): lax.dot_general(left, right, dims, preferred_element_type=jnp.float32)  4.65 us
    pallas_call x1, Pallas kernels, middle(): pl.pallas_call(middle_kernel, out_shape=(jax.ShapeDtypeStruct((blocks, pa...  3.58 us
  transfers between devices with their start and end apart: 2, of which 2 were waited for; matrix products, arithmetic and copies ran while one was open for 4% of the time, Pallas kernels for 0%

profile of v7, /device:TPU:1, one launch (start us, length us, event | category | flops | bytes accessed | tf_op | source)
XLA Modules:
  0.0 153.8 jit_solution(10142777264801335877)
XLA Ops:
  0.6 1.9 %pad_maximum_fusion = bf16[8,2,2,3072]{3,2,1,0:T(2,128)(2,1)} fusion(bf16[8,1,2,3072]{3,2,1,0:T(2,128)(2,1)} %bitcast.45, bf16[8,1,2,3072]{3,2,1,0:T(2,128)(2,1)} %bitcast.46), kind=kLoop, calls=%fused_computation.5 | loop fusion | flops 98304 | bytes 393216 | tf_op jit(solution)/shard_map/stack | solution.py:191
  2.5 10.2 %all-to-all-start = ((bf16[8,2,2,3072]{3,2,1,0:T(2,128)(2,1)}), bf16[8,2,2,3072]{3,2,1,0:T(2,128)(2,1)S(1)}, u32[]{:S(2)}, u32[]{:S(2)}) async-start(bf16[8,2,2,3072]{3,2,1,0:T(2,128)(2,1)} %pad_maximum_fusion), calls=%async_computation | async-start | bytes 393216 | tf_op jit(solution)/shard_map/all_to_all | solution.py:58
  12.7 0.8 select_reduce_fusion.1
  13.5 0.1 select_reduce_fusion
  13.6 0.1 add_select_fusion
  13.7 0.1 compare_convert_fusion
  15.1 0.1 add.28
  15.1 0.1 add.29
  15.2 0.1 lt.59
  15.3 0.1 lt.60
  15.4 0.1 lt.58
  15.5 0.1 broadcast_multiply_fusion
  15.6 0.1 mul.24
  15.7 0.1 fusion
  15.7 3.4 %all-to-all-done = bf16[8,2,2,3072]{3,2,1,0:T(2,128)(2,1)S(1)} async-done(((bf16[8,2,2,3072]{3,2,1,0:T(2,128)(2,1)}), bf16[8,2,2,3072]{3,2,1,0:T(2,128)(2,1)S(1)}, u32[]{:S(2)}, u32[]{:S(2)}) %all-to-all-start) | async-done | bytes 196640 | tf_op jit(solution)/shard_map/all_to_all | solution.py:58
  19.2 0.1 reshape.102
  19.2 0.2 convolution_convert_fusion.4
  19.4 44.6 %all_gather.3.line = bf16[128,3072]{1,0:T(8,128)(2,1)S(1)} all-gather(bf16[8,3072]{1,0:T(8,128)(2,1)S(1)} %convolution_convert_fusion.4), channel_id=1, replica_groups={{0,4,8,12,28,24,20,16,32,36,40,44,60,56,52,48},{1,5,9,13,29,25,21,17,33..., dimensions={0}, use_global_device_ids=true | all-gather | bytes 835584 | tf_op jit(solution)/shard_map/all_gather | solution.py:198
  64.0 1.1 shard_map.111
  65.2 0.0 copy-start
  65.2 0.0 copy-start.1
  65.2 0.0 copy-start.2
  65.2 23.7 %all_to_all.25 = bf16[4,4,32,3072]{3,2,1,0:T(8,128)(2,1)S(1)} all-to-all(bf16[4,4,32,3072]{3,2,1,0:T(8,128)(2,1)S(1)} %shard_map.111), channel_id=1, replica_groups={{0,1,2,3},{4,5,6,7},{8,9,10,11},{12,13,14,15},{64,68,72,76},{65,69,73,7..., dimensions={0} | all-to-all | bytes 6291456 | tf_op jit(solution)/shard_map/all_to_all | solution.py:58
  88.9 0.0 copy-done
  88.9 0.0 copy-done.1
  88.9 0.0 copy-done.2
  88.9 3.6 %shard_map.112 = (bf16[16,16,3072]{2,1,0:T(8,128)(2,1)S(1)}, bf16[256,128]{1,0:T(8,128)(2,1)S(1)}, bf16[256,128]{1,0:T(8,128)(2,1)S(1)}, bf16[256,128]{1,0:T(8,128)(2,1)S(1)}) custom-call(f32[8,128]{1,0:T(8,128)S(1)} %broadcast_in_dim.59.keep_row, bf16[16,32,3072]{2,1,0:T(8,128)(2,1)S(1)} %bitcast.33, bf16[3072,128]{1,0:T(8,128)(2,1)S(1)} %bitcast.35, ...), custom_call_target="tpu_custom_call" | custom-call | flops 1006632960 | bytes 8388608 | tf_op jit(solution)/shard_map/pallas_call | solution.py:137
  92.5 17.3 %all_to_all.26.parts = bf16[16,16,3072]{2,1,0:T(8,128)(2,1)S(1)} all-to-all(bf16[16,16,3072]{2,1,0:T(8,128)(2,1)S(1)} %get-tuple-element.25), channel_id=1, replica_groups={{0,4,8,12,1,5,9,13,2,6,10,14,3,7,11,15},{64,65,66,67,68,69,70,71,72,73,..., dimensions={0} | all-to-all | bytes 3145728 | tf_op jit(solution)/shard_map/all_to_all | solution.py:58
  109.8 0.2 shard_map.113
  110.0 0.7 reshape.104
  110.7 7.7 %all-to-all-start.3 = ((bf16[4,4,3072]{2,1,0:T(4,128)(2,1)}), bf16[4,4,3072]{2,1,0:T(4,128)(2,1)S(1)}, u32[]{:S(2)}, u32[]{:S(2)}) async-start(bf16[4,4,3072]{2,1,0:T(4,128)(2,1)} %reshape.104), calls=%async_computation.3 | async-start | bytes 196608 | tf_op jit(solution)/shard_map/all_to_all | solution.py:58
  118.4 0.2 fusion.1
  118.6 1.5 convolution_convert_fusion.1
  120.1 1.5 convolution_convert_fusion.2
  121.6 1.3 convolution_convert_fusion
  122.9 7.3 %all-to-all-done.3 = bf16[4,4,3072]{2,1,0:T(4,128)(2,1)S(1)} async-done(((bf16[4,4,3072]{2,1,0:T(4,128)(2,1)}), bf16[4,4,3072]{2,1,0:T(4,128)(2,1)S(1)}, u32[]{:S(2)}, u32[]{:S(2)}) %all-to-all-start.3) | async-done | bytes 98336 | tf_op jit(solution)/shard_map/all_to_all | solution.py:58
  130.3 0.1 reduce_sum.32
  130.3 0.1 convolution_convert_fusion.3
  130.5 22.6 %all_to_all.27 = bf16[8,2,3072]{2,1,0:T(2,128)(2,1)S(1)} all-to-all(bf16[8,2,3072]{2,1,0:T(2,128)(2,1)S(1)} %reshape.107), channel_id=1, replica_groups=mesh['z_lo'=4,'core'=2,'z_hi'=4,'x'=4,'y'=4] {'z_lo','core'}, dimensions={0} | all-to-all | bytes 196608 | tf_op jit(solution)/shard_map/all_to_all | solution.py:58
  153.1 0.6 copy.16
  (6 shorter events, 0.1 us)
Async XLA Ops:
  2.5 16.6 %all-to-all-start = ((bf16[8,2,2,3072]{3,2,1,0:T(2,128)(2,1)}), bf16[8,2,2,3072]{3,2,1,0:T(2,128)(2,1)S(1)}, u32[]{:S(2)}, u32[]{:S(2)}) async-start(bf16[8,2,2,3072]{3,2,1,0:T(2,128)(2,1)} %pad_maximum_fusion), calls=%async_computation | async-start | bytes 393216 | tf_op jit(solution)/shard_map/all_to_all | solution.py:58
  65.2 23.7 %copy-start = (bf16[1,3072,128]{2,1,0:T(8,128)(2,1)S(1)}, bf16[1,3072,128]{2,1,0:T(8,128)(2,1)}, u32[]{:S(2)}) copy-start(bf16[1,3072,128]{2,1,0:T(8,128)(2,1)} %param.11) | copy-start | bytes 2359300
  65.2 23.7 %copy-start.1 = (bf16[1,3072,128]{2,1,0:T(8,128)(2,1)S(1)}, bf16[1,3072,128]{2,1,0:T(8,128)(2,1)}, u32[]{:S(2)}) copy-start(bf16[1,3072,128]{2,1,0:T(8,128)(2,1)} %param.12) | copy-start | bytes 2359300
  65.2 23.7 %copy-start.2 = (bf16[1,128,3072]{2,1,0:T(8,128)(2,1)S(1)}, bf16[1,128,3072]{2,1,0:T(8,128)(2,1)}, u32[]{:S(2)}) copy-start(bf16[1,128,3072]{2,1,0:T(8,128)(2,1)} %param.13) | copy-start | bytes 2359300
  110.7 19.5 %all-to-all-start.3 = ((bf16[4,4,3072]{2,1,0:T(4,128)(2,1)}), bf16[4,4,3072]{2,1,0:T(4,128)(2,1)S(1)}, u32[]{:S(2)}, u32[]{:S(2)}) async-start(bf16[4,4,3072]{2,1,0:T(4,128)(2,1)} %reshape.104), calls=%async_computation.3 | async-start | bytes 196608 | tf_op jit(solution)/shard_map/all_to_all | solution.py:58

commit v8 on v6

--- a/solution.py
+++ b/solution.py
@@ -40,6 +40,8 @@
     return first + [[16 + place for place in group] for group in second]
 
 
+NEAR = per_core(ALONG_X, ALONG_Y)
+FAR = per_core(ALONG_Y, ALONG_X)
 WHOLE = per_core([sum(ALONG_X, [])], [sum(ALONG_Y, [])])
 
 
@@ -59,9 +61,14 @@
         fan[i] = ordered
 
 
-def fan_out(block, receivers):
+def copy_kernel(block, fan):
+    for i in range(fan.shape[0]):
+        fan[i] = block[...]
+
+
+def fan_out(kernel, block, receivers):
     return pl.pallas_call(
-        order_kernel,
+        kernel,
         out_shape=jax.ShapeDtypeStruct((receivers,) + block.shape, jnp.bfloat16),
         in_specs=[pl.BlockSpec(memory_space=pltpu.VMEM)],
         out_specs=pl.BlockSpec(memory_space=pltpu.VMEM),
@@ -177,7 +184,10 @@
     got = got.reshape(experts * 2 * capacity, width)
     packed = dot(both, got).astype(jnp.bfloat16)
     column = lax.all_gather(packed, "z_hi", axis=0, tiled=True)
-    group = exchange(fan_out(column, 16), CHIP_PLANE, WHOLE)
+    column = fan_out(order_kernel, column, 1)[0]
+    line = lax.all_gather(column, CHIP_PLANE, axis=0, axis_index_groups=NEAR)
+    group = exchange(fan_out(copy_kernel, line, 4), CHIP_PLANE, FAR)
+    group = group.reshape(16, 8 * LIVE, width)
     term, hidden, gate_grad, up_grad = middle(
         keep, group, w_gate[0], w_up[0], w_down[0]
     )

time: 145 us -> 141 us (0.972)
  blocking collectives: 101 us -> 96.6 us
    all_to_all x3, blocking collectives: 82 us -> 66.6 us  [exchange(): lax.all_to_all(array, axes, split_axis=0, concat_axis=0, axis_index_group...]
    all_gather x0 -> x1, blocking collectives: none -> 11.2 us  [body(): line = lax.all_gather(column, CHIP_PLANE, axis=0, axis_index_groups=NEAR)]
where the time goes in v8:
time: 141 us; the launch traced here: 140 us
  blocking collectives  96.6 us (69%)
  starting transfers between devices  16.5 us (12%)
  waiting for transfers between devices  10.7 us (8%)
  matrix products  4.65 us (3%)
  Pallas kernels  4.24 us (3%)
  other arithmetic  3.19 us (2%)
  local copies, waits for them, and re-layouts  2.17 us (2%)
  between operations  2.03 us (1%)
    all_to_all x3, blocking collectives, exchange(): lax.all_to_all(array, axes, split_axis=0, concat_axis=0, axis_index_group...  66.6 us
    all_gather x1, blocking collectives, body(): column = lax.all_gather(packed, 'z_hi', axis=0, tiled=True)  18.8 us
    all_to_all x2, starting transfers between devices, exchange(): lax.all_to_all(array, axes, split_axis=0, concat_axis=0, axis_index_group...  16.5 us
    all_gather x1, blocking collectives, body(): line = lax.all_gather(column, CHIP_PLANE, axis=0, axis_index_groups=NEAR)  11.2 us
    all_to_all x2, waiting for transfers between devices, exchange(): lax.all_to_all(array, axes, split_axis=0, concat_axis=0, axis_index_group...  10.7 us
    dot_general x5, matrix products, dot(): lax.dot_general(left, right, dims, preferred_element_type=jnp.float32)  4.65 us
    pallas_call x1, Pallas kernels, middle(): pl.pallas_call(middle_kernel, out_shape=(jax.ShapeDtypeStruct((blocks, pa...  3.61 us
  transfers between devices with their start and end apart: 2, of which 2 were waited for; matrix products, arithmetic and copies ran while one was open for 4% of the time, Pallas kernels for 0%

profile of v8, /device:TPU:1, one launch (start us, length us, event | category | flops | bytes accessed | tf_op | source)
XLA Modules:
  0.0 140.2 jit_solution(14105314970856905185)
XLA Ops:
  0.6 1.9 %pad_maximum_fusion = bf16[8,2,2,3072]{3,2,1,0:T(2,128)(2,1)} fusion(bf16[8,1,2,3072]{3,2,1,0:T(2,128)(2,1)} %bitcast.45, bf16[8,1,2,3072]{3,2,1,0:T(2,128)(2,1)} %bitcast.46), kind=kLoop, calls=%fused_computation.5 | loop fusion | flops 98304 | bytes 393216 | tf_op jit(solution)/shard_map/stack | solution.py:179
  2.5 10.2 %all-to-all-start = ((bf16[8,2,2,3072]{3,2,1,0:T(2,128)(2,1)}), bf16[8,2,2,3072]{3,2,1,0:T(2,128)(2,1)S(1)}, u32[]{:S(2)}, u32[]{:S(2)}) async-start(bf16[8,2,2,3072]{3,2,1,0:T(2,128)(2,1)} %pad_maximum_fusion), calls=%async_computation | async-start | bytes 393216 | tf_op jit(solution)/shard_map/all_to_all | solution.py:49
  12.7 0.8 select_reduce_fusion.1
  13.5 0.1 select_reduce_fusion
  13.6 0.1 add_select_fusion
  13.7 0.1 compare_convert_fusion
  15.1 0.1 add.28
  15.1 0.1 add.29
  15.2 0.1 lt.59
  15.3 0.1 lt.60
  15.4 0.1 lt.58
  15.5 0.1 broadcast_multiply_fusion
  15.6 0.1 mul.24
  15.7 0.1 fusion
  15.7 3.4 %all-to-all-done = bf16[8,2,2,3072]{3,2,1,0:T(2,128)(2,1)S(1)} async-done(((bf16[8,2,2,3072]{3,2,1,0:T(2,128)(2,1)}), bf16[8,2,2,3072]{3,2,1,0:T(2,128)(2,1)S(1)}, u32[]{:S(2)}, u32[]{:S(2)}) %all-to-all-start) | async-done | bytes 196640 | tf_op jit(solution)/shard_map/all_to_all | solution.py:49
  19.2 0.1 reshape.102
  19.2 0.2 convolution_convert_fusion.4
  19.4 18.8 %all_gather.6.column = bf16[32,3072]{1,0:T(8,128)(2,1)S(1)} all-gather(bf16[8,3072]{1,0:T(8,128)(2,1)S(1)} %convolution_convert_fusion.4), channel_id=1, replica_groups=mesh['z_lo'=4,'core'=2,'z_hi'=4,'x'=4,'y'=4] {'z_hi'}, dimensions={0}, use_global_device_ids=true | all-gather | bytes 245760 | tf_op jit(solution)/shard_map/all_gather | solution.py:186
  38.3 0.2 shard_map.111
  38.4 11.2 %all_gather.7.block = bf16[4,32,3072]{2,1,0:T(8,128)(2,1)S(1)} all-gather(bf16[1,32,3072]{2,1,0:T(8,128)(2,1)S(1)} %shard_map.111), channel_id=1, replica_groups={{0,4,8,12},{1,5,9,13},{2,6,10,14},{3,7,11,15},{64,65,66,67},{68,69,70,7..., dimensions={0}, use_global_device_ids=true | all-gather | bytes 983040 | tf_op jit(solution)/shard_map/all_gather | solution.py:188
  49.7 0.2 shard_map.112
  49.9 0.0 copy-start
  49.9 0.0 copy-start.1
  49.9 0.0 copy-start.2
  49.9 24.8 %all_to_all.25 = bf16[4,4,32,3072]{3,2,1,0:T(8,128)(2,1)S(1)} all-to-all(bf16[4,4,32,3072]{3,2,1,0:T(8,128)(2,1)S(1)} %shard_map.112), channel_id=1, replica_groups={{0,1,2,3},{4,5,6,7},{8,9,10,11},{12,13,14,15},{64,68,72,76},{65,69,73,7..., dimensions={0} | all-to-all | bytes 6291456 | tf_op jit(solution)/shard_map/all_to_all | solution.py:49
  74.7 0.0 copy-done
  74.8 0.0 copy-done.1
  74.8 0.0 copy-done.2
  74.8 3.6 %shard_map.113 = (bf16[16,16,3072]{2,1,0:T(8,128)(2,1)S(1)}, bf16[256,128]{1,0:T(8,128)(2,1)S(1)}, bf16[256,128]{1,0:T(8,128)(2,1)S(1)}, bf16[256,128]{1,0:T(8,128)(2,1)S(1)}) custom-call(f32[8,128]{1,0:T(8,128)S(1)} %broadcast_in_dim.59.keep_row, bf16[16,32,3072]{2,1,0:T(8,128)(2,1)S(1)} %bitcast.33, bf16[3072,128]{1,0:T(8,128)(2,1)S(1)} %bitcast.35, ...), custom_call_target="tpu_custom_call" | custom-call | flops 1006632960 | bytes 8388608 | tf_op jit(solution)/shard_map/pallas_call | solution.py:125
  78.4 18.9 %all_to_all.26.parts = bf16[16,16,3072]{2,1,0:T(8,128)(2,1)S(1)} all-to-all(bf16[16,16,3072]{2,1,0:T(8,128)(2,1)S(1)} %get-tuple-element.25), channel_id=1, replica_groups={{0,4,8,12,1,5,9,13,2,6,10,14,3,7,11,15},{64,65,66,67,68,69,70,71,72,73,..., dimensions={0} | all-to-all | bytes 3145728 | tf_op jit(solution)/shard_map/all_to_all | solution.py:49
  97.3 0.2 shard_map.114
  97.6 0.7 reshape.104
  98.2 6.4 %all-to-all-start.3 = ((bf16[4,4,3072]{2,1,0:T(4,128)(2,1)}), bf16[4,4,3072]{2,1,0:T(4,128)(2,1)S(1)}, u32[]{:S(2)}, u32[]{:S(2)}) async-start(bf16[4,4,3072]{2,1,0:T(4,128)(2,1)} %reshape.104), calls=%async_computation.3 | async-start | bytes 196608 | tf_op jit(solution)/shard_map/all_to_all | solution.py:49
  104.6 0.2 fusion.1
  104.9 1.5 %convolution_convert_fusion.1 = bf16[3072,128]{1,0:T(8,128)(2,1)} fusion(bf16[256,3072]{1,0:T(8,128)(2,1)S(1)} %bitcast.38, bf16[256,128]{1,0:T(8,128)(2,1)S(1)} %get-tuple-element.32), kind=kOutput, calls=%fused_computation.1 | convolution fusion | flops 201719808 | bytes 2424832 | tf_op jit(solution)/shard_map/dot_general | solution.py:21
  106.4 1.5 %convolution_convert_fusion.2 = bf16[3072,128]{1,0:T(8,128)(2,1)} fusion(bf16[256,3072]{1,0:T(8,128)(2,1)S(1)} %bitcast.39, bf16[256,128]{1,0:T(8,128)(2,1)S(1)} %get-tuple-element.31), kind=kOutput, calls=%fused_computation.2 | convolution fusion | flops 201719808 | bytes 2424832 | tf_op jit(solution)/shard_map/dot_general | solution.py:21
  107.9 1.3 convolution_convert_fusion
  109.2 7.3 %all-to-all-done.3 = bf16[4,4,3072]{2,1,0:T(4,128)(2,1)S(1)} async-done(((bf16[4,4,3072]{2,1,0:T(4,128)(2,1)}), bf16[4,4,3072]{2,1,0:T(4,128)(2,1)S(1)}, u32[]{:S(2)}, u32[]{:S(2)}) %all-to-all-start.3) | async-done | bytes 98336 | tf_op jit(solution)/shard_map/all_to_all | solution.py:49
  116.5 0.1 reduce_sum.32
  116.5 0.1 convolution_convert_fusion.3
  116.7 22.8 %all_to_all.27 = bf16[8,2,3072]{2,1,0:T(2,128)(2,1)S(1)} all-to-all(bf16[8,2,3072]{2,1,0:T(2,128)(2,1)S(1)} %reshape.107), channel_id=1, replica_groups=mesh['z_lo'=4,'core'=2,'z_hi'=4,'x'=4,'y'=4] {'z_lo','core'}, dimensions={0} | all-to-all | bytes 196608 | tf_op jit(solution)/shard_map/all_to_all | solution.py:49
  139.5 0.6 copy.16
  (6 shorter events, 0.1 us)
Async XLA Ops:
  2.5 16.6 %all-to-all-start = ((bf16[8,2,2,3072]{3,2,1,0:T(2,128)(2,1)}), bf16[8,2,2,3072]{3,2,1,0:T(2,128)(2,1)S(1)}, u32[]{:S(2)}, u32[]{:S(2)}) async-start(bf16[8,2,2,3072]{3,2,1,0:T(2,128)(2,1)} %pad_maximum_fusion), calls=%async_computation | async-start | bytes 393216 | tf_op jit(solution)/shard_map/all_to_all | solution.py:49
  49.9 24.9 %copy-start = (bf16[1,3072,128]{2,1,0:T(8,128)(2,1)S(1)}, bf16[1,3072,128]{2,1,0:T(8,128)(2,1)}, u32[]{:S(2)}) copy-start(bf16[1,3072,128]{2,1,0:T(8,128)(2,1)} %param.11) | copy-start | bytes 2359300
  49.9 24.8 %copy-start.1 = (bf16[1,3072,128]{2,1,0:T(8,128)(2,1)S(1)}, bf16[1,3072,128]{2,1,0:T(8,128)(2,1)}, u32[]{:S(2)}) copy-start(bf16[1,3072,128]{2,1,0:T(8,128)(2,1)} %param.12) | copy-start | bytes 2359300
  49.9 24.8 %copy-start.2 = (bf16[1,128,3072]{2,1,0:T(8,128)(2,1)S(1)}, bf16[1,128,3072]{2,1,0:T(8,128)(2,1)}, u32[]{:S(2)}) copy-start(bf16[1,128,3072]{2,1,0:T(8,128)(2,1)} %param.13) | copy-start | bytes 2359300
  98.2 18.2 %all-to-all-start.3 = ((bf16[4,4,3072]{2,1,0:T(4,128)(2,1)}), bf16[4,4,3072]{2,1,0:T(4,128)(2,1)S(1)}, u32[]{:S(2)}, u32[]{:S(2)}) async-start(bf16[4,4,3072]{2,1,0:T(4,128)(2,1)} %reshape.104), calls=%async_computation.3 | async-start | bytes 196608 | tf_op jit(solution)/shard_map/all_to_all | solution.py:49

commit v9 on v8

--- a/solution.py
+++ b/solution.py
@@ -49,6 +49,28 @@
     return lax.all_to_all(
         array, axes, split_axis=0, concat_axis=0, axis_index_groups=groups, tiled=True
     )
+
+
+def pair_kernel(rows, cots, pairs, sems):
+    copies = [
+        pltpu.make_async_copy(source, pairs.at[:, i], sems.at[i])
+        for i, source in enumerate((rows, cots))
+    ]
+    for copy in copies:
+        copy.start()
+    for copy in copies:
+        copy.wait()
+
+
+def pair_up(rows, cots):
+    anywhere = pl.BlockSpec(memory_space=pl.ANY)
+    return pl.pallas_call(
+        pair_kernel,
+        out_shape=jax.ShapeDtypeStruct((rows.shape[0], 2) + rows.shape[1:], jnp.bfloat16),
+        in_specs=[anywhere, anywhere],
+        out_specs=anywhere,
+        scratch_shapes=[pltpu.SemaphoreType.DMA((2,))],
+    )(rows, cots)
 
 
 def order_kernel(column, fan):
@@ -176,7 +198,7 @@
     both = kind[:, None, None, :, None] * chooser[None, :, :, None, :]
     both = both.reshape(2 * LIVE, experts * 2 * capacity)
 
-    slots = jnp.stack((x_rows[0, 0], cot_rows[0, 0]), axis=1)
+    slots = pair_up(x_rows[0, 0], cot_rows[0, 0])
     keep = (block_rank.reshape(()) < kept_blocks.reshape(())).astype(jnp.float32)
     keep = jnp.broadcast_to(keep, (8, w_gate.shape[2]))
     got = exchange(slots, EXPERT)
@@ -184,8 +206,7 @@
     got = got.reshape(experts * 2 * capacity, width)
     packed = dot(both, got).astype(jnp.bfloat16)
     column = lax.all_gather(packed, "z_hi", axis=0, tiled=True)
-    column = fan_out(order_kernel, column, 1)[0]
-    line = lax.all_gather(column, CHIP_PLANE, axis=0, axis_index_groups=NEAR)
+    line = exchange(fan_out(order_kernel, column, 4), CHIP_PLANE, NEAR)
     group = exchange(fan_out(copy_kernel, line, 4), CHIP_PLANE, FAR)
     group = group.reshape(16, 8 * LIVE, width)
     term, hidden, gate_grad, up_grad = middle(

time: 141 us -> 143 us (1.014)
  Pallas kernels: 4.24 us -> 11.3 us
  blocking collectives: 96.6 us -> 94 us
  other arithmetic: 3.19 us -> 1.31 us
    all_gather x1 -> x0, blocking collectives: 11.2 us -> none  [body(): line = lax.all_gather(column, CHIP_PLANE, axis=0, axis_index_groups=NEAR)]
    all_to_all x3 -> x4, blocking collectives: 66.6 us -> 75.2 us  [exchange(): lax.all_to_all(array, axes, split_axis=0, concat_axis=0, axis_index_group...]
    pallas_call x0 -> x1, Pallas kernels: none -> 7.08 us  [pair_up(): pl.pallas_call(pair_kernel, out_shape=jax.ShapeDtypeStruct((rows.shape[0]...]
    another operation x1 -> x0, other arithmetic: 1.88 us -> none  [body(): slots = jnp.stack((x_rows[0, 0], cot_rows[0, 0]), axis=1)]
where the time goes in v9:
time: 143 us
  blocking collectives  94 us (66%)
  starting transfers between devices  16.6 us (12%)
  Pallas kernels  11.3 us (8%)
  waiting for transfers between devices  10.7 us (7%)
  matrix products  4.65 us (3%)
  local copies, waits for them, and re-layouts  2.17 us (2%)
  between operations  2.04 us (1%)
    all_to_all x4, blocking collectives, exchange(): lax.all_to_all(array, axes, split_axis=0, concat_axis=0, axis_index_group...  75.2 us
    all_gather x1, blocking collectives, body(): column = lax.all_gather(packed, 'z_hi', axis=0, tiled=True)  18.8 us
    all_to_all x2, starting transfers between devices, exchange(): lax.all_to_all(array, axes, split_axis=0, concat_axis=0, axis_index_group...  16.6 us
    all_to_all x2, waiting for transfers between devices, exchange(): lax.all_to_all(array, axes, split_axis=0, concat_axis=0, axis_index_group...  10.7 us
    pallas_call x1, Pallas kernels, pair_up(): pl.pallas_call(pair_kernel, out_shape=jax.ShapeDtypeStruct((rows.shape[0]...  7.08 us
    dot_general x5, matrix products, dot(): lax.dot_general(left, right, dims, preferred_element_type=jnp.float32)  4.65 us
    pallas_call x1, Pallas kernels, middle(): pl.pallas_call(middle_kernel, out_shape=(jax.ShapeDtypeStruct((blocks, pa...  3.54 us
  transfers between devices with their start and end apart: 2, of which 2 were waited for; matrix products, arithmetic and copies ran while one was open for 4% of the time, Pallas kernels for 0%

profile of v9, /device:TPU:1, one launch (start us, length us, event | category | flops | bytes accessed | tf_op | source)
XLA Modules:
  0.0 142.7 jit_solution(3273008153020279477)
XLA Ops:
  0.6 7.1 %shard_map.111 = bf16[8,2,2,3072]{3,2,1,0:T(2,128)(2,1)} custom-call(bf16[8,2,3072]{2,1,0:T(2,128)(2,1)} %bitcast.45, bf16[8,2,3072]{2,1,0:T(2,128)(2,1)} %bitcast.46), custom_call_target="tpu_custom_call" | custom-call | tf_op jit(solution)/shard_map/pallas_call | solution.py:67
  7.7 10.2 %all-to-all-start = ((bf16[8,2,2,3072]{3,2,1,0:T(2,128)(2,1)}), bf16[8,2,2,3072]{3,2,1,0:T(2,128)(2,1)S(1)}, u32[]{:S(2)}, u32[]{:S(2)}) async-start(bf16[8,2,2,3072]{3,2,1,0:T(2,128)(2,1)} %shard_map.111), calls=%async_computation | async-start | bytes 393216 | tf_op jit(solution)/shard_map/all_to_all | solution.py:49
  17.9 0.8 select_reduce_fusion.1
  18.7 0.1 select_reduce_fusion
  18.8 0.1 add_select_fusion
  18.9 0.1 compare_convert_fusion
  20.3 0.1 add.28
  20.4 0.1 add.29
  20.4 0.1 lt.59
  20.5 0.1 lt.60
  20.6 0.1 lt.58
  20.7 0.1 broadcast_multiply_fusion
  20.8 0.1 mul.24
  20.9 0.1 fusion
  20.9 3.4 %all-to-all-done = bf16[8,2,2,3072]{3,2,1,0:T(2,128)(2,1)S(1)} async-done(((bf16[8,2,2,3072]{3,2,1,0:T(2,128)(2,1)}), bf16[8,2,2,3072]{3,2,1,0:T(2,128)(2,1)S(1)}, u32[]{:S(2)}, u32[]{:S(2)}) %all-to-all-start) | async-done | bytes 196640 | tf_op jit(solution)/shard_map/all_to_all | solution.py:49
  24.4 0.1 reshape.102
  24.4 0.2 convolution_convert_fusion.4
  24.7 18.8 %all_gather.3.column = bf16[32,3072]{1,0:T(8,128)(2,1)S(1)} all-gather(bf16[8,3072]{1,0:T(8,128)(2,1)S(1)} %convolution_convert_fusion.4), channel_id=1, replica_groups=mesh['z_lo'=4,'core'=2,'z_hi'=4,'x'=4,'y'=4] {'z_hi'}, dimensions={0}, use_global_device_ids=true | all-gather | bytes 245760 | tf_op jit(solution)/shard_map/all_gather | solution.py:208
  43.5 0.2 shard_map.112
  43.7 12.3 %all_to_all.30.block = bf16[4,32,3072]{2,1,0:T(8,128)(2,1)S(1)} all-to-all(bf16[4,32,3072]{2,1,0:T(8,128)(2,1)S(1)} %shard_map.112), channel_id=1, replica_groups={{0,4,8,12},{1,5,9,13},{2,6,10,14},{3,7,11,15},{64,65,66,67},{68,69,70,7..., dimensions={0} | all-to-all | bytes 1572864 | tf_op jit(solution)/shard_map/all_to_all | solution.py:49
  56.0 0.2 shard_map.113
  56.2 0.0 copy-start
  56.2 0.0 copy-start.1
  56.2 0.0 copy-start.2
  56.2 25.2 %all_to_all.31 = bf16[4,4,32,3072]{3,2,1,0:T(8,128)(2,1)S(1)} all-to-all(bf16[4,4,32,3072]{3,2,1,0:T(8,128)(2,1)S(1)} %shard_map.113), channel_id=1, replica_groups={{0,1,2,3},{4,5,6,7},{8,9,10,11},{12,13,14,15},{64,68,72,76},{65,69,73,7..., dimensions={0} | all-to-all | bytes 6291456 | tf_op jit(solution)/shard_map/all_to_all | solution.py:49
  81.5 0.0 copy-done
  81.5 0.0 copy-done.1
  81.5 0.0 copy-done.2
  81.5 3.5 %shard_map.114 = (bf16[16,16,3072]{2,1,0:T(8,128)(2,1)S(1)}, bf16[256,128]{1,0:T(8,128)(2,1)S(1)}, bf16[256,128]{1,0:T(8,128)(2,1)S(1)}, bf16[256,128]{1,0:T(8,128)(2,1)S(1)}) custom-call(f32[8,128]{1,0:T(8,128)S(1)} %broadcast_in_dim.59.keep_row, bf16[16,32,3072]{2,1,0:T(8,128)(2,1)S(1)} %bitcast.33, bf16[3072,128]{1,0:T(8,128)(2,1)S(1)} %bitcast.35, ...), custom_call_target="tpu_custom_call" | custom-call | flops 1006632960 | bytes 8388608 | tf_op jit(solution)/shard_map/pallas_call | solution.py:147
  85.0 17.4 %all_to_all.32.parts = bf16[16,16,3072]{2,1,0:T(8,128)(2,1)S(1)} all-to-all(bf16[16,16,3072]{2,1,0:T(8,128)(2,1)S(1)} %get-tuple-element.25), channel_id=1, replica_groups={{0,4,8,12,1,5,9,13,2,6,10,14,3,7,11,15},{64,65,66,67,68,69,70,71,72,73,..., dimensions={0} | all-to-all | bytes 3145728 | tf_op jit(solution)/shard_map/all_to_all | solution.py:49
  102.5 0.2 shard_map.115
  102.7 0.7 reshape.104
  103.4 6.4 %all-to-all-start.4 = ((bf16[4,4,3072]{2,1,0:T(4,128)(2,1)}), bf16[4,4,3072]{2,1,0:T(4,128)(2,1)S(1)}, u32[]{:S(2)}, u32[]{:S(2)}) async-start(bf16[4,4,3072]{2,1,0:T(4,128)(2,1)} %reshape.104), calls=%async_computation.4 | async-start | bytes 196608 | tf_op jit(solution)/shard_map/all_to_all | solution.py:49
  109.8 0.2 fusion.1
  110.0 1.5 %convolution_convert_fusion.1 = bf16[3072,128]{1,0:T(8,128)(2,1)} fusion(bf16[256,3072]{1,0:T(8,128)(2,1)S(1)} %bitcast.38, bf16[256,128]{1,0:T(8,128)(2,1)S(1)} %get-tuple-element.32), kind=kOutput, calls=%fused_computation.1 | convolution fusion | flops 201719808 | bytes 2424832 | tf_op jit(solution)/shard_map/dot_general | solution.py:21
  111.5 1.5 %convolution_convert_fusion.2 = bf16[3072,128]{1,0:T(8,128)(2,1)} fusion(bf16[256,3072]{1,0:T(8,128)(2,1)S(1)} %bitcast.39, bf16[256,128]{1,0:T(8,128)(2,1)S(1)} %get-tuple-element.31), kind=kOutput, calls=%fused_computation.2 | convolution fusion | flops 201719808 | bytes 2424832 | tf_op jit(solution)/shard_map/dot_general | solution.py:21
  113.0 1.3 convolution_convert_fusion
  114.3 7.3 %all-to-all-done.4 = bf16[4,4,3072]{2,1,0:T(4,128)(2,1)S(1)} async-done(((bf16[4,4,3072]{2,1,0:T(4,128)(2,1)}), bf16[4,4,3072]{2,1,0:T(4,128)(2,1)S(1)}, u32[]{:S(2)}, u32[]{:S(2)}) %all-to-all-start.4) | async-done | bytes 98336 | tf_op jit(solution)/shard_map/all_to_all | solution.py:49
  121.7 0.1 reduce_sum.32
  121.7 0.1 convolution_convert_fusion.3
  121.9 20.2 %all_to_all.33 = bf16[8,2,3072]{2,1,0:T(2,128)(2,1)S(1)} all-to-all(bf16[8,2,3072]{2,1,0:T(2,128)(2,1)S(1)} %reshape.107), channel_id=1, replica_groups=mesh['z_lo'=4,'core'=2,'z_hi'=4,'x'=4,'y'=4] {'z_lo','core'}, dimensions={0} | all-to-all | bytes 196608 | tf_op jit(solution)/shard_map/all_to_all | solution.py:49
  142.1 0.6 copy.15
  (6 shorter events, 0.1 us)
Async XLA Ops:
  7.7 16.7 %all-to-all-start = ((bf16[8,2,2,3072]{3,2,1,0:T(2,128)(2,1)}), bf16[8,2,2,3072]{3,2,1,0:T(2,128)(2,1)S(1)}, u32[]{:S(2)}, u32[]{:S(2)}) async-start(bf16[8,2,2,3072]{3,2,1,0:T(2,128)(2,1)} %shard_map.111), calls=%async_computation | async-start | bytes 393216 | tf_op jit(solution)/shard_map/all_to_all | solution.py:49
  56.2 25.3 %copy-start = (bf16[1,3072,128]{2,1,0:T(8,128)(2,1)S(1)}, bf16[1,3072,128]{2,1,0:T(8,128)(2,1)}, u32[]{:S(2)}) copy-start(bf16[1,3072,128]{2,1,0:T(8,128)(2,1)} %param.11) | copy-start | bytes 2359300
  56.2 25.2 %copy-start.1 = (bf16[1,3072,128]{2,1,0:T(8,128)(2,1)S(1)}, bf16[1,3072,128]{2,1,0:T(8,128)(2,1)}, u32[]{:S(2)}) copy-start(bf16[1,3072,128]{2,1,0:T(8,128)(2,1)} %param.12) | copy-start | bytes 2359300
  56.2 25.2 %copy-start.2 = (bf16[1,128,3072]{2,1,0:T(8,128)(2,1)S(1)}, bf16[1,128,3072]{2,1,0:T(8,128)(2,1)}, u32[]{:S(2)}) copy-start(bf16[1,128,3072]{2,1,0:T(8,128)(2,1)} %param.13) | copy-start | bytes 2359300
  103.4 18.3 %all-to-all-start.4 = ((bf16[4,4,3072]{2,1,0:T(4,128)(2,1)}), bf16[4,4,3072]{2,1,0:T(4,128)(2,1)S(1)}, u32[]{:S(2)}, u32[]{:S(2)}) async-start(bf16[4,4,3072]{2,1,0:T(4,128)(2,1)} %reshape.104), calls=%async_computation.4 | async-start | bytes 196608 | tf_op jit(solution)/shard_map/all_to_all | solution.py:49

commit v10 on v8

--- a/solution.py
+++ b/solution.py
@@ -40,9 +40,9 @@
     return first + [[16 + place for place in group] for group in second]
 
 
-NEAR = per_core(ALONG_X, ALONG_Y)
-FAR = per_core(ALONG_Y, ALONG_X)
-WHOLE = per_core([sum(ALONG_X, [])], [sum(ALONG_Y, [])])
+NEAR = per_core(ALONG_Y, ALONG_X)
+FAR = per_core(ALONG_X, ALONG_Y)
+WHOLE = per_core([sum(ALONG_Y, [])], [sum(ALONG_X, [])])
 
 
 def exchange(array, axes, groups=None):
@@ -149,16 +149,17 @@
         total = parts[0, :, part].astype(jnp.float32)
         for j in range(1, parts.shape[0]):
             total += parts[j, :, part].astype(jnp.float32)
-        out[:, part] = total.astype(jnp.bfloat16)
+        for j in range(out.shape[0]):
+            out[j, :, part] = total[j * LIVE : (j + 1) * LIVE].astype(jnp.bfloat16)
         return carry
 
-    lax.fori_loop(0, out.shape[1] // STEP, step, 0)
+    lax.fori_loop(0, out.shape[2] // STEP, step, 0)
 
 
 def sum_parts(parts):
     return pl.pallas_call(
         sum_kernel,
-        out_shape=jax.ShapeDtypeStruct(parts.shape[1:], jnp.bfloat16),
+        out_shape=jax.ShapeDtypeStruct((4, LIVE, parts.shape[2]), jnp.bfloat16),
         in_specs=[pl.BlockSpec(memory_space=pltpu.VMEM)],
         out_specs=pl.BlockSpec(memory_space=pltpu.VMEM),
         compiler_params=pltpu.CompilerParams(vmem_limit_bytes=VMEM_LIMIT),
@@ -184,8 +185,7 @@
     got = got.reshape(experts * 2 * capacity, width)
     packed = dot(both, got).astype(jnp.bfloat16)
     column = lax.all_gather(packed, "z_hi", axis=0, tiled=True)
-    column = fan_out(order_kernel, column, 1)[0]
-    line = lax.all_gather(column, CHIP_PLANE, axis=0, axis_index_groups=NEAR)
+    line = exchange(fan_out(order_kernel, column, 4), CHIP_PLANE, NEAR)
     group = exchange(fan_out(copy_kernel, line, 4), CHIP_PLANE, FAR)
     group = group.reshape(16, 8 * LIVE, width)
     term, hidden, gate_grad, up_grad = middle(
@@ -196,7 +196,7 @@
     plane_sum, group, hidden, gate_grad, up_grad = lax.optimization_barrier(
         (plane_sum, group, hidden, gate_grad, up_grad)
     )
-    parts = exchange(plane_sum.reshape(4, LIVE, width), "z_hi")
+    parts = exchange(plane_sum, "z_hi")
     rows = group[:, : 4 * LIVE].reshape(64 * LIVE, width)
     cots = group[:, 4 * LIVE :].reshape(64 * LIVE, width)
     grad_down = dot(hidden, cots, TN).astype(jnp.bfloat16)

time: 141 us -> 138 us (0.979)
  blocking collectives: 96.6 us -> 93.7 us
    all_gather x1 -> x0, blocking collectives: 11.2 us -> none  [body(): line = lax.all_gather(column, CHIP_PLANE, axis=0, axis_index_groups=NEAR)]
    all_to_all x3 -> x4, blocking collectives: 66.6 us -> 74.9 us  [exchange(): lax.all_to_all(array, axes, split_axis=0, concat_axis=0, axis_index_group...]
  transfers between devices with their start and end apart: 2 -> 2, of which waited for: 2 -> 2; matrix products, arithmetic and copies ran while one was open for 4% -> 5% of each run, Pallas kernels for 0% -> 0%
where the time goes in v10:
time: 138 us; the launch traced here: 137 us
  blocking collectives  93.7 us (68%)
  starting transfers between devices  16.5 us (12%)
  waiting for transfers between devices  10.7 us (8%)
  Pallas kernels  4.9 us (4%)
  matrix products  4.65 us (3%)
  other arithmetic  3.19 us (2%)
  between operations  2.03 us (1%)
  local copies, waits for them, and re-layouts  1.49 us (1%)
    all_to_all x4, blocking collectives, exchange(): lax.all_to_all(array, axes, split_axis=0, concat_axis=0, axis_index_group...  74.9 us
    all_gather x1, blocking collectives, body(): column = lax.all_gather(packed, 'z_hi', axis=0, tiled=True)  18.8 us
    all_to_all x2, starting transfers between devices, exchange(): lax.all_to_all(array, axes, split_axis=0, concat_axis=0, axis_index_group...  16.5 us
    all_to_all x2, waiting for transfers between devices, exchange(): lax.all_to_all(array, axes, split_axis=0, concat_axis=0, axis_index_group...  10.7 us
    dot_general x5, matrix products, dot(): lax.dot_general(left, right, dims, preferred_element_type=jnp.float32)  4.65 us
    pallas_call x1, Pallas kernels, middle(): pl.pallas_call(middle_kernel, out_shape=(jax.ShapeDtypeStruct((blocks, pa...  3.61 us
  transfers between devices with their start and end apart: 2, of which 2 were waited for; matrix products, arithmetic and copies ran while one was open for 5% of the time, Pallas kernels for 0%

profile of v10, /device:TPU:1, one launch (start us, length us, event | category | flops | bytes accessed | tf_op | source)
XLA Modules:
  0.0 137.2 jit_solution(2712960886186024514)
XLA Ops:
  0.6 1.9 %pad_maximum_fusion = bf16[8,2,2,3072]{3,2,1,0:T(2,128)(2,1)} fusion(bf16[8,1,2,3072]{3,2,1,0:T(2,128)(2,1)} %bitcast.45, bf16[8,1,2,3072]{3,2,1,0:T(2,128)(2,1)} %bitcast.46), kind=kLoop, calls=%fused_computation.5 | loop fusion | flops 98304 | bytes 393216 | tf_op jit(solution)/shard_map/stack | solution.py:180
  2.5 10.2 %all-to-all-start = ((bf16[8,2,2,3072]{3,2,1,0:T(2,128)(2,1)}), bf16[8,2,2,3072]{3,2,1,0:T(2,128)(2,1)S(1)}, u32[]{:S(2)}, u32[]{:S(2)}) async-start(bf16[8,2,2,3072]{3,2,1,0:T(2,128)(2,1)} %pad_maximum_fusion), calls=%async_computation | async-start | bytes 393216 | tf_op jit(solution)/shard_map/all_to_all | solution.py:49
  12.7 0.8 select_reduce_fusion.1
  13.5 0.1 select_reduce_fusion
  13.6 0.1 add_select_fusion
  13.7 0.1 compare_convert_fusion
  15.1 0.1 add.28
  15.1 0.1 add.29
  15.2 0.1 lt.59
  15.3 0.1 lt.60
  15.4 0.1 lt.58
  15.5 0.1 broadcast_multiply_fusion
  15.6 0.1 mul.24
  15.7 0.1 fusion
  15.7 3.4 %all-to-all-done = bf16[8,2,2,3072]{3,2,1,0:T(2,128)(2,1)S(1)} async-done(((bf16[8,2,2,3072]{3,2,1,0:T(2,128)(2,1)}), bf16[8,2,2,3072]{3,2,1,0:T(2,128)(2,1)S(1)}, u32[]{:S(2)}, u32[]{:S(2)}) %all-to-all-start) | async-done | bytes 196640 | tf_op jit(solution)/shard_map/all_to_all | solution.py:49
  19.2 0.1 reshape.99
  19.2 0.2 convolution_convert_fusion.4
  19.4 18.8 %all_gather.3.column = bf16[32,3072]{1,0:T(8,128)(2,1)S(1)} all-gather(bf16[8,3072]{1,0:T(8,128)(2,1)S(1)} %convolution_convert_fusion.4), channel_id=1, replica_groups=mesh['z_lo'=4,'core'=2,'z_hi'=4,'x'=4,'y'=4] {'z_hi'}, dimensions={0}, use_global_device_ids=true | all-gather | bytes 245760 | tf_op jit(solution)/shard_map/all_gather | solution.py:187
  38.3 0.2 shard_map.111
  38.5 12.1 %all_to_all.30.block = bf16[4,32,3072]{2,1,0:T(8,128)(2,1)S(1)} all-to-all(bf16[4,32,3072]{2,1,0:T(8,128)(2,1)S(1)} %shard_map.111), channel_id=1, replica_groups={{0,1,2,3},{4,5,6,7},{8,9,10,11},{12,13,14,15},{64,68,72,76},{65,69,73,7..., dimensions={0} | all-to-all | bytes 1572864 | tf_op jit(solution)/shard_map/all_to_all | solution.py:49
  50.6 0.2 shard_map.112
  50.8 0.0 copy-start
  50.8 0.0 copy-start.1
  50.8 0.0 copy-start.2
  50.9 25.4 %all_to_all.31 = bf16[4,4,32,3072]{3,2,1,0:T(8,128)(2,1)S(1)} all-to-all(bf16[4,4,32,3072]{3,2,1,0:T(8,128)(2,1)S(1)} %shard_map.112), channel_id=1, replica_groups={{0,4,8,12},{1,5,9,13},{2,6,10,14},{3,7,11,15},{64,65,66,67},{68,69,70,7..., dimensions={0} | all-to-all | bytes 6291456 | tf_op jit(solution)/shard_map/all_to_all | solution.py:49
  76.2 0.0 copy-done
  76.2 0.0 copy-done.1
  76.2 0.0 copy-done.2
  76.3 3.6 %shard_map.113 = (bf16[16,16,3072]{2,1,0:T(8,128)(2,1)S(1)}, bf16[256,128]{1,0:T(8,128)(2,1)S(1)}, bf16[256,128]{1,0:T(8,128)(2,1)S(1)}, bf16[256,128]{1,0:T(8,128)(2,1)S(1)}) custom-call(f32[8,128]{1,0:T(8,128)S(1)} %broadcast_in_dim.59.keep_row, bf16[16,32,3072]{2,1,0:T(8,128)(2,1)S(1)} %bitcast.33, bf16[3072,128]{1,0:T(8,128)(2,1)S(1)} %bitcast.35, ...), custom_call_target="tpu_custom_call" | custom-call | flops 1006632960 | bytes 8388608 | tf_op jit(solution)/shard_map/pallas_call | solution.py:125
  79.9 17.7 %all_to_all.32.parts = bf16[16,16,3072]{2,1,0:T(8,128)(2,1)S(1)} all-to-all(bf16[16,16,3072]{2,1,0:T(8,128)(2,1)S(1)} %get-tuple-element.25), channel_id=1, replica_groups={{0,1,2,3,4,5,6,7,8,9,10,11,12,13,14,15},{64,68,72,76,65,69,73,77,66,70,..., dimensions={0} | all-to-all | bytes 3145728 | tf_op jit(solution)/shard_map/all_to_all | solution.py:49
  97.5 0.9 shard_map.114
  98.4 6.4 %all-to-all-start.4 = ((bf16[4,4,3072]{2,1,0:T(4,128)(2,1)}), bf16[4,4,3072]{2,1,0:T(4,128)(2,1)S(1)}, u32[]{:S(2)}, u32[]{:S(2)}) async-start(bf16[4,4,3072]{2,1,0:T(4,128)(2,1)} %shard_map.114), calls=%async_computation.4 | async-start | bytes 196608 | tf_op jit(solution)/shard_map/all_to_all | solution.py:49
  104.8 0.2 fusion.1
  105.0 1.5 %convolution_convert_fusion.1 = bf16[3072,128]{1,0:T(8,128)(2,1)} fusion(bf16[256,3072]{1,0:T(8,128)(2,1)S(1)} %bitcast.38, bf16[256,128]{1,0:T(8,128)(2,1)S(1)} %get-tuple-element.32), kind=kOutput, calls=%fused_computation.1 | convolution fusion | flops 201719808 | bytes 2424832 | tf_op jit(solution)/shard_map/dot_general | solution.py:21
  106.5 1.5 %convolution_convert_fusion.2 = bf16[3072,128]{1,0:T(8,128)(2,1)} fusion(bf16[256,3072]{1,0:T(8,128)(2,1)S(1)} %bitcast.39, bf16[256,128]{1,0:T(8,128)(2,1)S(1)} %get-tuple-element.31), kind=kOutput, calls=%fused_computation.2 | convolution fusion | flops 201719808 | bytes 2424832 | tf_op jit(solution)/shard_map/dot_general | solution.py:21
  108.0 1.3 convolution_convert_fusion
  109.3 7.3 %all-to-all-done.4 = bf16[4,4,3072]{2,1,0:T(4,128)(2,1)S(1)} async-done(((bf16[4,4,3072]{2,1,0:T(4,128)(2,1)}), bf16[4,4,3072]{2,1,0:T(4,128)(2,1)S(1)}, u32[]{:S(2)}, u32[]{:S(2)}) %all-to-all-start.4) | async-done | bytes 98336 | tf_op jit(solution)/shard_map/all_to_all | solution.py:49
  116.7 0.1 reduce_sum.32
  116.7 0.1 convolution_convert_fusion.3
  116.9 19.7 %all_to_all.33 = bf16[8,2,3072]{2,1,0:T(2,128)(2,1)S(1)} all-to-all(bf16[8,2,3072]{2,1,0:T(2,128)(2,1)S(1)} %reshape.103), channel_id=1, replica_groups=mesh['z_lo'=4,'core'=2,'z_hi'=4,'x'=4,'y'=4] {'z_lo','core'}, dimensions={0} | all-to-all | bytes 196608 | tf_op jit(solution)/shard_map/all_to_all | solution.py:49
  136.6 0.6 copy.16
  (6 shorter events, 0.1 us)
Async XLA Ops:
  2.5 16.6 %all-to-all-start = ((bf16[8,2,2,3072]{3,2,1,0:T(2,128)(2,1)}), bf16[8,2,2,3072]{3,2,1,0:T(2,128)(2,1)S(1)}, u32[]{:S(2)}, u32[]{:S(2)}) async-start(bf16[8,2,2,3072]{3,2,1,0:T(2,128)(2,1)} %pad_maximum_fusion), calls=%async_computation | async-start | bytes 393216 | tf_op jit(solution)/shard_map/all_to_all | solution.py:49
  50.8 25.4 %copy-start = (bf16[1,3072,128]{2,1,0:T(8,128)(2,1)S(1)}, bf16[1,3072,128]{2,1,0:T(8,128)(2,1)}, u32[]{:S(2)}) copy-start(bf16[1,3072,128]{2,1,0:T(8,128)(2,1)} %param.11) | copy-start | bytes 2359300
  50.8 25.4 %copy-start.1 = (bf16[1,3072,128]{2,1,0:T(8,128)(2,1)S(1)}, bf16[1,3072,128]{2,1,0:T(8,128)(2,1)}, u32[]{:S(2)}) copy-start(bf16[1,3072,128]{2,1,0:T(8,128)(2,1)} %param.12) | copy-start | bytes 2359300
  50.8 25.4 %copy-start.2 = (bf16[1,128,3072]{2,1,0:T(8,128)(2,1)S(1)}, bf16[1,128,3072]{2,1,0:T(8,128)(2,1)}, u32[]{:S(2)}) copy-start(bf16[1,128,3072]{2,1,0:T(8,128)(2,1)} %param.13) | copy-start | bytes 2359300
  98.4 18.2 %all-to-all-start.4 = ((bf16[4,4,3072]{2,1,0:T(4,128)(2,1)}), bf16[4,4,3072]{2,1,0:T(4,128)(2,1)S(1)}, u32[]{:S(2)}, u32[]{:S(2)}) async-start(bf16[4,4,3072]{2,1,0:T(4,128)(2,1)} %shard_map.114), calls=%async_computation.4 | async-start | bytes 196608 | tf_op jit(solution)/shard_map/all_to_all | solution.py:49

commit v11 on v10

--- a/solution.py
+++ b/solution.py
@@ -94,7 +94,7 @@
         sums[:, 2 * units :] += dot(cots, w_down[:, part], NT)
         return carry
 
-    lax.fori_loop(0, width // STEP, forward, 0)
+    lax.fori_loop(0, width // STEP, forward, 0, unroll=True)
     keep = keep_row[0:1, :]
     gate, up, hidden_grad = sums[:, :units], sums[:, units : 2 * units], sums[:, 2 * units :]
     sig = jax.nn.sigmoid(gate)
@@ -113,7 +113,7 @@
         term[:, :, part] = out.reshape(blocks, half, STEP)
         return carry
 
-    lax.fori_loop(0, width // STEP, backward, 0)
+    lax.fori_loop(0, width // STEP, backward, 0, unroll=True)
 
 
 def middle(keep, group, w_gate, w_up, w_down):
@@ -153,7 +153,7 @@
             out[j, :, part] = total[j * LIVE : (j + 1) * LIVE].astype(jnp.bfloat16)
         return carry
 
-    lax.fori_loop(0, out.shape[2] // STEP, step, 0)
+    lax.fori_loop(0, out.shape[2] // STEP, step, 0, unroll=True)
 
 
 def sum_parts(parts):

time: 138 us -> 136 us (0.986)
  Pallas kernels: 4.9 us -> 2.78 us
    pallas_call x1, Pallas kernels: 3.61 us -> 1.53 us  [middle(): pl.pallas_call(middle_kernel, out_shape=(jax.ShapeDtypeStruct((blocks, pa...]
where the time goes in v11:
time: 136 us; the launch traced here: 135 us
  blocking collectives  93.8 us (69%)
  starting transfers between devices  16.5 us (12%)
  waiting for transfers between devices  10.7 us (8%)
  matrix products  4.65 us (3%)
  other arithmetic  3.19 us (2%)
  Pallas kernels  2.78 us (2%)
  between operations  2.03 us (1%)
  local copies, waits for them, and re-layouts  1.49 us (1%)
    all_to_all x4, blocking collectives, exchange(): lax.all_to_all(array, axes, split_axis=0, concat_axis=0, axis_index_group...  74.9 us
    all_gather x1, blocking collectives, body(): column = lax.all_gather(packed, 'z_hi', axis=0, tiled=True)  18.8 us
    all_to_all x2, starting transfers between devices, exchange(): lax.all_to_all(array, axes, split_axis=0, concat_axis=0, axis_index_group...  16.5 us
    all_to_all x2, waiting for transfers between devices, exchange(): lax.all_to_all(array, axes, split_axis=0, concat_axis=0, axis_index_group...  10.7 us
    dot_general x5, matrix products, dot(): lax.dot_general(left, right, dims, preferred_element_type=jnp.float32)  4.65 us
  transfers between devices with their start and end apart: 2, of which 2 were waited for; matrix products, arithmetic and copies ran while one was open for 5% of the time, Pallas kernels for 0%

profile of v11, /device:TPU:1, one launch (start us, length us, event | category | flops | bytes accessed | tf_op | source)
XLA Modules:
  0.0 135.2 jit_solution(4129509162813968175)
XLA Ops:
  0.6 1.9 %pad_maximum_fusion = bf16[8,2,2,3072]{3,2,1,0:T(2,128)(2,1)} fusion(bf16[8,1,2,3072]{3,2,1,0:T(2,128)(2,1)} %bitcast.45, bf16[8,1,2,3072]{3,2,1,0:T(2,128)(2,1)} %bitcast.46), kind=kLoop, calls=%fused_computation.5 | loop fusion | flops 98304 | bytes 393216 | tf_op jit(solution)/shard_map/stack | solution.py:180
  2.5 10.2 %all-to-all-start = ((bf16[8,2,2,3072]{3,2,1,0:T(2,128)(2,1)}), bf16[8,2,2,3072]{3,2,1,0:T(2,128)(2,1)S(1)}, u32[]{:S(2)}, u32[]{:S(2)}) async-start(bf16[8,2,2,3072]{3,2,1,0:T(2,128)(2,1)} %pad_maximum_fusion), calls=%async_computation | async-start | bytes 393216 | tf_op jit(solution)/shard_map/all_to_all | solution.py:49
  12.7 0.8 select_reduce_fusion.1
  13.5 0.1 select_reduce_fusion
  13.6 0.1 add_select_fusion
  13.7 0.1 compare_convert_fusion
  15.1 0.1 add.28
  15.1 0.1 add.29
  15.2 0.1 lt.59
  15.3 0.1 lt.60
  15.4 0.1 lt.58
  15.5 0.1 broadcast_multiply_fusion
  15.6 0.1 mul.24
  15.7 0.1 fusion
  15.7 3.4 %all-to-all-done = bf16[8,2,2,3072]{3,2,1,0:T(2,128)(2,1)S(1)} async-done(((bf16[8,2,2,3072]{3,2,1,0:T(2,128)(2,1)}), bf16[8,2,2,3072]{3,2,1,0:T(2,128)(2,1)S(1)}, u32[]{:S(2)}, u32[]{:S(2)}) %all-to-all-start) | async-done | bytes 196640 | tf_op jit(solution)/shard_map/all_to_all | solution.py:49
  19.2 0.1 reshape.99
  19.2 0.2 convolution_convert_fusion.4
  19.4 18.8 %all_gather.3.column = bf16[32,3072]{1,0:T(8,128)(2,1)S(1)} all-gather(bf16[8,3072]{1,0:T(8,128)(2,1)S(1)} %convolution_convert_fusion.4), channel_id=1, replica_groups=mesh['z_lo'=4,'core'=2,'z_hi'=4,'x'=4,'y'=4] {'z_hi'}, dimensions={0}, use_global_device_ids=true | all-gather | bytes 245760 | tf_op jit(solution)/shard_map/all_gather | solution.py:187
  38.3 0.2 shard_map.111
  38.5 12.1 %all_to_all.30.block = bf16[4,32,3072]{2,1,0:T(8,128)(2,1)S(1)} all-to-all(bf16[4,32,3072]{2,1,0:T(8,128)(2,1)S(1)} %shard_map.111), channel_id=1, replica_groups={{0,1,2,3},{4,5,6,7},{8,9,10,11},{12,13,14,15},{64,68,72,76},{65,69,73,7..., dimensions={0} | all-to-all | bytes 1572864 | tf_op jit(solution)/shard_map/all_to_all | solution.py:49
  50.6 0.2 shard_map.112
  50.8 0.0 copy-start
  50.8 0.0 copy-start.1
  50.8 0.0 copy-start.2
  50.9 25.4 %all_to_all.31 = bf16[4,4,32,3072]{3,2,1,0:T(8,128)(2,1)S(1)} all-to-all(bf16[4,4,32,3072]{3,2,1,0:T(8,128)(2,1)S(1)} %shard_map.112), channel_id=1, replica_groups={{0,4,8,12},{1,5,9,13},{2,6,10,14},{3,7,11,15},{64,65,66,67},{68,69,70,7..., dimensions={0} | all-to-all | bytes 6291456 | tf_op jit(solution)/shard_map/all_to_all | solution.py:49
  76.2 0.0 copy-done
  76.2 0.0 copy-done.1
  76.2 0.0 copy-done.2
  76.3 1.5 %shard_map.113 = (bf16[16,16,3072]{2,1,0:T(8,128)(2,1)S(1)}, bf16[256,128]{1,0:T(8,128)(2,1)S(1)}, bf16[256,128]{1,0:T(8,128)(2,1)S(1)}, bf16[256,128]{1,0:T(8,128)(2,1)S(1)}) custom-call(f32[8,128]{1,0:T(8,128)S(1)} %broadcast_in_dim.59.keep_row, bf16[16,32,3072]{2,1,0:T(8,128)(2,1)S(1)} %bitcast.33, bf16[3072,128]{1,0:T(8,128)(2,1)S(1)} %bitcast.35, ...), custom_call_target="tpu_custom_call" | custom-call | flops 1006632960 | bytes 8388608 | tf_op jit(solution)/shard_map/pallas_call | solution.py:125
  77.8 17.7 %all_to_all.32.parts = bf16[16,16,3072]{2,1,0:T(8,128)(2,1)S(1)} all-to-all(bf16[16,16,3072]{2,1,0:T(8,128)(2,1)S(1)} %get-tuple-element.25), channel_id=1, replica_groups={{0,1,2,3,4,5,6,7,8,9,10,11,12,13,14,15},{64,68,72,76,65,69,73,77,66,70,..., dimensions={0} | all-to-all | bytes 3145728 | tf_op jit(solution)/shard_map/all_to_all | solution.py:49
  95.5 0.9 shard_map.114
  96.3 6.4 %all-to-all-start.4 = ((bf16[4,4,3072]{2,1,0:T(4,128)(2,1)}), bf16[4,4,3072]{2,1,0:T(4,128)(2,1)S(1)}, u32[]{:S(2)}, u32[]{:S(2)}) async-start(bf16[4,4,3072]{2,1,0:T(4,128)(2,1)} %shard_map.114), calls=%async_computation.4 | async-start | bytes 196608 | tf_op jit(solution)/shard_map/all_to_all | solution.py:49
  102.7 0.2 fusion.1
  102.9 1.5 %convolution_convert_fusion.1 = bf16[3072,128]{1,0:T(8,128)(2,1)} fusion(bf16[256,3072]{1,0:T(8,128)(2,1)S(1)} %bitcast.38, bf16[256,128]{1,0:T(8,128)(2,1)S(1)} %get-tuple-element.32), kind=kOutput, calls=%fused_computation.1 | convolution fusion | flops 201719808 | bytes 2424832 | tf_op jit(solution)/shard_map/dot_general | solution.py:21
  104.4 1.5 %convolution_convert_fusion.2 = bf16[3072,128]{1,0:T(8,128)(2,1)} fusion(bf16[256,3072]{1,0:T(8,128)(2,1)S(1)} %bitcast.39, bf16[256,128]{1,0:T(8,128)(2,1)S(1)} %get-tuple-element.31), kind=kOutput, calls=%fused_computation.2 | convolution fusion | flops 201719808 | bytes 2424832 | tf_op jit(solution)/shard_map/dot_general | solution.py:21
  105.9 1.3 convolution_convert_fusion
  107.2 7.3 %all-to-all-done.4 = bf16[4,4,3072]{2,1,0:T(4,128)(2,1)S(1)} async-done(((bf16[4,4,3072]{2,1,0:T(4,128)(2,1)}), bf16[4,4,3072]{2,1,0:T(4,128)(2,1)S(1)}, u32[]{:S(2)}, u32[]{:S(2)}) %all-to-all-start.4) | async-done | bytes 98336 | tf_op jit(solution)/shard_map/all_to_all | solution.py:49
  114.5 0.1 reduce_sum.32
  114.6 0.1 convolution_convert_fusion.3
  114.8 19.7 %all_to_all.33 = bf16[8,2,3072]{2,1,0:T(2,128)(2,1)S(1)} all-to-all(bf16[8,2,3072]{2,1,0:T(2,128)(2,1)S(1)} %reshape.103), channel_id=1, replica_groups=mesh['z_lo'=4,'core'=2,'z_hi'=4,'x'=4,'y'=4] {'z_lo','core'}, dimensions={0} | all-to-all | bytes 196608 | tf_op jit(solution)/shard_map/all_to_all | solution.py:49
  134.5 0.6 copy.16
  (6 shorter events, 0.1 us)
Async XLA Ops:
  2.5 16.6 %all-to-all-start = ((bf16[8,2,2,3072]{3,2,1,0:T(2,128)(2,1)}), bf16[8,2,2,3072]{3,2,1,0:T(2,128)(2,1)S(1)}, u32[]{:S(2)}, u32[]{:S(2)}) async-start(bf16[8,2,2,3072]{3,2,1,0:T(2,128)(2,1)} %pad_maximum_fusion), calls=%async_computation | async-start | bytes 393216 | tf_op jit(solution)/shard_map/all_to_all | solution.py:49
  50.8 25.4 %copy-start = (bf16[1,3072,128]{2,1,0:T(8,128)(2,1)S(1)}, bf16[1,3072,128]{2,1,0:T(8,128)(2,1)}, u32[]{:S(2)}) copy-start(bf16[1,3072,128]{2,1,0:T(8,128)(2,1)} %param.11) | copy-start | bytes 2359300
  50.8 25.4 %copy-start.1 = (bf16[1,3072,128]{2,1,0:T(8,128)(2,1)S(1)}, bf16[1,3072,128]{2,1,0:T(8,128)(2,1)}, u32[]{:S(2)}) copy-start(bf16[1,3072,128]{2,1,0:T(8,128)(2,1)} %param.12) | copy-start | bytes 2359300
  50.8 25.4 %copy-start.2 = (bf16[1,128,3072]{2,1,0:T(8,128)(2,1)S(1)}, bf16[1,128,3072]{2,1,0:T(8,128)(2,1)}, u32[]{:S(2)}) copy-start(bf16[1,128,3072]{2,1,0:T(8,128)(2,1)} %param.13) | copy-start | bytes 2359300
  96.3 18.2 %all-to-all-start.4 = ((bf16[4,4,3072]{2,1,0:T(4,128)(2,1)}), bf16[4,4,3072]{2,1,0:T(4,128)(2,1)S(1)}, u32[]{:S(2)}, u32[]{:S(2)}) async-start(bf16[4,4,3072]{2,1,0:T(4,128)(2,1)} %shard_map.114), calls=%async_computation.4 | async-start | bytes 196608 | tf_op jit(solution)/shard_map/all_to_all | solution.py:49

commit v12 on v11

--- a/solution.py
+++ b/solution.py
@@ -49,6 +49,21 @@
     return lax.all_to_all(
         array, axes, split_axis=0, concat_axis=0, axis_index_groups=groups, tiled=True
     )
+
+
+def pair_kernel(rows, cots, pairs):
+    pairs[:, 0] = rows[...]
+    pairs[:, 1] = cots[...]
+
+
+def pair_up(rows, cots):
+    vmem = pl.BlockSpec(memory_space=pltpu.VMEM)
+    return pl.pallas_call(
+        pair_kernel,
+        out_shape=jax.ShapeDtypeStruct((rows.shape[0], 2) + rows.shape[1:], jnp.bfloat16),
+        in_specs=[vmem, vmem],
+        out_specs=vmem,
+    )(rows, cots)
 
 
 def order_kernel(column, fan):
@@ -177,7 +192,7 @@
     both = kind[:, None, None, :, None] * chooser[None, :, :, None, :]
     both = both.reshape(2 * LIVE, experts * 2 * capacity)
 
-    slots = jnp.stack((x_rows[0, 0], cot_rows[0, 0]), axis=1)
+    slots = pair_up(x_rows[0, 0], cot_rows[0, 0])
     keep = (block_rank.reshape(()) < kept_blocks.reshape(())).astype(jnp.float32)
     keep = jnp.broadcast_to(keep, (8, w_gate.shape[2]))
     got = exchange(slots, EXPERT)

time: 136 us -> 135 us (level)
  other arithmetic: 3.19 us -> 1.31 us
  Pallas kernels: 2.78 us -> 4.34 us
    another operation x1 -> x0, other arithmetic: 1.88 us -> none  [body(): slots = jnp.stack((x_rows[0, 0], cot_rows[0, 0]), axis=1)]
    pallas_call x0 -> x1, Pallas kernels: none -> 1.63 us  [pair_up(): pl.pallas_call(pair_kernel, out_shape=jax.ShapeDtypeStruct((rows.shape[0]...]
where the time goes in v12:
time: 135 us
  blocking collectives  93.7 us (69%)
  starting transfers between devices  16.5 us (12%)
  waiting for transfers between devices  10.7 us (8%)
  matrix products  4.65 us (3%)
  Pallas kernels  4.34 us (3%)
  between operations  2.03 us (2%)
  local copies, waits for them, and re-layouts  1.49 us (1%)
    all_to_all x4, blocking collectives, exchange(): lax.all_to_all(array, axes, split_axis=0, concat_axis=0, axis_index_group...  74.9 us
    all_gather x1, blocking collectives, body(): column = lax.all_gather(packed, 'z_hi', axis=0, tiled=True)  18.8 us
    all_to_all x2, starting transfers between devices, exchange(): lax.all_to_all(array, axes, split_axis=0, concat_axis=0, axis_index_group...  16.5 us
    all_to_all x2, waiting for transfers between devices, exchange(): lax.all_to_all(array, axes, split_axis=0, concat_axis=0, axis_index_group...  10.7 us
    dot_general x5, matrix products, dot(): lax.dot_general(left, right, dims, preferred_element_type=jnp.float32)  4.65 us
  transfers between devices with their start and end apart: 2, of which 2 were waited for; matrix products, arithmetic and copies ran while one was open for 5% of the time, Pallas kernels for 0%

profile of v12, /device:TPU:1, one launch (start us, length us, event | category | flops | bytes accessed | tf_op | source)
XLA Modules:
  0.0 134.9 jit_solution(77317882111007990)
XLA Ops:
  0.6 1.6 %shard_map.111 = bf16[8,2,2,3072]{3,2,1,0:T(2,128)(2,1)} custom-call(bf16[8,2,3072]{2,1,0:T(2,128)(2,1)} %bitcast.45, bf16[8,2,3072]{2,1,0:T(2,128)(2,1)} %bitcast.46), custom_call_target="tpu_custom_call" | custom-call | tf_op jit(solution)/shard_map/pallas_call | solution.py:61
  2.3 10.2 %all-to-all-start = ((bf16[8,2,2,3072]{3,2,1,0:T(2,128)(2,1)}), bf16[8,2,2,3072]{3,2,1,0:T(2,128)(2,1)S(1)}, u32[]{:S(2)}, u32[]{:S(2)}) async-start(bf16[8,2,2,3072]{3,2,1,0:T(2,128)(2,1)} %shard_map.111), calls=%async_computation | async-start | bytes 393216 | tf_op jit(solution)/shard_map/all_to_all | solution.py:49
  12.4 0.8 select_reduce_fusion.1
  13.2 0.1 select_reduce_fusion
  13.4 0.1 add_select_fusion
  13.4 0.1 compare_convert_fusion
  14.8 0.1 add.28
  14.9 0.1 add.29
  15.0 0.1 lt.59
  15.1 0.1 lt.60
  15.1 0.1 lt.58
  15.2 0.1 broadcast_multiply_fusion
  15.3 0.1 mul.24
  15.4 0.1 fusion
  15.5 3.4 %all-to-all-done = bf16[8,2,2,3072]{3,2,1,0:T(2,128)(2,1)S(1)} async-done(((bf16[8,2,2,3072]{3,2,1,0:T(2,128)(2,1)}), bf16[8,2,2,3072]{3,2,1,0:T(2,128)(2,1)S(1)}, u32[]{:S(2)}, u32[]{:S(2)}) %all-to-all-start) | async-done | bytes 196640 | tf_op jit(solution)/shard_map/all_to_all | solution.py:49
  18.9 0.1 reshape.99
  19.0 0.2 convolution_convert_fusion.4
  19.2 18.8 %all_gather.3.column = bf16[32,3072]{1,0:T(8,128)(2,1)S(1)} all-gather(bf16[8,3072]{1,0:T(8,128)(2,1)S(1)} %convolution_convert_fusion.4), channel_id=1, replica_groups=mesh['z_lo'=4,'core'=2,'z_hi'=4,'x'=4,'y'=4] {'z_hi'}, dimensions={0}, use_global_device_ids=true | all-gather | bytes 245760 | tf_op jit(solution)/shard_map/all_gather | solution.py:202
  38.0 0.2 shard_map.112
  38.2 12.2 %all_to_all.30.block = bf16[4,32,3072]{2,1,0:T(8,128)(2,1)S(1)} all-to-all(bf16[4,32,3072]{2,1,0:T(8,128)(2,1)S(1)} %shard_map.112), channel_id=1, replica_groups={{0,1,2,3},{4,5,6,7},{8,9,10,11},{12,13,14,15},{64,68,72,76},{65,69,73,7..., dimensions={0} | all-to-all | bytes 1572864 | tf_op jit(solution)/shard_map/all_to_all | solution.py:49
  50.4 0.2 shard_map.113
  50.6 0.0 copy-start
  50.6 0.0 copy-start.1
  50.6 0.0 copy-start.2
  50.6 25.4 %all_to_all.31 = bf16[4,4,32,3072]{3,2,1,0:T(8,128)(2,1)S(1)} all-to-all(bf16[4,4,32,3072]{3,2,1,0:T(8,128)(2,1)S(1)} %shard_map.113), channel_id=1, replica_groups={{0,4,8,12},{1,5,9,13},{2,6,10,14},{3,7,11,15},{64,65,66,67},{68,69,70,7..., dimensions={0} | all-to-all | bytes 6291456 | tf_op jit(solution)/shard_map/all_to_all | solution.py:49
  76.0 0.0 copy-done
  76.0 0.0 copy-done.1
  76.0 0.0 copy-done.2
  76.0 1.5 %shard_map.114 = (bf16[16,16,3072]{2,1,0:T(8,128)(2,1)S(1)}, bf16[256,128]{1,0:T(8,128)(2,1)S(1)}, bf16[256,128]{1,0:T(8,128)(2,1)S(1)}, bf16[256,128]{1,0:T(8,128)(2,1)S(1)}) custom-call(f32[8,128]{1,0:T(8,128)S(1)} %broadcast_in_dim.59.keep_row, bf16[16,32,3072]{2,1,0:T(8,128)(2,1)S(1)} %bitcast.33, bf16[3072,128]{1,0:T(8,128)(2,1)S(1)} %bitcast.35, ...), custom_call_target="tpu_custom_call" | custom-call | flops 1006632960 | bytes 8388608 | tf_op jit(solution)/shard_map/pallas_call | solution.py:140
  77.5 17.7 %all_to_all.32.parts = bf16[16,16,3072]{2,1,0:T(8,128)(2,1)S(1)} all-to-all(bf16[16,16,3072]{2,1,0:T(8,128)(2,1)S(1)} %get-tuple-element.25), channel_id=1, replica_groups={{0,1,2,3,4,5,6,7,8,9,10,11,12,13,14,15},{64,68,72,76,65,69,73,77,66,70,..., dimensions={0} | all-to-all | bytes 3145728 | tf_op jit(solution)/shard_map/all_to_all | solution.py:49
  95.1 0.9 shard_map.115
  96.0 6.4 %all-to-all-start.4 = ((bf16[4,4,3072]{2,1,0:T(4,128)(2,1)}), bf16[4,4,3072]{2,1,0:T(4,128)(2,1)S(1)}, u32[]{:S(2)}, u32[]{:S(2)}) async-start(bf16[4,4,3072]{2,1,0:T(4,128)(2,1)} %shard_map.115), calls=%async_computation.4 | async-start | bytes 196608 | tf_op jit(solution)/shard_map/all_to_all | solution.py:49
  102.4 0.2 fusion.1
  102.6 1.5 %convolution_convert_fusion.1 = bf16[3072,128]{1,0:T(8,128)(2,1)} fusion(bf16[256,3072]{1,0:T(8,128)(2,1)S(1)} %bitcast.38, bf16[256,128]{1,0:T(8,128)(2,1)S(1)} %get-tuple-element.32), kind=kOutput, calls=%fused_computation.1 | convolution fusion | flops 201719808 | bytes 2424832 | tf_op jit(solution)/shard_map/dot_general | solution.py:21
  104.1 1.5 %convolution_convert_fusion.2 = bf16[3072,128]{1,0:T(8,128)(2,1)} fusion(bf16[256,3072]{1,0:T(8,128)(2,1)S(1)} %bitcast.39, bf16[256,128]{1,0:T(8,128)(2,1)S(1)} %get-tuple-element.31), kind=kOutput, calls=%fused_computation.2 | convolution fusion | flops 201719808 | bytes 2424832 | tf_op jit(solution)/shard_map/dot_general | solution.py:21
  105.6 1.3 convolution_convert_fusion
  106.9 7.3 %all-to-all-done.4 = bf16[4,4,3072]{2,1,0:T(4,128)(2,1)S(1)} async-done(((bf16[4,4,3072]{2,1,0:T(4,128)(2,1)}), bf16[4,4,3072]{2,1,0:T(4,128)(2,1)S(1)}, u32[]{:S(2)}, u32[]{:S(2)}) %all-to-all-start.4) | async-done | bytes 98336 | tf_op jit(solution)/shard_map/all_to_all | solution.py:49
  114.2 0.1 reduce_sum.32
  114.3 0.1 convolution_convert_fusion.3
  114.5 19.7 %all_to_all.33 = bf16[8,2,3072]{2,1,0:T(2,128)(2,1)S(1)} all-to-all(bf16[8,2,3072]{2,1,0:T(2,128)(2,1)S(1)} %reshape.103), channel_id=1, replica_groups=mesh['z_lo'=4,'core'=2,'z_hi'=4,'x'=4,'y'=4] {'z_lo','core'}, dimensions={0} | all-to-all | bytes 196608 | tf_op jit(solution)/shard_map/all_to_all | solution.py:49
  134.2 0.6 copy.15
  (6 shorter events, 0.1 us)
Async XLA Ops:
  2.3 16.6 %all-to-all-start = ((bf16[8,2,2,3072]{3,2,1,0:T(2,128)(2,1)}), bf16[8,2,2,3072]{3,2,1,0:T(2,128)(2,1)S(1)}, u32[]{:S(2)}, u32[]{:S(2)}) async-start(bf16[8,2,2,3072]{3,2,1,0:T(2,128)(2,1)} %shard_map.111), calls=%async_computation | async-start | bytes 393216 | tf_op jit(solution)/shard_map/all_to_all | solution.py:49
  50.6 25.4 %copy-start = (bf16[1,3072,128]{2,1,0:T(8,128)(2,1)S(1)}, bf16[1,3072,128]{2,1,0:T(8,128)(2,1)}, u32[]{:S(2)}) copy-start(bf16[1,3072,128]{2,1,0:T(8,128)(2,1)} %param.11) | copy-start | bytes 2359300
  50.6 25.4 %copy-start.1 = (bf16[1,3072,128]{2,1,0:T(8,128)(2,1)S(1)}, bf16[1,3072,128]{2,1,0:T(8,128)(2,1)}, u32[]{:S(2)}) copy-start(bf16[1,3072,128]{2,1,0:T(8,128)(2,1)} %param.12) | copy-start | bytes 2359300
  50.6 25.4 %copy-start.2 = (bf16[1,128,3072]{2,1,0:T(8,128)(2,1)S(1)}, bf16[1,128,3072]{2,1,0:T(8,128)(2,1)}, u32[]{:S(2)}) copy-start(bf16[1,128,3072]{2,1,0:T(8,128)(2,1)} %param.13) | copy-start | bytes 2359300
  96.0 18.2 %all-to-all-start.4 = ((bf16[4,4,3072]{2,1,0:T(4,128)(2,1)}), bf16[4,4,3072]{2,1,0:T(4,128)(2,1)S(1)}, u32[]{:S(2)}, u32[]{:S(2)}) async-start(bf16[4,4,3072]{2,1,0:T(4,128)(2,1)} %shard_map.115), calls=%async_computation.4 | async-start | bytes 196608 | tf_op jit(solution)/shard_map/all_to_all | solution.py:49
